TPU v7x, 256 devices: a whole 4x4x8 slice. The times are simulated.
256 devices in a mesh: dp: 64 (over y, x, z_lo), tensor: 4 (over z_hi, core).
Axes of the slice: x: 4, y: 4, z: 8 (z_hi: 2, z_lo: 4; z = z_hi * 4 + z_lo), core: 2. Of those that a mesh axis runs over, the one named last changes fastest.
Arguments:
- attn_out: bfloat16 [8192, 4096], P('dp', 'tensor'), may hold values from -6 to 6
- out_proj: bfloat16 [4096, 4096], P('tensor', 'dp'), may hold values from -0.09375 to 0.09375
- residual: bfloat16 [8192, 4096], P('dp', 'tensor')
- teacher_gain: float32 [4096], P('tensor'), may hold values from 0.25 to 1.75
- student_feats: bfloat16 [57344, 1024], P('dp')
- head_small: bfloat16 [384, 4096], P(None, 'tensor'), may hold values from -0.3125 to 0.3125
- head_base: bfloat16 [768, 4096], P(None, 'tensor'), may hold values from -0.21875 to 0.21875
- head_large: bfloat16 [1024, 4096], P(None, 'tensor'), may hold values from -0.1875 to 0.1875
- gain_small: float32 [384], replicated, may hold values from 0.25 to 1.75
- gain_base: float32 [768], replicated, may hold values from 0.25 to 1.75
- gain_large: float32 [1024], replicated, may hold values from 0.25 to 1.75
- row_shard: int32 [8192, 3], P('dp'), may hold values from 0 to 63, as said below
Outputs:
- grad_head_small: float32 [384, 4096], P('dp', 'tensor')
- grad_head_base: float32 [768, 4096], P('dp', 'tensor')
- grad_head_large: float32 [1024, 4096], P('dp', 'tensor')
- grad_gain_small: float32 [384], P('tensor')
- grad_gain_base: float32 [768], P('tensor')
- grad_gain_large: float32 [1024], P('tensor')
- token_gradient: bfloat16 [57344, 1024], P('dp', 'tensor')
- losses: float32 [3], replicated
Inputs may be any that keep to these rules, and one draw needn't show every extreme that they name: `row_shard`: column g names only shards of group g: 12, 20 and 32 distinct shards for g = 0, 1, 2, no shard in two columns, every shard in some column. In each column, of the 128 tokens of one index of dp at most 14 name one shard; in each column one shard is named by exactly min(14, 128 - G + 1) tokens of every index of dp (G the group's shard count), and every shard of the group by at least one token of every index of dp.
All inputs are finite; a program needn't handle non-finite values.
Results may differ from a plain program's by a relative error of at most 0.0072.
Values may be sent and summed in bfloat16 or wider, within the bound.
No kernel may reach another device: no remote copies, remote signals or barrier semaphores. Data moves between devices by JAX's collectives and lax.ppermute only.
A program may use at most 128 MiB of HBM per device.

v0:
```python
import math

import jax
import jax.numpy as jnp
from jax import lax
from jax.sharding import PartitionSpec as P

D = 4096


def row_norm_values(value_list):
    center = jnp.mean(value_list, axis=1, keepdims=True)
    spread = jnp.mean(value_list * value_list, axis=1, keepdims=True) - center * center
    scale_factor = lax.rsqrt(spread + 1e-06)
    return ((value_list - center) * scale_factor, scale_factor)


def group_counts(shards):
    small_count = shards // 8 + shards // 16
    base_count = shards // 4 + shards // 16
    return (small_count, base_count, shards - small_count - base_count)


def per_device(
    attn_out,
    out_proj,
    residual,
    teacher_gain,
    student_feats,
    head_small,
    head_base,
    head_large,
    gain_small,
    gain_base,
    gain_large,
    row_shard,
):
    shards = lax.axis_size("dp")
    split_points = lax.axis_size("tensor")
    rows = attn_out.shape[0]
    total = rows * shards
    square_root = math.sqrt(total)
    sizes = group_counts(shards)
    heads = (head_small, head_base, head_large)
    gain_list = (gain_small, gain_base, gain_large)
    widths = tuple((item.shape[0] for item in heads))
    block_wide = widths[2] // split_points
    slot_list = student_feats.shape[0]
    slot_cap = slot_list // shards
    tensor_position = lax.axis_index("tensor")
    dp_pos = lax.axis_index("dp")
    shard_ids = jnp.arange(shards, dtype=jnp.int32)
    partial_sum = jnp.dot(
        attn_out,
        lax.all_gather(out_proj, "dp", axis=1, tiled=True),
        preferred_element_type=jnp.float32,
    )
    summed = lax.psum_scatter(partial_sum, "tensor", scatter_dimension=1, tiled=True)
    hidden = residual.astype(jnp.float32) + summed
    first_sum, square_sum = lax.psum(
        (jnp.sum(hidden, axis=1), jnp.sum(hidden * hidden, axis=1)), "tensor"
    )
    center = first_sum[:, None] / D
    spread = square_sum[:, None] / D - center * center
    target = ((hidden - center) * lax.rsqrt(spread + 1e-06) * teacher_gain).astype(jnp.bfloat16)
    named = jnp.stack(
        [
            jnp.any(row_shard[:, selected_index][:, None] == shard_ids[None, :], axis=0)
            for selected_index in range(3)
        ]
    ).astype(jnp.int32)
    shard_group = named[1] + 2 * named[2]
    group_id = shard_group[dp_pos]
    slot_ids = jnp.arange(slot_list, dtype=jnp.int32)
    selector = jnp.zeros((rows, slot_list), jnp.float32)
    for selected_index in range(3):
        destination = row_shard[:, selected_index]
        onehot = (destination[:, None] == shard_ids[None, :]).astype(jnp.int32)
        earlier = jnp.cumsum(onehot, axis=0) - onehot
        placing = destination * slot_cap + jnp.sum(earlier * onehot, axis=1)
        selector = selector + (placing[:, None] == slot_ids[None, :]).astype(jnp.float32)
    send_live = jnp.sum(selector, axis=0)
    selector = selector.astype(jnp.bfloat16)
    send_target = jnp.einsum(
        "rs,rc->sc", selector, target, preferred_element_type=jnp.float32
    ).astype(jnp.bfloat16)
    recv_target, recv_live = (
        lax.all_to_all(
            send_target.reshape(shards, slot_cap, -1), "dp", split_axis=0, concat_axis=0, tiled=True
        ),
        lax.all_to_all(
            send_live.astype(jnp.bfloat16).reshape(shards, slot_cap),
            "dp",
            split_axis=0,
            concat_axis=0,
            tiled=True,
        ),
    )
    recv_target = recv_target.reshape(slot_list, -1)
    live = recv_live.reshape(slot_list).astype(jnp.float32)
    members = jnp.array(sizes, jnp.float32)[group_id]
    weight = live * (total / (members * jnp.sum(live)))

    def make_branch(selected_index):

        def run(operands):
            feats, target_in, weight_in = operands
            feature_width = widths[selected_index]
            portion_width = feature_width // split_points
            packed_rows = feats.reshape(slot_list, split_points, block_wide)[
                :, :, :portion_width
            ].reshape(slot_list, feature_width)
            centered_scaled, scale_factor = row_norm_values(packed_rows.astype(jnp.float32))
            normalized_rows = (centered_scaled * gain_list[selected_index]).astype(jnp.bfloat16)
            student_out = jnp.dot(
                normalized_rows, heads[selected_index], preferred_element_type=jnp.float32
            )
            diff = student_out - target_in.astype(jnp.float32)
            error = (weight_in[:, None] * diff).astype(jnp.bfloat16)
            grad_head = (
                jnp.einsum("rw,rc->wc", normalized_rows, error, preferred_element_type=jnp.float32)
                / square_root
            )
            backward_value = jnp.dot(
                error, heads[selected_index].T, preferred_element_type=jnp.float32
            )
            loss = jnp.sum(weight_in * jnp.sum(diff * diff, axis=1)) / (2.0 * D * total)
            padding_amount = ((0, 0), (0, 0), (0, block_wide - portion_width))
            backward_block_list = jnp.pad(
                backward_value.reshape(slot_list, split_points, portion_width), padding_amount
            )
            centered_block_list = jnp.pad(
                centered_scaled.reshape(slot_list, split_points, portion_width), padding_amount
            )
            gain_block_list = jnp.pad(
                gain_list[selected_index].reshape(split_points, portion_width),
                ((0, 0), (0, block_wide - portion_width)),
            )
            head_row_list = jnp.pad(
                grad_head.reshape(shards, feature_width // shards, -1),
                ((0, 0), (0, widths[2] // shards - feature_width // shards), (0, 0)),
            )
            loss_values_all = jnp.where(jnp.arange(3) == selected_index, loss, 0.0).astype(
                jnp.float32
            )
            return (
                backward_block_list,
                centered_block_list,
                scale_factor[:, 0],
                gain_block_list,
                head_row_list,
                loss_values_all,
                jnp.float32(feature_width),
            )

        return run

    output_list = lax.switch(
        group_id,
        [make_branch(selected_index) for selected_index in range(3)],
        (student_feats, recv_target, weight),
    )
    (
        backward_block_list,
        centered_block_list,
        scale_factor,
        gain_block_list,
        head_row_list,
        loss_values_all,
        width_number,
    ) = output_list
    centered_local = lax.dynamic_index_in_dim(
        centered_block_list, tensor_position, 1, keepdims=False
    )
    backward_local = lax.psum_scatter(
        backward_block_list, "tensor", scatter_dimension=1, tiled=True
    )[:, 0, :]
    gain_mine = lax.dynamic_index_in_dim(gain_block_list, tensor_position, 0, keepdims=False)
    upper_limit = backward_local * gain_mine
    first_moment, second_moment, loss_values_all = lax.psum(
        (
            jnp.sum(upper_limit, axis=1),
            jnp.sum(upper_limit * centered_local, axis=1),
            loss_values_all,
        ),
        "tensor",
    )
    grad_rows = scale_factor[:, None] * (
        upper_limit
        - first_moment[:, None] / width_number
        - centered_local * second_moment[:, None] / width_number
    )
    used_cols = jnp.arange(block_wide, dtype=jnp.float32) < width_number / split_points
    token_gradient = jnp.where(used_cols[None, :], grad_rows, 0.0).astype(jnp.bfloat16)
    gain_portion = jnp.sum(backward_local * centered_local, axis=0) / square_root
    gain_terms = tuple(
        (
            jnp.where(
                group_id == selected_index,
                gain_portion[: widths[selected_index] // split_points],
                0.0,
            )
            for selected_index in range(3)
        )
    )
    head_terms = tuple(
        (
            jnp.where(
                group_id == selected_index,
                head_row_list[:, : widths[selected_index] // shards, :].reshape(
                    widths[selected_index], -1
                ),
                0.0,
            )
            for selected_index in range(3)
        )
    )
    grad_small, grad_base, grad_large = (
        lax.psum_scatter(head_terms[0], "dp", scatter_dimension=0, tiled=True),
        lax.psum_scatter(head_terms[1], "dp", scatter_dimension=0, tiled=True),
        lax.psum_scatter(head_terms[2], "dp", scatter_dimension=0, tiled=True),
    )
    gain_small_out, gain_base_out, gain_large_out, losses = lax.psum(
        (gain_terms[0], gain_terms[1], gain_terms[2], loss_values_all), "dp"
    )
    return (
        grad_small,
        grad_base,
        grad_large,
        gain_small_out,
        gain_base_out,
        gain_large_out,
        token_gradient,
        losses,
    )


def solution(mesh):
    placed = (
        P("dp", "tensor"),
        P("tensor", "dp"),
        P("dp", "tensor"),
        P("tensor"),
        P("dp", None),
        P(None, "tensor"),
        P(None, "tensor"),
        P(None, "tensor"),
        P(),
        P(),
        P(),
        P("dp", None),
    )
    return jax.shard_map(
        per_device,
        mesh=mesh,
        in_specs=placed,
        out_specs=(
            P("dp", "tensor"),
            P("dp", "tensor"),
            P("dp", "tensor"),
            P("tensor"),
            P("tensor"),
            P("tensor"),
            P("dp", "tensor"),
            P(),
        ),
        check_vma=False,
    )
```

profile of v0, /device:TPU:32, one launch (start us, length us, event | category | flops | bytes accessed | tf_op | source)
XLA Modules:
  0.0 1148.2 jit_solution(14111432830275258085)
XLA Ops:
  8.0 381.8 %all-gather.2.cloned.1.call-done = bf16[1024,4096]{0,1:T(8,128)(2,1)} async-done(((bf16[1024,64]{0,1:T(8,128)(2,1)}), bf16[1024,4096]{0,1:T(8,128)(2,1)}) %all-gather.2.cloned.1.call-update) | async-done | bytes 8388624 | tf_op jit(solution)/shard_map/all_gather | solution.py:55
  389.8 7.6 fusion.42
  400.3 10.0 all-to-all-start
  410.3 42.0 %reduce-scatter.8.cloned.1.call-done = f32[128,1024]{1,0:T(8,128)} async-done(((f32[128,4096]{1,0:T(8,128)}), f32[128,1024]{1,0:T(8,128)}) %reduce-scatter.8.cloned.1.call-update) | async-done | bytes 524304 | tf_op jit(solution)/shard_map/reduce_scatter | solution.py:58
  453.6 9.7 all-reduce.14
  463.3 1.9 convolution_convert_fusion
  466.8 10.9 all-to-all-start.1
  484.0 43.1 %all-to-all-done.1 = bf16[64,14,1024]{2,1,0:T(8,128)(2,1)} async-done(((bf16[64,14,1024]{2,1,0:T(8,128)(2,1)}), bf16[64,14,1024]{2,1,0:T(8,128)(2,1)}, u32[]{:S(2)}, u32[]{:S(2)}) %all-to-all-start.1) | async-done | bytes 1835040 | tf_op jit(solution)/shard_map/all_to_all | solution.py:88
  527.1 3.8 reshape.205
  531.0 28.4 %conditional.1 = (f32[896,4,256]{0,2,1:T(8,128)}, f32[896,4,256]{0,2,1:T(8,128)}, f32[896]{0:T(1024)}, f32[4,256]{1,0:T(4,128)S(1)}, f32[64,16,1024]{2,1,0:T(8,1...) conditional(s32[]{:T(128)} %clamp.3, (f32[896]{0:T(1024)S(1)}, ...), branch_computations={%region_16.21_spmd, %region_21.26_spmd, %region_26.31_spmd} | conditional | flops 5659299328 | bytes 122619232 | solution.py:158
  531.7 2.5 copy.46
  534.2 2.0 convert_reduce_fusion.2
  536.8 5.5 multiply_reduce_fusion.6
  542.3 3.1 convolution_multiply_fusion.2
  545.4 2.0 copy.76
  550.2 4.2 fusion.41
  555.7 3.7 fusion.8
  559.4 4.6 copy.47
  564.7 4.9 broadcast_select_fusion
  571.0 2.8 broadcast_select_fusion.1
  573.8 5.0 select_n.90
  580.3 2.8 select_n.87
  583.0 263.2 %fusion.38 = (f32[8,1024]{1,0:T(8,128)S(1)}, f32[16,1024]{1,0:T(8,128)S(1)}) fusion(f32[384,1024]{1,0:T(8,128)} %select_n.87, f32[768,1024]{1,0:T(8,128)S(1)} %copy-done.8), kind=kCustom, calls=%all-reduce-scatter.2 | all-reduce-scatter fusion | flops 1572866 | bytes 4817920
  846.2 1.9 collective-permute-start
  854.7 6.4 collective-permute-start.13
  861.2 6.9 collective-permute-start.14
  868.0 7.0 collective-permute-start.2
  875.1 2.7 collective-permute-start.3
  879.2 6.1 collective-permute-start.5
  887.2 1.9 collective-permute-start.6
  889.2 2.8 collective-permute-start.7
  892.0 4.3 collective-permute-start.8
  896.3 3.4 collective-permute-start.9
  902.6 1.9 collective-permute-start.16
  904.5 3.9 collective-permute-start.17
  909.9 2.4 collective-permute-start.19
  912.3 5.0 collective-permute-start.20
  917.4 3.3 collective-permute-start.21
  922.2 2.5 collective-permute-start.23
  924.7 2.2 collective-permute-start.24
  927.0 2.0 collective-permute-start.25
  929.0 1.7 concatenate
  930.7 2.2 collective-permute-start.26
  940.4 2.2 concatenate.1
  943.3 1.6 fusion.12
  944.9 10.4 all-reduce.13
  955.4 184.4 %all-reduce.12 = (f32[96]{0:T(128)}, f32[192]{0:T(256)}, f32[256]{0:T(256)}, f32[3]{0:T(128)}) all-reduce(f32[96]{0:T(128)S(1)} %broadcast_select_fusion.4, f32[192]{0:T(256)S(1)} %slice_select_fusion, f32[256]{0:T(256)S(1)} %get-tuple-element.204, f32[3]{0:T(128)S(1)} %get-tuple-element.177), channel_id=1, replica_groups=mesh['dp'=64,'tensor'=4] {'dp'}, use_global_device_ids=true, to_apply=%region_36.37 | all-reduce | flops 547 | bytes 4376 | tf_op jit(solution)/shard_map/psum | solution.py:223
  1139.8 1.9 fusion.17
  (131 shorter events, 36.7 us)
Async XLA Ops:
  7.2 382.6 %copy-start = (bf16[128,1024]{1,0:T(8,128)(2,1)S(1)}, bf16[128,1024]{1,0:T(8,128)(2,1)}, u32[]{:S(2)}) copy-start(bf16[128,1024]{1,0:T(8,128)(2,1)} %param.16) | copy-start | bytes 786436
  7.2 382.6 %all-gather.2.cloned.1.call-start = ((), (), s32[]{:S(2)}) async-start(), calls=%async_computation.5 | async-start | bytes 8519680 | tf_op jit(solution)/shard_map/all_gather | solution.py:55
  7.9 444.5 %reduce-scatter.8.cloned.1.call-start = ((), (), s32[]{:S(2)}) async-start(), calls=%async_computation.6 | async-start | bytes 2621440 | tf_op jit(solution)/shard_map/reduce_scatter | solution.py:58
  397.4 55.0 %copy-start.12 = (bf16[128,1024]{1,0:T(8,128)(2,1)S(1)}, bf16[128,1024]{1,0:T(8,128)(2,1)}, u32[]{:S(2)}) copy-start(bf16[128,1024]{1,0:T(8,128)(2,1)} %param.18) | copy-start | bytes 786436
  397.4 65.9 %copy-start.16 = (f32[1024]{0:T(1024)S(1)}, f32[1024]{0:T(1024)}, u32[]{:S(2)}) copy-start(f32[1024]{0:T(1024)} %param.19) | copy-start | bytes 12292
  400.3 66.5 %all-to-all-start = ((bf16[64,1,14]{2,1,0:T(2,128)(2,1)}), bf16[64,1,14]{2,1,0:T(2,128)(2,1)S(1)}, u32[]{:S(2)}, u32[]{:S(2)}) async-start(bf16[64,1,14]{2,1,0:T(2,128)(2,1)} %convert_element_type.139), calls=%async_computation | async-start | bytes 65536 | tf_op jit(solution)/shard_map/all_to_all | solution.py:91
  466.8 60.3 %all-to-all-start.1 = ((bf16[64,14,1024]{2,1,0:T(8,128)(2,1)}), bf16[64,14,1024]{2,1,0:T(8,128)(2,1)}, u32[]{:S(2)}, u32[]{:S(2)}) async-start(bf16[64,14,1024]{2,1,0:T(8,128)(2,1)} %reshape.204), calls=%async_computation.2 | async-start | bytes 4194304 | tf_op jit(solution)/shard_map/all_to_all | solution.py:88
  477.7 53.2 %copy-start.5 = (bf16[896,1024]{1,0:T(8,128)(2,1)S(1)}, bf16[896,1024]{1,0:T(8,128)(2,1)}, u32[]{:S(2)}) copy-start(bf16[896,1024]{1,0:T(8,128)(2,1)} %param.20) | copy-start | bytes 5505028
  477.7 53.2 %copy-start.13 = (f32[768]{0:T(1024)S(1)}, f32[768]{0:T(1024)}, u32[]{:S(2)}) copy-start(f32[768]{0:T(1024)} %param.25) | copy-start | bytes 9220
  477.7 53.2 %copy-start.14 = (f32[384]{0:T(512)S(1)}, f32[384]{0:T(512)}, u32[]{:S(2)}) copy-start(f32[384]{0:T(512)} %param.24) | copy-start | bytes 4612
  477.8 53.2 %copy-start.17 = (f32[1024]{0:T(1024)S(1)}, f32[1024]{0:T(1024)}, u32[]{:S(2)}) copy-start(f32[1024]{0:T(1024)} %param.26) | copy-start | bytes 12292
  477.8 465.5 %reduce-scatter.12.cloned.1.call-start = ((), (), s32[]{:S(2)}) async-start(), calls=%async_computation.8 | async-start | bytes 4587520 | tf_op jit(solution)/shard_map/reduce_scatter | solution.py:175
  564.0 577.7 %reduce-scatter.10.cloned.1.call-start = ((), (), s32[]{:S(2)}) async-start(), calls=%async_computation.7 | async-start | bytes 4259840 | tf_op jit(solution)/shard_map/reduce_scatter | solution.py:221
  583.0 302.3 %copy-start.18 = (u32[256]{0:T(256)S(1)}, u32[256]{0:T(256)}, u32[]{:S(2)}) copy-start(u32[256]{0:T(256)} %constant.138) | copy-start | bytes 3076
  846.2 8.5 collective-permute-start
  848.1 5.2 collective-permute-start.15
  849.4 11.7 %collective-permute-start.1 = (f32[8,1024]{1,0:T(8,128)S(1)}, f32[8,1024]{1,0:T(8,128)S(1)}, u32[]{:S(2)}, u32[]{:S(2)}) collective-permute-start(f32[8,1024]{1,0:T(8,128)S(1)} %get-tuple-element.184), channel_id=1, source_target_pairs={{0,8},{4,12},{8,16},{12,20},{16,24},{20,28},{24,32},{28,36},{32,40... | collective-permute-start | bytes 98312
  850.7 17.3 %collective-permute-start.10 = (f32[8,1024]{1,0:T(8,128)S(1)}, f32[8,1024]{1,0:T(8,128)S(1)}, u32[]{:S(2)}, u32[]{:S(2)}) collective-permute-start(f32[8,1024]{1,0:T(8,128)S(1)} %get-tuple-element.184), channel_id=1, source_target_pairs={{0,44},{4,48},{8,52},{12,56},{16,60},{20,64},{24,68},{28,72},{32,7... | collective-permute-start | bytes 98312
  852.0 23.1 %collective-permute-start.11 = (f32[8,1024]{1,0:T(8,128)S(1)}, f32[8,1024]{1,0:T(8,128)S(1)}, u32[]{:S(2)}, u32[]{:S(2)}) collective-permute-start(f32[8,1024]{1,0:T(8,128)S(1)} %get-tuple-element.184), channel_id=1, source_target_pairs={{0,48},{4,52},{8,56},{12,60},{16,64},{20,68},{24,72},{28,76},{32,8... | collective-permute-start | bytes 98312
  853.4 24.5 %collective-permute-start.12 = (f32[8,1024]{1,0:T(8,128)S(1)}, f32[8,1024]{1,0:T(8,128)S(1)}, u32[]{:S(2)}, u32[]{:S(2)}) collective-permute-start(f32[8,1024]{1,0:T(8,128)S(1)} %get-tuple-element.184), channel_id=1, source_target_pairs={{0,52},{4,56},{8,60},{12,64},{16,68},{20,72},{24,76},{28,80},{32,8... | collective-permute-start | bytes 98312
  854.7 24.5 %collective-permute-start.13 = (f32[8,1024]{1,0:T(8,128)S(1)}, f32[8,1024]{1,0:T(8,128)S(1)}, u32[]{:S(2)}, u32[]{:S(2)}) collective-permute-start(f32[8,1024]{1,0:T(8,128)S(1)} %get-tuple-element.184), channel_id=1, source_target_pairs={{0,56},{4,60},{8,64},{12,68},{16,72},{20,76},{24,80},{28,84},{32,8... | collective-permute-start | bytes 98312
  861.2 26.1 %collective-permute-start.14 = (f32[8,1024]{1,0:T(8,128)S(1)}, f32[8,1024]{1,0:T(8,128)S(1)}, u32[]{:S(2)}, u32[]{:S(2)}) collective-permute-start(f32[8,1024]{1,0:T(8,128)S(1)} %get-tuple-element.184), channel_id=1, source_target_pairs={{0,60},{4,64},{8,68},{12,72},{16,76},{20,80},{24,84},{28,88},{32,9... | collective-permute-start | bytes 98312
  868.0 21.1 %collective-permute-start.2 = (f32[8,1024]{1,0:T(8,128)S(1)}, f32[8,1024]{1,0:T(8,128)S(1)}, u32[]{:S(2)}, u32[]{:S(2)}) collective-permute-start(f32[8,1024]{1,0:T(8,128)S(1)} %get-tuple-element.184), channel_id=1, source_target_pairs={{0,12},{4,16},{8,20},{12,24},{16,28},{20,32},{24,36},{28,40},{32,4... | collective-permute-start | bytes 98312
  875.1 16.9 %collective-permute-start.3 = (f32[8,1024]{1,0:T(8,128)S(1)}, f32[8,1024]{1,0:T(8,128)S(1)}, u32[]{:S(2)}, u32[]{:S(2)}) collective-permute-start(f32[8,1024]{1,0:T(8,128)S(1)} %get-tuple-element.184), channel_id=1, source_target_pairs={{0,16},{4,20},{8,24},{12,28},{16,32},{20,36},{24,40},{28,44},{32,4... | collective-permute-start | bytes 98312
  877.9 18.4 %collective-permute-start.4 = (f32[8,1024]{1,0:T(8,128)S(1)}, f32[8,1024]{1,0:T(8,128)S(1)}, u32[]{:S(2)}, u32[]{:S(2)}) collective-permute-start(f32[8,1024]{1,0:T(8,128)S(1)} %get-tuple-element.184), channel_id=1, source_target_pairs={{0,20},{4,24},{8,28},{12,32},{16,36},{20,40},{24,44},{28,48},{32,5... | collective-permute-start | bytes 98312
  879.2 20.5 %collective-permute-start.5 = (f32[8,1024]{1,0:T(8,128)S(1)}, f32[8,1024]{1,0:T(8,128)S(1)}, u32[]{:S(2)}, u32[]{:S(2)}) collective-permute-start(f32[8,1024]{1,0:T(8,128)S(1)} %get-tuple-element.184), channel_id=1, source_target_pairs={{0,24},{4,28},{8,32},{12,36},{16,40},{20,44},{24,48},{28,52},{32,5... | collective-permute-start | bytes 98312
  887.2 15.3 %collective-permute-start.6 = (f32[8,1024]{1,0:T(8,128)S(1)}, f32[8,1024]{1,0:T(8,128)S(1)}, u32[]{:S(2)}, u32[]{:S(2)}) collective-permute-start(f32[8,1024]{1,0:T(8,128)S(1)} %get-tuple-element.184), channel_id=1, source_target_pairs={{0,28},{4,32},{8,36},{12,40},{16,44},{20,48},{24,52},{28,56},{32,6... | collective-permute-start | bytes 98312
  889.2 15.3 %collective-permute-start.7 = (f32[8,1024]{1,0:T(8,128)S(1)}, f32[8,1024]{1,0:T(8,128)S(1)}, u32[]{:S(2)}, u32[]{:S(2)}) collective-permute-start(f32[8,1024]{1,0:T(8,128)S(1)} %get-tuple-element.184), channel_id=1, source_target_pairs={{0,32},{4,36},{8,40},{12,44},{16,48},{20,52},{24,56},{28,60},{32,6... | collective-permute-start | bytes 98312
  892.0 16.4 %collective-permute-start.8 = (f32[8,1024]{1,0:T(8,128)S(1)}, f32[8,1024]{1,0:T(8,128)S(1)}, u32[]{:S(2)}, u32[]{:S(2)}) collective-permute-start(f32[8,1024]{1,0:T(8,128)S(1)} %get-tuple-element.184), channel_id=1, source_target_pairs={{0,36},{4,40},{8,44},{12,48},{16,52},{20,56},{24,60},{28,64},{32,6... | collective-permute-start | bytes 98312
  896.3 13.6 %collective-permute-start.9 = (f32[8,1024]{1,0:T(8,128)S(1)}, f32[8,1024]{1,0:T(8,128)S(1)}, u32[]{:S(2)}, u32[]{:S(2)}) collective-permute-start(f32[8,1024]{1,0:T(8,128)S(1)} %get-tuple-element.184), channel_id=1, source_target_pairs={{0,40},{4,44},{8,48},{12,52},{16,56},{20,60},{24,64},{28,68},{32,7... | collective-permute-start | bytes 98312
  899.7 12.6 %collective-permute-start.31 = (f32[12,1024]{1,0:T(8,128)S(1)}, f32[12,1024]{1,0:T(8,128)S(1)}, u32[]{:S(2)}, u32[]{:S(2)}) collective-permute-start(f32[12,1024]{1,0:T(8,128)S(1)} %slice.58), channel_id=1, source_target_pairs={{0,64},{4,68},{8,72},{12,76},{16,80},{20,84},{24,88},{28,92},{32,9... | collective-permute-start | bytes 147464
  902.6 14.8 %collective-permute-start.16 = (f32[16,1024]{1,0:T(8,128)S(1)}, f32[16,1024]{1,0:T(8,128)S(1)}, u32[]{:S(2)}, u32[]{:S(2)}) collective-permute-start(f32[16,1024]{1,0:T(8,128)S(1)} %get-tuple-element.185), channel_id=1, source_target_pairs={{0,4},{4,8},{8,12},{12,16},{16,20},{20,24},{24,28},{28,32},{32,36}... | collective-permute-start | bytes 196616
  904.5 16.2 %collective-permute-start.17 = (f32[16,1024]{1,0:T(8,128)S(1)}, f32[16,1024]{1,0:T(8,128)S(1)}, u32[]{:S(2)}, u32[]{:S(2)}) collective-permute-start(f32[16,1024]{1,0:T(8,128)S(1)} %get-tuple-element.185), channel_id=1, source_target_pairs={{0,8},{4,12},{8,16},{12,20},{16,24},{20,28},{24,32},{28,36},{32,40... | collective-permute-start | bytes 196616
  908.4 13.8 %collective-permute-start.18 = (f32[16,1024]{1,0:T(8,128)S(1)}, f32[16,1024]{1,0:T(8,128)S(1)}, u32[]{:S(2)}, u32[]{:S(2)}) collective-permute-start(f32[16,1024]{1,0:T(8,128)S(1)} %get-tuple-element.185), channel_id=1, source_target_pairs={{0,12},{4,16},{8,20},{12,24},{16,28},{20,32},{24,36},{28,40},{32,4... | collective-permute-start | bytes 196616
  909.9 14.8 %collective-permute-start.19 = (f32[16,1024]{1,0:T(8,128)S(1)}, f32[16,1024]{1,0:T(8,128)S(1)}, u32[]{:S(2)}, u32[]{:S(2)}) collective-permute-start(f32[16,1024]{1,0:T(8,128)S(1)} %get-tuple-element.185), channel_id=1, source_target_pairs={{0,16},{4,20},{8,24},{12,28},{16,32},{20,36},{24,40},{28,44},{32,4... | collective-permute-start | bytes 196616
  912.3 14.6 %collective-permute-start.20 = (f32[16,1024]{1,0:T(8,128)S(1)}, f32[16,1024]{1,0:T(8,128)S(1)}, u32[]{:S(2)}, u32[]{:S(2)}) collective-permute-start(f32[16,1024]{1,0:T(8,128)S(1)} %get-tuple-element.185), channel_id=1, source_target_pairs={{0,20},{4,24},{8,28},{12,32},{16,36},{20,40},{24,44},{28,48},{32,5... | collective-permute-start | bytes 196616
  917.4 13.3 %collective-permute-start.21 = (f32[16,1024]{1,0:T(8,128)S(1)}, f32[16,1024]{1,0:T(8,128)S(1)}, u32[]{:S(2)}, u32[]{:S(2)}) collective-permute-start(f32[16,1024]{1,0:T(8,128)S(1)} %get-tuple-element.185), channel_id=1, source_target_pairs={{0,24},{4,28},{8,32},{12,36},{16,40},{20,44},{24,48},{28,52},{32,5... | collective-permute-start | bytes 196616
  920.7 12.2 %collective-permute-start.22 = (f32[16,1024]{1,0:T(8,128)S(1)}, f32[16,1024]{1,0:T(8,128)S(1)}, u32[]{:S(2)}, u32[]{:S(2)}) collective-permute-start(f32[16,1024]{1,0:T(8,128)S(1)} %get-tuple-element.185), channel_id=1, source_target_pairs={{0,28},{4,32},{8,36},{12,40},{16,44},{20,48},{24,52},{28,56},{32,6... | collective-permute-start | bytes 196616
  922.2 12.0 %collective-permute-start.23 = (f32[16,1024]{1,0:T(8,128)S(1)}, f32[16,1024]{1,0:T(8,128)S(1)}, u32[]{:S(2)}, u32[]{:S(2)}) collective-permute-start(f32[16,1024]{1,0:T(8,128)S(1)} %get-tuple-element.185), channel_id=1, source_target_pairs={{0,32},{4,36},{8,40},{12,44},{16,48},{20,52},{24,56},{28,60},{32,6... | collective-permute-start | bytes 196616
  924.7 10.8 collective-permute-start.24
  927.0 10.0 collective-permute-start.25
  930.7 8.2 collective-permute-start.26
  932.9 6.0 collective-permute-start.27
  934.2 4.7 collective-permute-start.28
  935.5 3.4 collective-permute-start.29
  937.0 3.4 collective-permute-start.30
  943.3 196.5 %copy-start.9 = (f32[896,1,256]{2,0,1:T(8,128)S(1)}, f32[896,1,256]{2,0,1:T(8,128)}, u32[]{:S(2)}) copy-start(f32[896,1,256]{2,0,1:T(8,128)} %reduce-scatter.12.cloned.1.call-done) | copy-start | bytes 2752516
  943.3 198.4 %copy-start.1 = (bf16[128,1024]{1,0:T(8,128)(2,1)S(1)}, bf16[128,1024]{1,0:T(8,128)(2,1)}, u32[]{:S(2)}) copy-start(bf16[128,1024]{1,0:T(8,128)(2,1)} %param.16) | copy-start | bytes 786436
  (7 other events, 81.3 us)
Sparse Core Ops, SparseCore 0:
  9.8 379.9 all-gather.1
  397.6 54.7 reduce-scatter.7
  564.1 92.5 reduce-scatter.11
  659.6 394.8 reduce-scatter.9
where the time goes:
time: 1150 us
  waiting for transfers between devices  469 us (41%)
  blocking collectives  468 us (41%)
  starting transfers between devices  107 us (9%)
  local copies, waits for them, and re-layouts  35.2 us (3%)
  other arithmetic  23.1 us (2%)
  matrix products  22.3 us (2%)
  between operations  21.8 us (2%)
    all_gather x1, waiting for transfers between devices, per_device(): lax.all_gather(out_proj, 'dp', axis=1, tiled=True)  382 us
    unnamed x1, blocking collectives  263 us
    psum x1, blocking collectives, per_device(): lax.psum((gain_terms[0], gain_terms[1], gain_terms[2], loss_values_all),...  184 us
    unnamed x32, starting transfers between devices  86.2 us
    all_to_all x1, waiting for transfers between devices, per_device(): lax.all_to_all(send_target.reshape(shards, slot_cap, -1), 'dp', split_axi...  43.1 us
    reduce_scatter x1, waiting for transfers between devices, per_device(): lax.psum_scatter(partial_sum, 'tensor', scatter_dimension=1, tiled=True)  42 us
  transfers between devices with their start and end apart: 38, of which 5 were waited for; matrix products, arithmetic and copies ran while one was open for 26% of the time, Pallas kernels for 0%

commit v1 on v0

v1 whole, which is shorter than its diff:
```python
import math

import jax
import jax.numpy as jnp
from jax import lax
from jax.sharding import Mesh
from jax.sharding import PartitionSpec as P

D = 4096
TOKENS = 8192
ROWS = 128
SHARDS = 64
CAP = 14
SLOT = 16
GROUPS = (12, 20, 32)
WIDTHS = (384, 768, 1024)
OFFSETS = (512, 256, 0)
PADDED = (128, 256, 256)
BLOCK = 640
ROOT = math.sqrt(TOKENS)
F32 = jnp.float32
BF16 = jnp.bfloat16
SWAP = [(0, 1), (1, 0)]


def shifted(value, axis, step):
    return lax.ppermute(value, axis, [(i, (i + step) % 4) for i in range(4)])


def gather4(value, axis):
    pos = lax.axis_index(axis)
    out = jnp.zeros((4,) + value.shape, value.dtype)
    parts = [value] + [shifted(value, axis, step) for step in (1, 2, 3)]
    for step in range(4):
        out = lax.dynamic_update_index_in_dim(out, parts[step], (pos + 4 - step) % 4, 0)
    return out


def reduce4(blocks, axis):
    pos = lax.axis_index(axis)
    total = lax.dynamic_index_in_dim(blocks, pos, 0, keepdims=False).astype(F32)
    for step in (1, 2, 3):
        part = lax.dynamic_index_in_dim(blocks, (pos + step) % 4, 0, keepdims=False)
        total = total + shifted(part.astype(BF16), axis, step).astype(F32)
    return total


def gather2(value, axis):
    pos = lax.axis_index(axis)
    other = lax.ppermute(value, axis, SWAP)
    first = jnp.where(pos == 0, value, other)
    second = jnp.where(pos == 0, other, value)
    return jnp.stack([first, second])


def sum2(value, axis):
    return value + lax.ppermute(value, axis, SWAP)


def pick(value, index, axis):
    return lax.dynamic_index_in_dim(value, index, axis, keepdims=False)


def pad_head(head, index):
    quarter = WIDTHS[index] // 4
    blocks = head.reshape(4, quarter, head.shape[1])
    blocks = jnp.pad(blocks, ((0, 0), (0, PADDED[index] - quarter), (0, 0)))
    return blocks.reshape(4 * PADDED[index], head.shape[1])


def pad_gain(gain, index):
    quarter = WIDTHS[index] // 4
    return jnp.pad(gain.reshape(4, quarter), ((0, 0), (0, PADDED[index] - quarter)))


def teacher_sum(attn_out, out_proj):
    y = lax.axis_index("y")
    zh = lax.axis_index("zh")
    c = lax.axis_index("c")
    weights = gather4(out_proj.T, "zl").reshape(256, 1024)
    weights = gather4(weights, "x").reshape(1024, 1024)
    rows = gather4(attn_out, "y").reshape(512, 1024)
    partial = lax.dot_general(rows, weights, (((1,), (1,)), ((), ())), preferred_element_type=F32)
    partial = partial.reshape(2, 2, ROWS, 1024)
    mine = pick(partial, c, 1)
    other = pick(partial, 1 - c, 1).astype(BF16)
    pair = (mine + lax.ppermute(other, "c", SWAP).astype(F32)).astype(BF16)
    total = None
    for k in range(2):
        links = []
        for py in range(4):
            for pzh in range(2):
                for pc in range(2):
                    links.append(((py * 2 + pzh) * 2 + pc, (pc + 2 * ((pzh + k) % 2)) * 4 + py))
        part = lax.ppermute(pick(pair, (zh + k) % 2, 0), ("y", "zh", "c"), links).astype(F32)
        total = part if total is None else total + part
    return total


def per_device(
    attn_out,
    out_proj,
    residual,
    teacher_gain,
    student_feats,
    head_small,
    head_base,
    head_large,
    gain_small,
    gain_base,
    gain_large,
    row_shard,
):
    zh = lax.axis_index("zh")
    c = lax.axis_index("c")
    tensor = zh * 2 + c
    heads = [pad_head(h, i) for i, h in enumerate((head_small, head_base, head_large))]
    gains = [pad_gain(g, i) for i, g in enumerate((gain_small, gain_base, gain_large))]

    shard_ids = jnp.arange(SHARDS, dtype=jnp.int32)
    lower = jnp.arange(ROWS)[:, None] > jnp.arange(ROWS)[None, :]
    slot_ids = jnp.arange(SHARDS * SLOT, dtype=jnp.int32)
    onehots, selectors = [], []
    for i in range(3):
        column = row_shard[:, i]
        onehots.append((column[:, None] == shard_ids[None, :]).astype(F32))
        same = (column[:, None] == column[None, :]) & lower
        rank = jnp.sum(same.astype(jnp.int32), axis=1)
        place = column * SLOT + rank
        selectors.append((place[:, None] == slot_ids[None, :]).astype(BF16))
    own_counts = jnp.concatenate([jnp.sum(o, axis=0) for o in onehots])

    feats = lax.dynamic_slice(student_feats, (0, tensor * 256), (SHARDS * CAP, 256))
    counts_row = jnp.pad(own_counts.astype(BF16), (0, 64))
    extra = jnp.broadcast_to(counts_row[None, None, :], (SHARDS, 1, 256))
    sent = jnp.concatenate(
        [feats.reshape(SHARDS, CAP, 256), extra, jnp.zeros((SHARDS, 1, 256), BF16)], axis=1
    )
    got = lax.all_to_all(sent, ("y", "x", "zl"), 0, 0, tiled=True)
    counts = jnp.sum(got[:, CAP, :192].astype(F32), axis=0)
    got = got.reshape(SHARDS * SLOT, 256)
    parts = [None] * 3
    for i in range(3):
        block = jnp.dot(selectors[i], got, preferred_element_type=F32).astype(BF16)
        quarter = WIDTHS[i] // 4
        parts[i] = jnp.pad(block[:, :quarter], ((0, 0), (0, PADDED[i] - quarter)))
    block = jnp.concatenate([parts[2], parts[1], parts[0]], axis=1)
    blocks = gather2(gather2(block, "c"), "zh").reshape(4, ROWS, BLOCK)

    xhats, normeds, scales, outs, weights = [], [], [], [], []
    for i in range(3):
        x = blocks[:, :, OFFSETS[i] : OFFSETS[i] + PADDED[i]].astype(F32)
        center = jnp.sum(x, axis=(0, 2)) / WIDTHS[i]
        spread = jnp.sum(x * x, axis=(0, 2)) / WIDTHS[i] - center * center
        scale = lax.rsqrt(spread + 1e-06)
        xhat = (x - center[None, :, None]) * scale[None, :, None]
        normed = (xhat * gains[i][:, None, :]).astype(BF16)
        normed = jnp.transpose(normed, (1, 0, 2)).reshape(ROWS, 4 * PADDED[i])
        xhats.append(xhat)
        scales.append(scale)
        normeds.append(normed)
        outs.append(jnp.dot(normed, heads[i], preferred_element_type=F32))
        owned = jnp.sum(onehots[i] * counts[None, 64 * i : 64 * i + 64], axis=1)
        weights.append(TOKENS / (GROUPS[i] * owned))

    hidden = residual.astype(F32) + teacher_sum(attn_out, out_proj)
    sums = jnp.stack([jnp.sum(hidden, axis=1), jnp.sum(hidden * hidden, axis=1)])
    sums = sum2(sum2(sums, "c"), "zh")
    center = sums[0] / D
    spread = sums[1] / D - center * center
    target = (
        (hidden - center[:, None]) * lax.rsqrt(spread + 1e-06)[:, None] * teacher_gain
    ).astype(BF16).astype(F32)

    grads, backs, moments = [], [], []
    for i in range(3):
        diff = outs[i] - target
        error = (weights[i][:, None] * diff).astype(BF16)
        grad = lax.dot_general(normeds[i], error, (((0,), (0,)), ((), ())), preferred_element_type=F32)
        grad = (grad / ROOT).astype(BF16).reshape(4, PADDED[i], 1024)
        grads.append(grad[:, : WIDTHS[i] // 4])
        back = lax.dot_general(error, heads[i], (((1,), (1,)), ((), ())), preferred_element_type=F32)
        back = jnp.transpose(back.reshape(ROWS, 4, PADDED[i]), (1, 0, 2))
        backs.append(back)
        upper = back * gains[i][:, None, :]
        moments.append(jnp.sum(upper, axis=(0, 2)))
        moments.append(jnp.sum(upper * xhats[i], axis=(0, 2)))
        moments.append(weights[i] * jnp.sum(diff * diff, axis=1))

    back = jnp.concatenate([backs[2], backs[1], backs[0]], axis=2).reshape(2, 2, ROWS, BLOCK)
    back = pick(back, c, 1) + lax.ppermute(pick(back, 1 - c, 1).astype(BF16), "c", SWAP).astype(F32)
    back = pick(back, zh, 0) + lax.ppermute(pick(back, 1 - zh, 0).astype(BF16), "zh", SWAP).astype(F32)
    moments = sum2(sum2(jnp.stack(moments), "c"), "zh")

    slots = jnp.zeros((SHARDS * SLOT, 256), F32)
    gain_parts = []
    for i in range(3):
        quarter = WIDTHS[i] // 4
        mine = back[:, OFFSETS[i] : OFFSETS[i] + PADDED[i]]
        xhat = pick(xhats[i], tensor, 0)
        upper = mine * pick(gains[i], tensor, 0)[None, :]
        first = moments[3 * i][:, None] / WIDTHS[i]
        second = moments[3 * i + 1][:, None] / WIDTHS[i]
        rows = scales[i][:, None] * (upper - first - xhat * second)
        rows = jnp.pad(rows[:, :quarter], ((0, 0), (0, 256 - quarter))).astype(BF16)
        slots = slots + lax.dot_general(
            selectors[i], rows, (((0,), (0,)), ((), ())), preferred_element_type=F32
        )
        gain_parts.append(jnp.sum(mine * xhat, axis=0)[:quarter] / ROOT)
    slots = slots.astype(BF16).reshape(SHARDS, SLOT, 256)
    token_gradient = lax.all_to_all(slots, ("y", "x", "zl"), 0, 0, tiled=True)
    token_gradient = token_gradient[:, :CAP].reshape(SHARDS * CAP, 256)

    tree = jnp.concatenate([grads[2], grads[1], grads[0]], axis=1)
    tree = reduce4(tree, "y")
    edges = (0, 256, 448, 544)
    for axis in ("x", "zl"):
        tree = jnp.concatenate(
            [tree[edges[j] : edges[j + 1]].reshape(4, -1, 1024) for j in range(3)], axis=1
        )
        tree = reduce4(tree, axis)
        edges = tuple(e // 4 for e in edges)

    losses = jnp.stack([jnp.sum(moments[3 * i + 2]) for i in range(3)]) / (2.0 * D * TOKENS)
    small = jnp.concatenate(gain_parts + [losses, jnp.zeros((1024 - 547,), F32)]).reshape(8, 128)
    for axis in ("y", "x", "zl"):
        small = small + shifted(small, axis, 1) + shifted(small, axis, 2) + shifted(small, axis, 3)
    small = small.reshape(1024)
    return (
        tree[28:34],
        tree[16:28],
        tree[0:16],
        small[0:96],
        small[96:288],
        small[288:544],
        token_gradient,
        small[544:547],
    )


def solution(mesh):
    fine = Mesh(mesh.devices.reshape(4, 4, 4, 2, 2), ("y", "x", "zl", "zh", "c"))
    dp = ("y", "x", "zl")
    tp = ("zh", "c")
    return jax.shard_map(
        per_device,
        mesh=fine,
        in_specs=(
            P(dp, tp),
            P(tp, dp),
            P(dp, tp),
            P(tp),
            P(dp, None),
            P(None, tp),
            P(None, tp),
            P(None, tp),
            P(),
            P(),
            P(),
            P(dp, None),
        ),
        out_specs=(
            P(dp, tp),
            P(dp, tp),
            P(dp, tp),
            P(tp),
            P(tp),
            P(tp),
            P(dp, tp),
            P(),
        ),
        check_vma=False,
    )
```

time: 1150 us -> 273 us (0.24)
  blocking collectives: 468 us -> 0 us
  waiting for transfers between devices: 469 us -> 79.2 us
  between operations: 21.8 us -> 1.94 us
    all_gather x1 -> x0, waiting for transfers between devices: 382 us -> none  [per_device(): lax.all_gather(out_proj, 'dp', axis=1, tiled=True)]
    unnamed x1 -> x0, blocking collectives: 263 us -> none
    psum x3 -> x0, blocking collectives: 205 us -> none  [the longest x1 184 us: per_device(): lax.psum((gain_terms[0], gain_terms[1], gain_terms[2], loss_values_all),...]
    ppermute x0 -> x38, starting transfers between devices: none -> 91.4 us  [the longest x27 65.5 us: shifted(): return lax.ppermute(value, axis, [(i, (i + step) % 4) for i in range(4)])]
    unnamed x32 -> x0, starting transfers between devices: 86.2 us -> none
    ppermute x0 -> x38, waiting for transfers between devices: none -> 79.2 us  [the longest x27 47.2 us: shifted(): return lax.ppermute(value, axis, [(i, (i + step) % 4) for i in range(4)])]
    all_to_all x2, waiting for transfers between devices: 43.1 us -> 0.01 us  [the longest x1 0.01 us: per_device(): got = lax.all_to_all(sent, ('y', 'x', 'zl'), 0, 0, tiled=True)]
    reduce_scatter x3 -> x0, waiting for transfers between devices: 42 us -> none  [the longest x1 42 us: per_device(): lax.psum_scatter(partial_sum, 'tensor', scatter_dimension=1, tiled=True)]
  transfers between devices with their start and end apart: 38 -> 40, of which waited for: 5 -> 11; matrix products, arithmetic and copies ran while one was open for 26% -> 19% of each run, Pallas kernels for 0% -> 0%
where the time goes in v1:
time: 273 us; the launch traced here: 267 us
  starting transfers between devices  106 us (39%)
  waiting for transfers between devices  79.2 us (29%)
  local copies, waits for them, and re-layouts  36.1 us (13%)
  other arithmetic  26 us (10%)
  matrix products  18.1 us (7%)
    ppermute x27, starting transfers between devices, shifted(): return lax.ppermute(value, axis, [(i, (i + step) % 4) for i in range(4)])  65.5 us
    ppermute x27, waiting for transfers between devices, shifted(): return lax.ppermute(value, axis, [(i, (i + step) % 4) for i in range(4)])  47.2 us
    ppermute x2, waiting for transfers between devices, teacher_sum(): lax.ppermute(pick(pair, (zh + k) % 2, 0), ('y', 'zh', 'c'), links)  19.6 us
    ppermute x2, starting transfers between devices, teacher_sum(): lax.ppermute(pick(pair, (zh + k) % 2, 0), ('y', 'zh', 'c'), links)  10.6 us
    ppermute x2, waiting for transfers between devices, gather2(): other = lax.ppermute(value, axis, SWAP)  8.2 us
    all_to_all x1, starting transfers between devices, per_device(): got = lax.all_to_all(sent, ('y', 'x', 'zl'), 0, 0, tiled=True)  8.18 us
    dynamic_update_slice x12, local copies, waits for them, and re-layouts, gather4(): lax.dynamic_update_index_in_dim(out, parts[step], (pos + 4 - step) % 4, 0)  7.73 us
    all_to_all x1, starting transfers between devices, per_device(): token_gradient = lax.all_to_all(slots, ('y', 'x', 'zl'), 0, 0, tiled=True)  6.44 us
  transfers between devices with their start and end apart: 40, of which 11 were waited for; matrix products, arithmetic and copies ran while one was open for 19% of the time, Pallas kernels for 0%

profile of v1, /device:TPU:32, one launch (start us, length us, event | category | flops | bytes accessed | tf_op | source)
XLA Modules:
  0.0 267.4 jit_solution(2943070416694047550)
XLA Ops:
  0.6 3.4 %collective-permute-start.6 = (bf16[64,1024]{1,0:T(8,128)(2,1)}, bf16[64,1024]{1,0:T(8,128)(2,1)}, u32[]{:S(2)}, u32[]{:S(2)}) collective-permute-start(bf16[64,1024]{1,0:T(8,128)(2,1)} %bitcast.307), channel_id=1, source_target_pairs={{0,8},{4,12},{8,0},{12,4},{1,9},{5,13},{9,1},{13,5},{2,10},{6,14},... | collective-permute-start | bytes 393224 | tf_op jit(solution)/shard_map/ppermute | solution.py:27
  4.0 2.0 collective-permute-start.7
  6.0 1.6 collective-permute-start.2
  7.6 1.7 collective-permute-start.4
  13.0 8.2 %all-to-all-start = ((bf16[64,16,256]{2,1,0:T(8,128)(2,1)}), bf16[64,16,256]{2,1,0:T(8,128)(2,1)S(1)}, u32[]{:S(2)}, u32[]{:S(2)}) async-start(bf16[64,16,256]{2,1,0:T(8,128)(2,1)} %maximum_maximum_fusion), calls=%async_computation | async-start | bytes 1048576 | tf_op jit(solution)/shard_map/all_to_all | solution.py:139
  21.2 1.4 convert_reduce_fusion.5
  28.0 3.1 %collective-permute-start.3 = (bf16[128,1024]{1,0:T(8,128)(2,1)S(1)}, bf16[128,1024]{1,0:T(8,128)(2,1)S(1)}, u32[]{:S(2)}, u32[]{:S(2)}) collective-permute-start(bf16[128,1024]{1,0:T(8,128)(2,1)S(1)} %copy-done.18), channel_id=1, source_target_pairs={{0,128},{64,192},{128,0},{192,64},{1,129},{65,193},{129,1},{193,65... | collective-permute-start | bytes 786440 | tf_op jit(solution)/shard_map/ppermute | solution.py:27
  33.8 2.8 %collective-permute-start.10 = (bf16[256,1024]{1,0:T(8,128)(2,1)S(1)}, bf16[256,1024]{1,0:T(8,128)(2,1)S(1)}, u32[]{:S(2)}, u32[]{:S(2)}) collective-permute-start(bf16[256,1024]{1,0:T(8,128)(2,1)S(1)} %bitcast.296), channel_id=1, source_target_pairs={{0,48},{16,0},{32,16},{48,32},{1,49},{17,1},{33,17},{49,33},{2,50}... | collective-permute-start | bytes 1572872 | tf_op jit(solution)/shard_map/ppermute | solution.py:27
  38.8 1.7 bitcast_dynamic-update-slice_fusion.6
  41.2 1.7 bitcast_dynamic-update-slice_fusion.4
  42.8 17.7 %collective-permute-done.8 = bf16[256,1024]{1,0:T(8,128)(2,1)S(1)} collective-permute-done((bf16[256,1024]{1,0:T(8,128)(2,1)S(1)}, bf16[256,1024]{1,0:T(8,128)(2,1)S(1)}, u32[]{:S(2)}, u32[]{:S(2)}) %collective-permute-start.8) | collective-permute-done | bytes 524320 | tf_op jit(solution)/shard_map/ppermute | solution.py:27
  60.7 2.5 fusion.113
  69.7 9.9 %collective-permute-start.13 = (bf16[128,1024]{1,0:T(8,128)(2,1)S(1)}, bf16[128,1024]{1,0:T(8,128)(2,1)S(1)}, u32[]{:S(2)}, u32[]{:S(2)}) collective-permute-start(bf16[128,1024]{1,0:T(8,128)(2,1)S(1)} %get-tuple-element.52), channel_id=1, source_target_pairs={{0,128},{1,192},{2,0},{3,64},{64,129},{65,193},{66,1},{67,65},{128... | collective-permute-start | bytes 786440 | tf_op jit(solution)/shard_map/ppermute | solution.py:95
  81.0 19.6 %collective-permute-done.13 = bf16[128,1024]{1,0:T(8,128)(2,1)S(1)} collective-permute-done((bf16[128,1024]{1,0:T(8,128)(2,1)S(1)}, bf16[128,1024]{1,0:T(8,128)(2,1)S(1)}, u32[]{:S(2)}, u32[]{:S(2)}) %collective-permute-start.13) | collective-permute-done | bytes 262176 | tf_op jit(solution)/shard_map/ppermute | solution.py:95
  102.1 2.5 collective-permute-start.15
  104.7 3.6 %collective-permute-start.1 = (bf16[2,128,640]{2,1,0:T(8,128)(2,1)S(1)}, bf16[2,128,640]{2,1,0:T(8,128)(2,1)S(1)}, u32[]{:S(2)}, u32[]{:S(2)}) collective-permute-start(bf16[2,128,640]{2,1,0:T(8,128)(2,1)S(1)} %pad_maximum_fusion.5), channel_id=1, source_target_pairs={{0,2},{2,0},{1,3},{3,1},{4,6},{6,4},{5,7},{7,5},{8,10},{10,8},{9,1... | collective-permute-start | bytes 983048 | tf_op jit(solution)/shard_map/ppermute | solution.py:50
  108.3 1.5 collective-permute-done.15
  110.0 8.2 %collective-permute-done.1 = bf16[2,128,640]{2,1,0:T(8,128)(2,1)S(1)} collective-permute-done((bf16[2,128,640]{2,1,0:T(8,128)(2,1)S(1)}, bf16[2,128,640]{2,1,0:T(8,128)(2,1)S(1)}, u32[]{:S(2)}, u32[]{:S(2)}) %collective-permute-start.1) | collective-permute-done | bytes 327712 | tf_op jit(solution)/shard_map/ppermute | solution.py:50
  122.5 2.1 multiply_convert_fusion.1
  125.9 1.6 copy.30
  127.5 1.8 copy.29
  129.3 2.1 multiply_reduce_fusion.2
  132.4 1.7 multiply_reduce_fusion.8
  137.0 2.4 multiply_reduce_fusion.1
  139.4 1.5 stack.78
  143.8 1.4 copy-done.2
  145.8 3.6 %collective-permute-start.28 = (f32[9,128]{1,0:T(8,128)S(1)}, f32[9,128]{1,0:T(8,128)S(1)}, u32[]{:S(2)}, u32[]{:S(2)}) collective-permute-start(f32[9,128]{1,0:T(8,128)S(1)} %add.420), channel_id=1, source_target_pairs={{0,2},{2,0},{1,3},{3,1},{4,6},{6,4},{5,7},{7,5},{8,10},{10,8},{9,1... | collective-permute-start | bytes 13832 | tf_op jit(solution)/shard_map/ppermute | solution.py:57
  149.4 1.9 dynamic-slice_bitcast_fusion.2
  151.3 1.6 collective-permute-start.16
  152.9 10.2 %collective-permute-start.18 = (bf16[544,1024]{1,0:T(8,128)(2,1)}, bf16[544,1024]{1,0:T(8,128)(2,1)}, u32[]{:S(2)}, u32[]{:S(2)}) collective-permute-start(bf16[544,1024]{1,0:T(8,128)(2,1)} %get-tuple-element.36), channel_id=1, source_target_pairs={{0,192},{64,0},{128,64},{192,128},{1,193},{65,1},{129,65},{193,129... | collective-permute-start | bytes 3342344 | tf_op jit(solution)/shard_map/ppermute | solution.py:27
  163.1 9.3 %collective-permute-start.17 = (bf16[544,1024]{1,0:T(8,128)(2,1)}, bf16[544,1024]{1,0:T(8,128)(2,1)}, u32[]{:S(2)}, u32[]{:S(2)}) collective-permute-start(bf16[544,1024]{1,0:T(8,128)(2,1)} %get-tuple-element.37), channel_id=1, source_target_pairs={{0,128},{64,192},{128,0},{192,64},{1,129},{65,193},{129,1},{193,65... | collective-permute-start | bytes 3342344 | tf_op jit(solution)/shard_map/ppermute | solution.py:27
  172.5 4.8 %collective-permute-start.26 = (bf16[128,640]{1,0:T(8,128)(2,1)S(1)}, bf16[128,640]{1,0:T(8,128)(2,1)S(1)}, u32[]{:S(2)}, u32[]{:S(2)}) collective-permute-start(bf16[128,640]{1,0:T(8,128)(2,1)S(1)} %fusion.46), channel_id=1, source_target_pairs={{0,2},{2,0},{1,3},{3,1},{4,6},{6,4},{5,7},{7,5},{8,10},{10,8},{9,1... | collective-permute-start | bytes 491528 | tf_op jit(solution)/shard_map/ppermute | solution.py:192
  178.5 2.6 maximum_multiply_fusion
  181.9 1.5 multiply_reduce_fusion.10
  186.1 2.1 collective-permute-start.31
  190.2 20.5 %collective-permute-done.30 = f32[8,128]{1,0:T(8,128)S(1)} collective-permute-done((f32[8,128]{1,0:T(8,128)S(1)}, f32[8,128]{1,0:T(8,128)S(1)}, u32[]{:S(2)}, u32[]{:S(2)}) %collective-permute-start.30) | collective-permute-done | bytes 4128 | tf_op jit(solution)/shard_map/ppermute | solution.py:27
  210.7 9.9 %collective-permute-start.29 = (f32[8,128]{1,0:T(8,128)S(1)}, f32[8,128]{1,0:T(8,128)S(1)}, u32[]{:S(2)}, u32[]{:S(2)}) collective-permute-start(f32[8,128]{1,0:T(8,128)S(1)} %bitcast.312), channel_id=1, source_target_pairs={{0,64},{64,128},{128,192},{192,0},{1,65},{65,129},{129,193},{193,1... | collective-permute-start | bytes 12296 | tf_op jit(solution)/shard_map/ppermute | solution.py:27
  221.8 1.5 collective-permute-done.29
  225.5 3.2 %fusion.1 = f32[544,1024]{1,0:T(8,128)S(1)} fusion(bf16[544,1024]{1,0:T(8,128)(2,1)} %collective-permute-done.18, bf16[544,1024]{1,0:T(8,128)(2,1)} %collective-permute-done.17, bf16[544,1024]{1,0:T(8,128)(2,1)} %collective-permute-done.16, bf16[4,544,1024]{2,1,0:T(8,128)(2,1)} %copy-done.1, s32[]{:T(128)S(6)} %select_n.237), kind=kLoop, calls=%fused_computation.6 | loop fusion | flops 3899392 | bytes 6684676 | tf_op jit(solution)/shard_map/add | solution.py:44
  231.4 1.9 collective-permute-start.19
  234.7 2.7 %collective-permute-start.20 = (bf16[136,1024]{1,0:T(8,128)(2,1)S(1)}, bf16[136,1024]{1,0:T(8,128)(2,1)}, u32[]{:S(2)}, u32[]{:S(2)}) collective-permute-start(bf16[136,1024]{1,0:T(8,128)(2,1)S(1)} %get-tuple-element.40), channel_id=1, source_target_pairs={{0,32},{16,48},{32,0},{48,16},{1,33},{17,49},{33,1},{49,17},{2,34}... | collective-permute-start | bytes 835592 | tf_op jit(solution)/shard_map/ppermute | solution.py:27
  238.7 6.4 %all-to-all-start.1 = ((bf16[64,16,256]{2,1,0:T(8,128)(2,1)}), bf16[64,16,256]{2,1,0:T(8,128)(2,1)S(1)}, u32[]{:S(2)}, u32[]{:S(2)}) async-start(bf16[64,16,256]{2,1,0:T(8,128)(2,1)} %bitcast.106), calls=%async_computation.1 | async-start | bytes 1048576 | tf_op jit(solution)/shard_map/all_to_all | solution.py:211
  245.9 2.5 collective-permute-start.36
  248.4 2.4 collective-permute-start.35
  250.7 1.5 fusion.22
  252.5 2.0 collective-permute-start.24
  254.6 4.5 %collective-permute-done.37 = f32[8,128]{1,0:T(8,128)S(1)} collective-permute-done((f32[8,128]{1,0:T(8,128)S(1)}, f32[8,128]{1,0:T(8,128)S(1)}, u32[]{:S(2)}, u32[]{:S(2)}) %collective-permute-start.37) | collective-permute-done | bytes 4128 | tf_op jit(solution)/shard_map/ppermute | solution.py:27
  261.4 2.9 %collective-permute-done.23 = bf16[34,1024]{1,0:T(8,128)(2,1)S(1)} collective-permute-done((bf16[34,1024]{1,0:T(8,128)(2,1)S(1)}, bf16[34,1024]{1,0:T(8,128)(2,1)S(1)}, u32[]{:S(2)}, u32[]{:S(2)}) %collective-permute-start.23) | collective-permute-done | bytes 69664 | tf_op jit(solution)/shard_map/ppermute | solution.py:27
  (277 shorter events, 58.3 us)
Async XLA Ops:
  0.6 119.8 %copy-start = (bf16[1024,1024]{1,0:T(8,128)(2,1)S(1)}, bf16[1024,1024]{1,0:T(8,128)(2,1)}, u32[]{:S(2)}) copy-start(bf16[1024,1024]{1,0:T(8,128)(2,1)} %param.19) | copy-start | bytes 6291460
  0.6 31.3 %collective-permute-start.6 = (bf16[64,1024]{1,0:T(8,128)(2,1)}, bf16[64,1024]{1,0:T(8,128)(2,1)}, u32[]{:S(2)}, u32[]{:S(2)}) collective-permute-start(bf16[64,1024]{1,0:T(8,128)(2,1)} %bitcast.307), channel_id=1, source_target_pairs={{0,8},{4,12},{8,0},{12,4},{1,9},{5,13},{9,1},{13,5},{2,10},{6,14},... | collective-permute-start | bytes 393224 | tf_op jit(solution)/shard_map/ppermute | solution.py:27
  4.0 24.0 %collective-permute-start.5 = (bf16[64,1024]{1,0:T(8,128)(2,1)}, bf16[64,1024]{1,0:T(8,128)(2,1)}, u32[]{:S(2)}, u32[]{:S(2)}) collective-permute-start(bf16[64,1024]{1,0:T(8,128)(2,1)} %bitcast.308), channel_id=1, source_target_pairs={{0,4},{4,8},{8,12},{12,0},{1,5},{5,9},{9,13},{13,1},{2,6},{6,10},{... | collective-permute-start | bytes 393224 | tf_op jit(solution)/shard_map/ppermute | solution.py:27
  4.0 28.9 %collective-permute-start.7 = (bf16[64,1024]{1,0:T(8,128)(2,1)}, bf16[64,1024]{1,0:T(8,128)(2,1)}, u32[]{:S(2)}, u32[]{:S(2)}) collective-permute-start(bf16[64,1024]{1,0:T(8,128)(2,1)} %bitcast.309), channel_id=1, source_target_pairs={{0,12},{4,0},{8,4},{12,8},{1,13},{5,1},{9,5},{13,9},{2,14},{6,2},{... | collective-permute-start | bytes 393224 | tf_op jit(solution)/shard_map/ppermute | solution.py:27
  6.0 31.8 %collective-permute-start.2 = (bf16[128,1024]{1,0:T(8,128)(2,1)}, bf16[128,1024]{1,0:T(8,128)(2,1)}, u32[]{:S(2)}, u32[]{:S(2)}) collective-permute-start(bf16[128,1024]{1,0:T(8,128)(2,1)} %param.12), channel_id=1, source_target_pairs={{0,64},{64,128},{128,192},{192,0},{1,65},{65,129},{129,193},{193,1... | collective-permute-start | bytes 786440 | tf_op jit(solution)/shard_map/ppermute | solution.py:27
  7.6 33.6 %collective-permute-start.4 = (bf16[128,1024]{1,0:T(8,128)(2,1)}, bf16[128,1024]{1,0:T(8,128)(2,1)}, u32[]{:S(2)}, u32[]{:S(2)}) collective-permute-start(bf16[128,1024]{1,0:T(8,128)(2,1)} %param.12), channel_id=1, source_target_pairs={{0,192},{64,0},{128,64},{192,128},{1,193},{65,1},{129,65},{193,129... | collective-permute-start | bytes 786440 | tf_op jit(solution)/shard_map/ppermute | solution.py:27
  13.0 52.5 %all-to-all-start = ((bf16[64,16,256]{2,1,0:T(8,128)(2,1)}), bf16[64,16,256]{2,1,0:T(8,128)(2,1)S(1)}, u32[]{:S(2)}, u32[]{:S(2)}) async-start(bf16[64,16,256]{2,1,0:T(8,128)(2,1)} %maximum_maximum_fusion), calls=%async_computation | async-start | bytes 1048576 | tf_op jit(solution)/shard_map/all_to_all | solution.py:139
  25.4 40.1 %copy-start.40 = (s32[128]{0:T(128)}, s32[128]{0:T(128)S(1)}, u32[]{:S(2)}) copy-start(s32[128]{0:T(128)S(1)} %get-tuple-element.66) | copy-start | bytes 1540
  25.4 40.6 %copy-start.37 = (s32[128]{0:T(128)}, s32[128]{0:T(128)S(1)}, u32[]{:S(2)}) copy-start(s32[128]{0:T(128)S(1)} %get-tuple-element.65) | copy-start | bytes 1540
  25.4 40.9 %copy-start.39 = (s32[128]{0:T(128)}, s32[128]{0:T(128)S(1)}, u32[]{:S(2)}) copy-start(s32[128]{0:T(128)S(1)} %get-tuple-element.67) | copy-start | bytes 1540
  28.0 12.5 %collective-permute-start.3 = (bf16[128,1024]{1,0:T(8,128)(2,1)S(1)}, bf16[128,1024]{1,0:T(8,128)(2,1)S(1)}, u32[]{:S(2)}, u32[]{:S(2)}) collective-permute-start(bf16[128,1024]{1,0:T(8,128)(2,1)S(1)} %copy-done.18), channel_id=1, source_target_pairs={{0,128},{64,192},{128,0},{192,64},{1,129},{65,193},{129,1},{193,65... | collective-permute-start | bytes 786440 | tf_op jit(solution)/shard_map/ppermute | solution.py:27
  33.8 26.8 %collective-permute-start.10 = (bf16[256,1024]{1,0:T(8,128)(2,1)S(1)}, bf16[256,1024]{1,0:T(8,128)(2,1)S(1)}, u32[]{:S(2)}, u32[]{:S(2)}) collective-permute-start(bf16[256,1024]{1,0:T(8,128)(2,1)S(1)} %bitcast.296), channel_id=1, source_target_pairs={{0,48},{16,0},{32,16},{48,32},{1,49},{17,1},{33,17},{49,33},{2,50}... | collective-permute-start | bytes 1572872 | tf_op jit(solution)/shard_map/ppermute | solution.py:27
  36.7 23.9 %collective-permute-start.9 = (bf16[256,1024]{1,0:T(8,128)(2,1)S(1)}, bf16[256,1024]{1,0:T(8,128)(2,1)S(1)}, u32[]{:S(2)}, u32[]{:S(2)}) collective-permute-start(bf16[256,1024]{1,0:T(8,128)(2,1)S(1)} %bitcast.297), channel_id=1, source_target_pairs={{0,32},{16,48},{32,0},{48,16},{1,33},{17,49},{33,1},{49,17},{2,34}... | collective-permute-start | bytes 1572872 | tf_op jit(solution)/shard_map/ppermute | solution.py:27
  37.8 22.8 %collective-permute-start.8 = (bf16[256,1024]{1,0:T(8,128)(2,1)S(1)}, bf16[256,1024]{1,0:T(8,128)(2,1)S(1)}, u32[]{:S(2)}, u32[]{:S(2)}) collective-permute-start(bf16[256,1024]{1,0:T(8,128)(2,1)S(1)} %bitcast.299), channel_id=1, source_target_pairs={{0,16},{16,32},{32,48},{48,0},{1,17},{17,33},{33,49},{49,1},{2,18}... | collective-permute-start | bytes 1572872 | tf_op jit(solution)/shard_map/ppermute | solution.py:27
  65.5 2.1 collective-permute-start.11
  66.3 34.4 %copy-start.15 = (bf16[128,1024]{1,0:T(8,128)(2,1)S(1)}, bf16[128,1024]{1,0:T(8,128)(2,1)}, u32[]{:S(2)}) copy-start(bf16[128,1024]{1,0:T(8,128)(2,1)} %param.14) | copy-start | bytes 786436
  69.0 40.8 %copy-start.35 = (f32[1024]{0:T(1024)S(1)}, f32[1024]{0:T(1024)}, u32[]{:S(2)}) copy-start(f32[1024]{0:T(1024)} %param.15) | copy-start | bytes 12292
  69.0 12.0 %collective-permute-start.12 = (bf16[128,1024]{1,0:T(8,128)(2,1)S(1)}, bf16[128,1024]{1,0:T(8,128)(2,1)S(1)}, u32[]{:S(2)}, u32[]{:S(2)}) collective-permute-start(bf16[128,1024]{1,0:T(8,128)(2,1)S(1)} %get-tuple-element.51), channel_id=1, source_target_pairs={{0,0},{1,64},{2,128},{3,192},{64,1},{65,65},{66,129},{67,193},{128... | collective-permute-start | bytes 786440 | tf_op jit(solution)/shard_map/ppermute | solution.py:95
  69.7 30.9 %collective-permute-start.13 = (bf16[128,1024]{1,0:T(8,128)(2,1)S(1)}, bf16[128,1024]{1,0:T(8,128)(2,1)S(1)}, u32[]{:S(2)}, u32[]{:S(2)}) collective-permute-start(bf16[128,1024]{1,0:T(8,128)(2,1)S(1)} %get-tuple-element.52), channel_id=1, source_target_pairs={{0,128},{1,192},{2,0},{3,64},{64,129},{65,193},{66,1},{67,65},{128... | collective-permute-start | bytes 786440 | tf_op jit(solution)/shard_map/ppermute | solution.py:95
  79.7 21.4 %collective-permute-start = (bf16[128,640]{1,0:T(8,128)(2,1)S(1)}, bf16[128,640]{1,0:T(8,128)(2,1)S(1)}, u32[]{:S(2)}, u32[]{:S(2)}) collective-permute-start(bf16[128,640]{1,0:T(8,128)(2,1)S(1)} %pad_maximum_fusion.6), channel_id=1, source_target_pairs={{0,1},{1,0},{2,3},{3,2},{4,5},{5,4},{6,7},{7,6},{8,9},{9,8},{10,11... | collective-permute-start | bytes 491528 | tf_op jit(solution)/shard_map/ppermute | solution.py:50
  100.9 1.2 collective-permute-start.14
  102.1 7.6 %collective-permute-start.15 = (f32[2,128]{1,0:T(2,128)S(1)}, f32[2,128]{1,0:T(2,128)S(1)}, u32[]{:S(2)}, u32[]{:S(2)}) collective-permute-start(f32[2,128]{1,0:T(2,128)S(1)} %fusion.110), channel_id=1, source_target_pairs={{0,2},{2,0},{1,3},{3,1},{4,6},{6,4},{5,7},{7,5},{8,10},{10,8},{9,1... | collective-permute-start | bytes 3080 | tf_op jit(solution)/shard_map/ppermute | solution.py:57
  104.7 13.5 %collective-permute-start.1 = (bf16[2,128,640]{2,1,0:T(8,128)(2,1)S(1)}, bf16[2,128,640]{2,1,0:T(8,128)(2,1)S(1)}, u32[]{:S(2)}, u32[]{:S(2)}) collective-permute-start(bf16[2,128,640]{2,1,0:T(8,128)(2,1)S(1)} %pad_maximum_fusion.5), channel_id=1, source_target_pairs={{0,2},{2,0},{1,3},{3,1},{4,6},{6,4},{5,7},{7,5},{8,10},{10,8},{9,1... | collective-permute-start | bytes 983048 | tf_op jit(solution)/shard_map/ppermute | solution.py:50
  140.9 4.9 %collective-permute-start.27 = (f32[9,128]{1,0:T(8,128)S(1)}, f32[9,128]{1,0:T(8,128)S(1)}, u32[]{:S(2)}, u32[]{:S(2)}) collective-permute-start(f32[9,128]{1,0:T(8,128)S(1)} %stack.78), channel_id=1, source_target_pairs={{0,1},{1,0},{2,3},{3,2},{4,5},{5,4},{6,7},{7,6},{8,9},{9,8},{10,11... | collective-permute-start | bytes 13832 | tf_op jit(solution)/shard_map/ppermute | solution.py:57
  142.2 30.2 %collective-permute-start.25 = (bf16[2,128,640]{2,1,0:T(8,128)(2,1)S(1)}, bf16[2,128,640]{2,1,0:T(8,128)(2,1)S(1)}, u32[]{:S(2)}, u32[]{:S(2)}) collective-permute-start(bf16[2,128,640]{2,1,0:T(8,128)(2,1)S(1)} %fusion.30), channel_id=1, source_target_pairs={{0,1},{1,0},{2,3},{3,2},{4,5},{5,4},{6,7},{7,6},{8,9},{9,8},{10,11... | collective-permute-start | bytes 983048 | tf_op jit(solution)/shard_map/ppermute | solution.py:191
  145.8 26.6 %collective-permute-start.28 = (f32[9,128]{1,0:T(8,128)S(1)}, f32[9,128]{1,0:T(8,128)S(1)}, u32[]{:S(2)}, u32[]{:S(2)}) collective-permute-start(f32[9,128]{1,0:T(8,128)S(1)} %add.420), channel_id=1, source_target_pairs={{0,2},{2,0},{1,3},{3,1},{4,6},{6,4},{5,7},{7,5},{8,10},{10,8},{9,1... | collective-permute-start | bytes 13832 | tf_op jit(solution)/shard_map/ppermute | solution.py:57
  151.3 32.1 %copy-start.13 = (f32[4,128,256]{2,1,0:T(8,128)S(1)}, f32[4,128,256]{2,1,0:T(8,128)}, u32[]{:S(2)}) copy-start(f32[4,128,256]{2,1,0:T(8,128)} %get-tuple-element.42) | copy-start | bytes 1572868
  151.3 32.1 %copy-start.14 = (f32[4,128,256]{2,1,0:T(8,128)S(1)}, f32[4,128,256]{2,1,0:T(8,128)}, u32[]{:S(2)}) copy-start(f32[4,128,256]{2,1,0:T(8,128)} %get-tuple-element.41) | copy-start | bytes 1572868
  151.3 73.4 %collective-permute-start.16 = (bf16[544,1024]{1,0:T(8,128)(2,1)}, bf16[544,1024]{1,0:T(8,128)(2,1)}, u32[]{:S(2)}, u32[]{:S(2)}) collective-permute-start(bf16[544,1024]{1,0:T(8,128)(2,1)} %get-tuple-element.35), channel_id=1, source_target_pairs={{0,64},{64,128},{128,192},{192,0},{1,65},{65,129},{129,193},{193,1... | collective-permute-start | bytes 3342344 | tf_op jit(solution)/shard_map/ppermute | solution.py:27
  152.9 72.7 %collective-permute-start.18 = (bf16[544,1024]{1,0:T(8,128)(2,1)}, bf16[544,1024]{1,0:T(8,128)(2,1)}, u32[]{:S(2)}, u32[]{:S(2)}) collective-permute-start(bf16[544,1024]{1,0:T(8,128)(2,1)} %get-tuple-element.36), channel_id=1, source_target_pairs={{0,192},{64,0},{128,64},{192,128},{1,193},{65,1},{129,65},{193,129... | collective-permute-start | bytes 3342344 | tf_op jit(solution)/shard_map/ppermute | solution.py:27
  163.1 62.4 %collective-permute-start.17 = (bf16[544,1024]{1,0:T(8,128)(2,1)}, bf16[544,1024]{1,0:T(8,128)(2,1)}, u32[]{:S(2)}, u32[]{:S(2)}) collective-permute-start(bf16[544,1024]{1,0:T(8,128)(2,1)} %get-tuple-element.37), channel_id=1, source_target_pairs={{0,128},{64,192},{128,0},{192,64},{1,129},{65,193},{129,1},{193,65... | collective-permute-start | bytes 3342344 | tf_op jit(solution)/shard_map/ppermute | solution.py:27
  172.5 9.3 %collective-permute-start.26 = (bf16[128,640]{1,0:T(8,128)(2,1)S(1)}, bf16[128,640]{1,0:T(8,128)(2,1)S(1)}, u32[]{:S(2)}, u32[]{:S(2)}) collective-permute-start(bf16[128,640]{1,0:T(8,128)(2,1)S(1)} %fusion.46), channel_id=1, source_target_pairs={{0,2},{2,0},{1,3},{3,1},{4,6},{6,4},{5,7},{7,5},{8,10},{10,8},{9,1... | collective-permute-start | bytes 491528 | tf_op jit(solution)/shard_map/ppermute | solution.py:192
  185.9 24.9 %collective-permute-start.30 = (f32[8,128]{1,0:T(8,128)S(1)}, f32[8,128]{1,0:T(8,128)S(1)}, u32[]{:S(2)}, u32[]{:S(2)}) collective-permute-start(f32[8,128]{1,0:T(8,128)S(1)} %bitcast.310), channel_id=1, source_target_pairs={{0,128},{64,192},{128,0},{192,64},{1,129},{65,193},{129,1},{193,65... | collective-permute-start | bytes 12296 | tf_op jit(solution)/shard_map/ppermute | solution.py:27
  186.1 35.7 %collective-permute-start.31 = (f32[8,128]{1,0:T(8,128)S(1)}, f32[8,128]{1,0:T(8,128)S(1)}, u32[]{:S(2)}, u32[]{:S(2)}) collective-permute-start(f32[8,128]{1,0:T(8,128)S(1)} %bitcast.311), channel_id=1, source_target_pairs={{0,192},{64,0},{128,64},{192,128},{1,193},{65,1},{129,65},{193,129... | collective-permute-start | bytes 12296 | tf_op jit(solution)/shard_map/ppermute | solution.py:27
  210.7 12.6 %collective-permute-start.29 = (f32[8,128]{1,0:T(8,128)S(1)}, f32[8,128]{1,0:T(8,128)S(1)}, u32[]{:S(2)}, u32[]{:S(2)}) collective-permute-start(f32[8,128]{1,0:T(8,128)S(1)} %bitcast.312), channel_id=1, source_target_pairs={{0,64},{64,128},{128,192},{192,0},{1,65},{65,129},{129,193},{193,1... | collective-permute-start | bytes 12296 | tf_op jit(solution)/shard_map/ppermute | solution.py:27
  223.3 11.4 %collective-permute-start.34 = (f32[8,128]{1,0:T(8,128)S(1)}, f32[8,128]{1,0:T(8,128)S(1)}, u32[]{:S(2)}, u32[]{:S(2)}) collective-permute-start(f32[8,128]{1,0:T(8,128)S(1)} %add_add_fusion.2), channel_id=1, source_target_pairs={{0,48},{16,0},{32,16},{48,32},{1,49},{17,1},{33,17},{49,33},{2,50}... | collective-permute-start | bytes 12296 | tf_op jit(solution)/shard_map/ppermute | solution.py:27
  223.9 21.2 %collective-permute-start.33 = (f32[8,128]{1,0:T(8,128)S(1)}, f32[8,128]{1,0:T(8,128)S(1)}, u32[]{:S(2)}, u32[]{:S(2)}) collective-permute-start(f32[8,128]{1,0:T(8,128)S(1)} %add_add_fusion.2), channel_id=1, source_target_pairs={{0,32},{16,48},{32,0},{48,16},{1,33},{17,49},{33,1},{49,17},{2,34}... | collective-permute-start | bytes 12296 | tf_op jit(solution)/shard_map/ppermute | solution.py:27
  224.7 20.4 %collective-permute-start.32 = (f32[8,128]{1,0:T(8,128)S(1)}, f32[8,128]{1,0:T(8,128)S(1)}, u32[]{:S(2)}, u32[]{:S(2)}) collective-permute-start(f32[8,128]{1,0:T(8,128)S(1)} %add_add_fusion.2), channel_id=1, source_target_pairs={{0,16},{16,32},{32,48},{48,0},{1,17},{17,33},{33,49},{49,1},{2,18}... | collective-permute-start | bytes 12296 | tf_op jit(solution)/shard_map/ppermute | solution.py:27
  231.4 16.9 %collective-permute-start.19 = (bf16[136,1024]{1,0:T(8,128)(2,1)}, bf16[136,1024]{1,0:T(8,128)(2,1)}, u32[]{:S(2)}, u32[]{:S(2)}) collective-permute-start(bf16[136,1024]{1,0:T(8,128)(2,1)} %get-tuple-element.38), channel_id=1, source_target_pairs={{0,16},{16,32},{32,48},{48,0},{1,17},{17,33},{33,49},{49,1},{2,18}... | collective-permute-start | bytes 835592 | tf_op jit(solution)/shard_map/ppermute | solution.py:27
  233.3 17.4 %collective-permute-start.21 = (bf16[136,1024]{1,0:T(8,128)(2,1)S(1)}, bf16[136,1024]{1,0:T(8,128)(2,1)}, u32[]{:S(2)}, u32[]{:S(2)}) collective-permute-start(bf16[136,1024]{1,0:T(8,128)(2,1)S(1)} %get-tuple-element.39), channel_id=1, source_target_pairs={{0,48},{16,0},{32,16},{48,32},{1,49},{17,1},{33,17},{49,33},{2,50}... | collective-permute-start | bytes 835592 | tf_op jit(solution)/shard_map/ppermute | solution.py:27
  234.7 16.1 %collective-permute-start.20 = (bf16[136,1024]{1,0:T(8,128)(2,1)S(1)}, bf16[136,1024]{1,0:T(8,128)(2,1)}, u32[]{:S(2)}, u32[]{:S(2)}) collective-permute-start(bf16[136,1024]{1,0:T(8,128)(2,1)S(1)} %get-tuple-element.40), channel_id=1, source_target_pairs={{0,32},{16,48},{32,0},{48,16},{1,33},{17,49},{33,1},{49,17},{2,34}... | collective-permute-start | bytes 835592 | tf_op jit(solution)/shard_map/ppermute | solution.py:27
  238.7 27.6 %all-to-all-start.1 = ((bf16[64,16,256]{2,1,0:T(8,128)(2,1)}), bf16[64,16,256]{2,1,0:T(8,128)(2,1)S(1)}, u32[]{:S(2)}, u32[]{:S(2)}) async-start(bf16[64,16,256]{2,1,0:T(8,128)(2,1)} %bitcast.106), calls=%async_computation.1 | async-start | bytes 1048576 | tf_op jit(solution)/shard_map/all_to_all | solution.py:211
  245.2 13.9 %collective-permute-start.37 = (f32[8,128]{1,0:T(8,128)S(1)}, f32[8,128]{1,0:T(8,128)S(1)}, u32[]{:S(2)}, u32[]{:S(2)}) collective-permute-start(f32[8,128]{1,0:T(8,128)S(1)} %add_add_fusion.1), channel_id=1, source_target_pairs={{0,12},{4,0},{8,4},{12,8},{1,13},{5,1},{9,5},{13,9},{2,14},{6,2},{... | collective-permute-start | bytes 12296 | tf_op jit(solution)/shard_map/ppermute | solution.py:27
  245.9 13.1 %collective-permute-start.36 = (f32[8,128]{1,0:T(8,128)S(1)}, f32[8,128]{1,0:T(8,128)S(1)}, u32[]{:S(2)}, u32[]{:S(2)}) collective-permute-start(f32[8,128]{1,0:T(8,128)S(1)} %add_add_fusion.1), channel_id=1, source_target_pairs={{0,8},{4,12},{8,0},{12,4},{1,9},{5,13},{9,1},{13,5},{2,10},{6,14},... | collective-permute-start | bytes 12296 | tf_op jit(solution)/shard_map/ppermute | solution.py:27
  248.4 10.6 %collective-permute-start.35 = (f32[8,128]{1,0:T(8,128)S(1)}, f32[8,128]{1,0:T(8,128)S(1)}, u32[]{:S(2)}, u32[]{:S(2)}) collective-permute-start(f32[8,128]{1,0:T(8,128)S(1)} %add_add_fusion.1), channel_id=1, source_target_pairs={{0,4},{4,8},{8,12},{12,0},{1,5},{5,9},{9,13},{13,1},{2,6},{6,10},{... | collective-permute-start | bytes 12296 | tf_op jit(solution)/shard_map/ppermute | solution.py:27
  252.4 9.0 %collective-permute-start.22 = (bf16[34,1024]{1,0:T(8,128)(2,1)S(1)}, bf16[34,1024]{1,0:T(8,128)(2,1)S(1)}, u32[]{:S(2)}, u32[]{:S(2)}) collective-permute-start(bf16[34,1024]{1,0:T(8,128)(2,1)S(1)} %get-tuple-element.44), channel_id=1, source_target_pairs={{0,4},{4,8},{8,12},{12,0},{1,5},{5,9},{9,13},{13,1},{2,6},{6,10},{... | collective-permute-start | bytes 208904 | tf_op jit(solution)/shard_map/ppermute | solution.py:27
  252.5 8.9 %collective-permute-start.24 = (bf16[34,1024]{1,0:T(8,128)(2,1)S(1)}, bf16[34,1024]{1,0:T(8,128)(2,1)S(1)}, u32[]{:S(2)}, u32[]{:S(2)}) collective-permute-start(bf16[34,1024]{1,0:T(8,128)(2,1)S(1)} %get-tuple-element.45), channel_id=1, source_target_pairs={{0,12},{4,0},{8,4},{12,8},{1,13},{5,1},{9,5},{13,9},{2,14},{6,2},{... | collective-permute-start | bytes 208904 | tf_op jit(solution)/shard_map/ppermute | solution.py:27
  259.0 5.3 %collective-permute-start.23 = (bf16[34,1024]{1,0:T(8,128)(2,1)S(1)}, bf16[34,1024]{1,0:T(8,128)(2,1)S(1)}, u32[]{:S(2)}, u32[]{:S(2)}) collective-permute-start(bf16[34,1024]{1,0:T(8,128)(2,1)S(1)} %get-tuple-element.46), channel_id=1, source_target_pairs={{0,8},{4,12},{8,0},{12,4},{1,9},{5,13},{9,1},{13,5},{2,10},{6,14},... | collective-permute-start | bytes 208904 | tf_op jit(solution)/shard_map/ppermute | solution.py:27
  (48 other events, 210.1 us)

commit v2 on v1

v2 whole, which is shorter than its diff:
```python
import functools
import math

import jax
import jax.numpy as jnp
from jax import lax
from jax.experimental import pallas as pl
from jax.experimental.pallas import tpu as pltpu
from jax.sharding import Mesh
from jax.sharding import PartitionSpec as P

D = 4096
TOKENS = 8192
ROWS = 128
SHARDS = 64
CAP = 14
SLOT = 16
GROUPS = (12, 20, 32)
WIDTHS = (384, 768, 1024)
QUARTERS = (96, 192, 256)
OFFSETS = (512, 256, 0)
BLOCK = 640
SPARE = 448
ROOT = math.sqrt(TOKENS)
F32 = jnp.float32
BF16 = jnp.bfloat16
SWAP = [(0, 1), (1, 0)]
VMEM_LIMIT = 48 * 1024 * 1024


def call(body, outs, *args, scratch=(), flops=0, moved=0):
    specs = [pl.BlockSpec(memory_space=pltpu.SMEM)]
    specs += [pl.BlockSpec(memory_space=pltpu.VMEM)] * (len(args) - 1)
    return pl.pallas_call(
        body,
        out_shape=[jax.ShapeDtypeStruct(shape, dtype) for shape, dtype in outs],
        in_specs=specs,
        out_specs=[pl.BlockSpec(memory_space=pltpu.VMEM)] * len(outs),
        scratch_shapes=[pltpu.VMEM(shape, dtype) for shape, dtype in scratch],
        compiler_params=pltpu.CompilerParams(vmem_limit_bytes=VMEM_LIMIT),
        cost_estimate=pl.CostEstimate(flops=flops, bytes_accessed=moved, transcendentals=0),
    )(*args)


def dot(a, b):
    return jnp.dot(a, b, preferred_element_type=F32)


def dot_t(a, b):
    return lax.dot_general(a, b, (((1,), (1,)), ((), ())), preferred_element_type=F32)


def shifted(value, axis, step):
    return lax.ppermute(value, axis, [(i, (i + step) % 4) for i in range(4)])


def swapped(value, axis):
    return lax.ppermute(value, axis, SWAP)


def split_sum(value):
    high = value.astype(BF16)
    return high, (value - high.astype(F32)).astype(BF16)


Y, X, ZL, ZH, C = range(5)


def teacher_kernel(pos, a0, a1, a2, a3, w0, w1, w2, w3, mine, other, rows, weights):
    y, x, zl, c = pos[Y], pos[X], pos[ZL], pos[C]
    for step, part in enumerate((a0, a1, a2, a3)):
        rows[lax.rem(y + 4 - step, 4)] = part[...]
    for step, part in enumerate((w0, w1, w2, w3)):
        first = lax.rem(x + 4 - step, 4) * 256
        for turn in range(4):
            start = pl.multiple_of(first + lax.rem(zl + 4 - turn, 4) * 64, 64)
            weights[pl.ds(start, 64), :] = part[turn * 64 : turn * 64 + 64, :]
    for half in range(2):
        mine[half] = dot_t(rows[c + 2 * half], weights[...])
        other[half] = dot_t(rows[1 - c + 2 * half], weights[...]).astype(BF16)


def pair_kernel(pos, mine, got, first, second):
    zh = pos[ZH]
    first[...] = (mine[zh] + got[zh].astype(F32)).astype(BF16)
    second[...] = (mine[1 - zh] + got[1 - zh].astype(F32)).astype(BF16)


def hidden_kernel(pos, first, second, residual, hidden, sums):
    value = residual[...].astype(F32) + (first[...].astype(F32) + second[...].astype(F32))
    hidden[...] = value
    lane = lax.broadcasted_iota(jnp.int32, (ROWS, 128), 1)
    total = jnp.sum(value, axis=1, keepdims=True)
    square = jnp.sum(value * value, axis=1, keepdims=True)
    both = jnp.where(lane == 0, total, jnp.where(lane == 1, square, 0.0))
    sums[...] = jnp.transpose(both)[0:8]


def place_kernel(pos, shard, shard_t, got, block, place_t, weights):
    token = lax.broadcasted_iota(jnp.int32, (ROWS, ROWS), 0)
    token_t = lax.broadcasted_iota(jnp.int32, (ROWS, ROWS), 1)
    slot = lax.broadcasted_iota(jnp.int32, (ROWS, SHARDS * SLOT), 1)
    spare = lax.broadcasted_iota(jnp.int32, (8, SHARDS * SLOT), 1)
    lane = lax.broadcasted_iota(jnp.int32, (ROWS, 256), 1)
    counts = dot((lax.rem(spare, SLOT) == CAP).astype(F32).astype(BF16), got[...])[0:1]
    block[...] = jnp.zeros_like(block)
    place_t[...] = jnp.zeros_like(place_t)
    for i in range(3):
        column = shard[:, i : i + 1]
        row = shard_t[i : i + 1, :]
        same = column == row
        rank = jnp.sum(jnp.where(same & (token_t < token), 1, 0), axis=1, keepdims=True)
        rank_t = jnp.sum(jnp.where(same & (token < token_t), 1, 0), axis=0, keepdims=True)
        place_t[i : i + 1, :] = row * SLOT + rank_t
        select = (slot == column * SLOT + rank).astype(F32).astype(BF16)
        value = dot(select, got[...]).astype(BF16)
        block[:, OFFSETS[i] : OFFSETS[i] + QUARTERS[i]] = value[:, : QUARTERS[i]]
        owned = jnp.sum(jnp.where(lane == column + 64 * i, counts, 0.0), axis=1, keepdims=True)
        weights[:, 128 * i : 128 * i + 128] = jnp.broadcast_to(
            TOKENS / (GROUPS[i] * owned), (ROWS, 128)
        )


def student_kernel(
    pos, own, own_c, own_z, own_zc, gain_s, gain_b, gain_l, head_s, head_b, head_l,
    xhat, scales, lines_l, lines_x, outs, blocks, lines_s,
):
    zh, c = pos[ZH], pos[C]
    blocks[2 * zh + c] = own[...]
    blocks[2 * zh + 1 - c] = own_c[...]
    blocks[2 * (1 - zh) + c] = own_z[...]
    blocks[2 * (1 - zh) + 1 - c] = own_zc[...]
    xhat[...] = jnp.zeros_like(xhat)
    for i, (gain, head) in enumerate(((gain_s, head_s), (gain_b, head_b), (gain_l, head_l))):
        wide, first = QUARTERS[i], OFFSETS[i]
        parts = [blocks[b, :, first : first + wide].astype(F32) for b in range(4)]
        total = sum(jnp.sum(p, axis=1, keepdims=True) for p in parts)
        square = sum(jnp.sum(p * p, axis=1, keepdims=True) for p in parts)
        center = total / WIDTHS[i]
        scale = lax.rsqrt(square / WIDTHS[i] - center * center + 1e-06)
        scales[:, 128 * i : 128 * i + 128] = jnp.broadcast_to(scale, (ROWS, 128))
        out = jnp.zeros((ROWS, 1024), F32)
        for b in range(4):
            value = (parts[b] - center) * scale
            xhat[b, :, first : first + wide] = value
            normed = value * gain[:, b * wide : b * wide + wide]
            out = out + dot(normed.astype(BF16), head[b * wide : b * wide + wide, :])
            lines = jnp.transpose(normed)
            if i == 2:
                lines_l[b] = lines.astype(BF16)
            elif i == 1:
                for x in range(4):
                    lines_x[x, b * 48 : b * 48 + 48, :] = lines[x * 48 : x * 48 + 48].astype(BF16)
            else:
                for x in range(4):
                    lines_s[x, b * 24 : b * 24 + 24, :] = lines[x * 24 : x * 24 + 24]
        outs[i] = out
    lines_x[:, 192:288, :] = lines_s[...].astype(BF16)


def error_kernel(
    pos, hidden, sums, teacher_gain, outs, weights, lines_l, lines_x, xhat,
    gain_s, gain_b, gain_l, head_s, head_b, head_l,
    l0, l1, l2, l3, x0, x1, x2, x3, mine, other, backs, extra,
):
    y, x, c = pos[Y], pos[X], pos[C]
    stats = jnp.transpose(jnp.concatenate([sums[...], jnp.zeros((120, 128), F32)], axis=0))
    center = stats[:, 0:1] / D
    spread = stats[:, 1:2] / D - center * center
    target = (hidden[...] - center) * lax.rsqrt(spread + 1e-06) * teacher_gain[...]
    target = target.astype(BF16).astype(F32)
    lane = lax.broadcasted_iota(jnp.int32, (ROWS, 64), 1)
    moments = jnp.zeros((ROWS, 64), F32)
    extra[...] = jnp.zeros_like(extra)
    errors = []
    for i, (gain, head) in enumerate(((gain_s, head_s), (gain_b, head_b), (gain_l, head_l))):
        wide, first = QUARTERS[i], OFFSETS[i]
        weight = weights[:, 128 * i : 128 * i + 1]
        diff = outs[i] - target
        error = (weight * diff).astype(BF16)
        errors.append(error)
        loss = jnp.sum(weight * jnp.sum(diff * diff, axis=1, keepdims=True), axis=0, keepdims=True)
        extra[0:1, BLOCK + 128 * i : BLOCK + 128 * i + 128] = jnp.broadcast_to(loss, (1, 128))
        one = jnp.zeros((ROWS, 1), F32)
        two = jnp.zeros((ROWS, 1), F32)
        for b in range(4):
            back = dot_t(error, head[b * wide : b * wide + wide, :])
            value = xhat[b, :, first : first + wide]
            upper = back * gain[:, b * wide : b * wide + wide]
            one = one + jnp.sum(upper, axis=1, keepdims=True)
            two = two + jnp.sum(upper * value, axis=1, keepdims=True)
            backs[b, :, first : first + wide] = back
            extra[b : b + 1, first : first + wide] = jnp.sum(back * value, axis=0, keepdims=True)
        moments = jnp.where(lane == 2 * i, one, jnp.where(lane == 2 * i + 1, two, moments))
    high, low = split_sum(moments)
    turned = jnp.concatenate([high.astype(F32)[:, :32], low.astype(F32)[:, :32]], axis=1)
    zeros = jnp.zeros((ROWS, 32), F32)
    for half in range(2):
        mine[half] = backs[2 * half + c]
        mine[half, :, SPARE : SPARE + 64] = moments
        mine[half, :, BLOCK - 32 : BLOCK] = zeros
        other[half] = backs[2 * half + 1 - c].astype(BF16)
        other[half, :, SPARE : SPARE + 64] = turned.astype(BF16)
        other[half, :, BLOCK - 32 : BLOCK] = zeros.astype(BF16)
    high, low = split_sum(extra[...])
    for step, out in enumerate((l0, l1, l2, l3)):
        out[0:256, :] = dot(lines_l[lax.rem(y + step, 4)], errors[2]).astype(BF16)
        out[256:272, :] = jnp.concatenate([high, low], axis=0)
    for step, out in enumerate((x0, x1, x2, x3)):
        index = lax.rem(x + step, 4)
        out[0:192, :] = dot(lines_x[index, 0:192, :], errors[1]).astype(BF16)
        out[192:288, :] = dot(lines_x[index, 192:288, :], errors[0]).astype(BF16)


def back_kernel(pos, mine, got, keep, send, both):
    zh = pos[ZH]
    for half in range(2):
        both[half] = mine[half] + got[half].astype(F32)
    keep[...] = both[zh]
    send[...] = both[1 - zh].astype(BF16)
    value = both[0, :, SPARE : SPARE + 64]
    moments = value[:, 0:32] + value[:, 32:64]
    high, low = split_sum(moments)
    keep[:, SPARE : SPARE + 64] = jnp.concatenate([moments, jnp.zeros((ROWS, 32), F32)], axis=1)
    send[:, SPARE : SPARE + 64] = jnp.concatenate(
        [high.astype(F32), low.astype(F32)], axis=1
    ).astype(BF16)


def rows_kernel(pos, keep, got, xhat, scales, place_t, gain_s, gain_b, gain_l, slots, gains):
    t = 2 * pos[ZH] + pos[C]
    back = keep[...] + got[...].astype(F32)
    moments = back[:, SPARE : SPARE + 32] + back[:, SPARE + 32 : SPARE + 64]
    value = xhat[t]
    for i, gain in enumerate((gain_s, gain_b, gain_l)):
        wide = QUARTERS[i]
        for b in range(4):
            gains[b : b + 1, OFFSETS[i] : OFFSETS[i] + wide] = gain[:, b * wide : b * wide + wide]
    gain_row = gains[pl.ds(t, 1), :]
    slot = lax.broadcasted_iota(jnp.int32, (SHARDS * SLOT, ROWS), 0)
    total = jnp.zeros((SHARDS * SLOT, 256), F32)
    for i in range(3):
        first, wide = OFFSETS[i], QUARTERS[i]
        hat = value[:, first : first + wide]
        upper = back[:, first : first + wide] * gain_row[:, first : first + wide]
        one = moments[:, 2 * i : 2 * i + 1] / WIDTHS[i]
        two = moments[:, 2 * i + 1 : 2 * i + 2] / WIDTHS[i]
        rows = scales[:, 128 * i : 128 * i + 1] * (upper - one - hat * two)
        if wide < 256:
            rows = jnp.concatenate([rows, jnp.zeros((ROWS, 256 - wide), F32)], axis=1)
        select = (slot == place_t[i : i + 1, :]).astype(F32).astype(BF16)
        total = total + dot(select, rows.astype(BF16))
    slots[...] = total.astype(BF16)


def large_kernel(pos, p0, p1, p2, p3, keep, m1, m2, m3, total):
    x = pos[X]
    total[...] = sum(p[...].astype(F32) for p in (p0, p1, p2, p3))
    pieces = total[256:264, :] + total[264:272, :]
    high, low = split_sum(pieces)
    keep[0:64, :] = total[pl.ds(pl.multiple_of(x * 64, 64), 64), :]
    keep[64:72, :] = pieces
    for step, out in ((1, m1), (2, m2), (3, m3)):
        start = pl.multiple_of(lax.rem(x + step, 4) * 64, 64)
        out[0:64, :] = total[pl.ds(start, 64), :].astype(BF16)
        out[64:80, :] = jnp.concatenate([high, low], axis=0)


def mixed_kernel(pos, p0, p1, p2, p3, keep, m1, m2, m3, total):
    y = pos[Y]
    total[...] = sum(p[...].astype(F32) for p in (p0, p1, p2, p3))
    keep[0:48, :] = total[pl.ds(pl.multiple_of(y * 48, 8), 48), :]
    keep[48:72, :] = total[pl.ds(pl.multiple_of(192 + y * 24, 8), 24), :]
    for step, out in ((1, m1), (2, m2), (3, m3)):
        index = lax.rem(y + step, 4)
        out[0:48, :] = total[pl.ds(pl.multiple_of(index * 48, 8), 48), :].astype(BF16)
        small = total[pl.ds(pl.multiple_of(192 + index * 24, 8), 24), :]
        out[48:80, :] = jnp.concatenate([small, jnp.zeros((8, 1024), F32)], axis=0).astype(BF16)


def third_kernel(pos, kl, l1, l2, l3, kx, x1, x2, x3, keep, m1, m2, m3, parts):
    zl = pos[ZL]
    large = kl[0:64, :] + sum(p[0:64, :].astype(F32) for p in (l1, l2, l3))
    pieces = kl[64:72, :] + sum(
        p[64:80, :].astype(F32)[0:8] + p[64:80, :].astype(F32)[8:16] for p in (l1, l2, l3)
    )
    mixed = kx[...] + sum(p[...].astype(F32)[0:72] for p in (x1, x2, x3))
    high, low = split_sum(pieces)
    for i in range(4):
        parts[i, 0:16, :] = large[16 * i : 16 * i + 16]
        parts[i, 16:28, :] = mixed[12 * i : 12 * i + 12]
        parts[i, 28:34, :] = mixed[48 + 6 * i : 48 + 6 * i + 6]
        parts[i, 34:48, :] = jnp.zeros((14, 1024), F32)
    keep[0:48, :] = parts[zl]
    keep[48:56, :] = pieces
    for step, out in ((1, m1), (2, m2), (3, m3)):
        out[0:48, :] = parts[lax.rem(zl + step, 4)].astype(BF16)
        out[48:64, :] = jnp.concatenate([high, low], axis=0)


def last_kernel(pos, keep, m1, m2, m3, small, base, large, pieces):
    total = keep[0:48, :] + sum(p[0:48, :].astype(F32) for p in (m1, m2, m3))
    total = total / ROOT
    large[...] = total[0:16]
    base[...] = total[16:28]
    small[...] = total[28:34]
    pieces[...] = keep[48:56, :] + sum(
        p[48:64, :].astype(F32)[0:8] + p[48:64, :].astype(F32)[8:16] for p in (m1, m2, m3)
    )


def per_device(
    attn_out,
    out_proj,
    residual,
    teacher_gain,
    student_feats,
    head_small,
    head_base,
    head_large,
    gain_small,
    gain_base,
    gain_large,
    row_shard,
):
    pos = jnp.stack([lax.axis_index(a).astype(jnp.int32) for a in ("y", "x", "zl", "zh", "c")])
    tensor = 2 * pos[ZH] + pos[C]
    heads = (head_small, head_base, head_large)
    gains = (gain_small[None, :], gain_base[None, :], gain_large[None, :])

    own = out_proj.T
    weights = jnp.concatenate([own] + [shifted(own, "zl", s) for s in (1, 2, 3)], axis=0)
    rows = [attn_out] + [shifted(attn_out, "y", s) for s in (1, 2, 3)]
    weights = [weights] + [shifted(weights, "x", s) for s in (1, 2, 3)]

    shard_t = jnp.pad(row_shard.T, ((0, 5), (0, 0)))
    shard_ids = jnp.arange(SHARDS, dtype=jnp.int32)
    named = (row_shard.T[:, :, None] == shard_ids[None, None, :]).astype(F32)
    own_counts = jnp.sum(named, axis=1).reshape(3 * SHARDS)
    feats = lax.dynamic_slice(student_feats, (0, tensor * 256), (SHARDS * CAP, 256))
    counts_row = jnp.pad(own_counts.astype(BF16), (0, 64))
    ride = jnp.broadcast_to(counts_row[None, None, :], (SHARDS, 2, 256))
    sent = jnp.concatenate([feats.reshape(SHARDS, CAP, 256), ride], axis=1)
    got = lax.all_to_all(sent, ("y", "x", "zl"), 0, 0, tiled=True).reshape(SHARDS * SLOT, 256)
    block, place_t, token_weights = call(
        place_kernel,
        [((ROWS, BLOCK), BF16), ((8, ROWS), jnp.int32), ((ROWS, 384), F32)],
        pos, row_shard, shard_t, got,
        flops=3 * 2 * 128 * 1024 * 256, moved=1 << 20,
    )
    block_c = swapped(block, "c")
    block_z = swapped(block, "zh")
    block_zc = swapped(block_z, "c")

    mine, other = call(
        teacher_kernel,
        [((2, ROWS, 1024), F32), ((2, ROWS, 1024), BF16)],
        pos, *rows, *weights,
        scratch=[((4, ROWS, 1024), BF16), ((1024, 1024), BF16)],
        flops=2 * 512 * 1024 * 1024, moved=5 << 20,
    )
    first, second = call(
        pair_kernel, [((ROWS, 1024), BF16)] * 2, pos, mine, swapped(other, "c"), moved=2 << 20
    )
    parts = []
    for k, value in enumerate((first, second)):
        links = []
        for py in range(4):
            for pzh in range(2):
                for pc in range(2):
                    links.append(((py * 2 + pzh) * 2 + pc, (pc + 2 * ((pzh + k) % 2)) * 4 + py))
        parts.append(lax.ppermute(value, ("y", "zh", "c"), links))

    xhat, scales, lines_l, lines_x, outs = call(
        student_kernel,
        [
            ((4, ROWS, BLOCK), F32),
            ((ROWS, 384), F32),
            ((4, 256, ROWS), BF16),
            ((4, 288, ROWS), BF16),
            ((3, ROWS, 1024), F32),
        ],
        pos, block, block_c, block_z, block_zc, *gains, *heads,
        scratch=[((4, ROWS, BLOCK), BF16), ((4, 96, ROWS), F32)],
        flops=2 * 128 * 2176 * 1024, moved=9 << 20,
    )
    parts, outs = lax.optimization_barrier((parts, outs))

    hidden, sums = call(
        hidden_kernel, [((ROWS, 1024), F32), ((8, ROWS), F32)], pos, *parts, residual, moved=1 << 20
    )
    sums = sums + swapped(sums, "c")
    sums = sums + swapped(sums, "zh")

    outputs = call(
        error_kernel,
        [((272, 1024), BF16)] * 4
        + [((288, 1024), BF16)] * 4
        + [((2, ROWS, BLOCK), F32), ((2, ROWS, BLOCK), BF16)],
        pos, hidden, sums, teacher_gain[None, :], outs, token_weights, lines_l, lines_x, xhat,
        *gains, *heads,
        scratch=[((4, ROWS, BLOCK), F32), ((8, 1024), F32)],
        flops=4 * 128 * 2176 * 1024, moved=15 << 20,
    )
    large, mixed, (mine, other) = outputs[0:4], outputs[4:8], outputs[8:10]

    keep, send = call(
        back_kernel,
        [((ROWS, BLOCK), F32), ((ROWS, BLOCK), BF16)],
        pos, mine, swapped(other, "c"),
        scratch=[((2, ROWS, BLOCK), F32)], moved=2 << 20,
    )
    (slots,) = call(
        rows_kernel,
        [((SHARDS * SLOT, 256), BF16)],
        pos, keep, swapped(send, "zh"), xhat, scales, place_t, *gains,
        scratch=[((8, BLOCK), F32)],
        flops=3 * 2 * 128 * 1024 * 256, moved=2 << 20,
    )
    token_gradient = lax.all_to_all(
        slots.reshape(SHARDS, SLOT, 256), ("y", "x", "zl"), 0, 0, tiled=True
    )
    token_gradient = token_gradient[:, :CAP].reshape(SHARDS * CAP, 256)

    keep_l, *sent_l = call(
        large_kernel,
        [((72, 1024), F32)] + [((80, 1024), BF16)] * 3,
        pos, large[0], *[shifted(large[s], "y", s) for s in (1, 2, 3)],
        scratch=[((272, 1024), F32)], moved=4 << 20,
    )
    keep_x, *sent_x = call(
        mixed_kernel,
        [((72, 1024), F32)] + [((80, 1024), BF16)] * 3,
        pos, mixed[0], *[shifted(mixed[s], "x", s) for s in (1, 2, 3)],
        scratch=[((288, 1024), F32)], moved=4 << 20,
    )
    keep, *sent = call(
        third_kernel,
        [((56, 1024), F32)] + [((64, 1024), BF16)] * 3,
        pos,
        keep_l, *[shifted(sent_l[s - 1], "x", s) for s in (1, 2, 3)],
        keep_x, *[shifted(sent_x[s - 1], "y", s) for s in (1, 2, 3)],
        scratch=[((4, 48, 1024), F32)], moved=2 << 20,
    )
    grad_small, grad_base, grad_large, pieces = call(
        last_kernel,
        [((6, 1024), F32), ((12, 1024), F32), ((16, 1024), F32), ((8, 1024), F32)],
        pos, keep, *[shifted(sent[s - 1], "zl", s) for s in (1, 2, 3)],
        moved=1 << 20,
    )

    pieces = pieces + swapped(pieces, "c")
    pieces = pieces + swapped(pieces, "zh")
    row = lax.dynamic_index_in_dim(pieces, tensor, 0, keepdims=False) / ROOT
    losses = jnp.stack([pieces[0, BLOCK + 128 * i] for i in range(3)]) / (2.0 * D * TOKENS)
    return (
        grad_small,
        grad_base,
        grad_large,
        row[OFFSETS[0] : OFFSETS[0] + 96],
        row[OFFSETS[1] : OFFSETS[1] + 192],
        row[OFFSETS[2] : OFFSETS[2] + 256],
        token_gradient,
        losses,
    )


def solution(mesh):
    fine = Mesh(mesh.devices.reshape(4, 4, 4, 2, 2), ("y", "x", "zl", "zh", "c"))
    dp = ("y", "x", "zl")
    tp = ("zh", "c")
    return jax.shard_map(
        per_device,
        mesh=fine,
        in_specs=(
            P(dp, tp),
            P(tp, dp),
            P(dp, tp),
            P(tp),
            P(dp, None),
            P(None, tp),
            P(None, tp),
            P(None, tp),
            P(),
            P(),
            P(),
            P(dp, None),
        ),
        out_specs=(
            P(dp, tp),
            P(dp, tp),
            P(dp, tp),
            P(tp),
            P(tp),
            P(tp),
            P(dp, tp),
            P(),
        ),
        check_vma=False,
    )
```

time: 273 us -> 211 us (0.77); the launches traced: 267 us -> 210 us
  starting transfers between devices: 106 us -> 63.9 us
  Pallas kernels: 0 us -> 28.3 us
  local copies, waits for them, and re-layouts: 36.1 us -> 10.2 us
  waiting for transfers between devices: 79.2 us -> 101 us
  other arithmetic: 26 us -> 5.32 us
  matrix products: 18.1 us -> 0 us
    pallas_call x0 -> x12, Pallas kernels: none -> 28.3 us  [call(): pl.pallas_call(body, out_shape=[jax.ShapeDtypeStruct(shape, dtype) for sh...]
    ppermute x27 -> x24, starting transfers between devices: 65.5 us -> 39.1 us  [shifted(): return lax.ppermute(value, axis, [(i, (i + step) % 4) for i in range(4)])]
    dot_general x16 -> x0, matrix products: 18.1 us -> none  [the longest x3 4.99 us: per_device(): lax.dot_general(error, heads[i], (((1,), (1,)), ((), ())), preferred_elem...]
    ppermute x11 -> x12, starting transfers between devices: 25.9 us -> 12 us  [the longest x2 6.25 us: per_device(): parts.append(lax.ppermute(value, ('y', 'zh', 'c'), links))]
    ppermute x11 -> x12, waiting for transfers between devices: 32 us -> 45.4 us  [the longest x10 25.5 us: swapped(): return lax.ppermute(value, axis, SWAP)]
    ppermute x27 -> x24, waiting for transfers between devices: 47.2 us -> 55.9 us  [shifted(): return lax.ppermute(value, axis, [(i, (i + step) % 4) for i in range(4)])]
    dynamic_update_slice x12 -> x0, local copies, waits for them, and re-layouts: 7.73 us -> none  [gather4(): lax.dynamic_update_index_in_dim(out, parts[step], (pos + 4 - step) % 4, 0)]
    reduce_sum x13 -> x1, other arithmetic: 6.45 us -> 0.82 us  [per_device(): own_counts = jnp.sum(named, axis=1).reshape(3 * SHARDS)]
  transfers between devices with their start and end apart: 40 -> 38, of which waited for: 11 -> 19; matrix products, arithmetic and copies ran while one was open for 19% -> 4% of each run, Pallas kernels for 0% -> 9%
where the time goes in v2:
time: 211 us; the launch traced here: 210 us
  waiting for transfers between devices  101 us (48%)
  starting transfers between devices  63.9 us (30%)
  Pallas kernels  28.3 us (13%)
  local copies, waits for them, and re-layouts  10.2 us (5%)
  other arithmetic  5.32 us (3%)
    ppermute x24, waiting for transfers between devices, shifted(): return lax.ppermute(value, axis, [(i, (i + step) % 4) for i in range(4)])  55.9 us
    ppermute x24, starting transfers between devices, shifted(): return lax.ppermute(value, axis, [(i, (i + step) % 4) for i in range(4)])  39.1 us
    pallas_call x12, Pallas kernels, call(): pl.pallas_call(body, out_shape=[jax.ShapeDtypeStruct(shape, dtype) for sh...  28.3 us
    ppermute x10, waiting for transfers between devices, swapped(): return lax.ppermute(value, axis, SWAP)  25.5 us
    ppermute x2, waiting for transfers between devices, per_device(): parts.append(lax.ppermute(value, ('y', 'zh', 'c'), links))  19.9 us
    all_to_all x1, starting transfers between devices, per_device(): lax.all_to_all(sent, ('y', 'x', 'zl'), 0, 0, tiled=True)  7.15 us
    ppermute x2, starting transfers between devices, per_device(): parts.append(lax.ppermute(value, ('y', 'zh', 'c'), links))  6.25 us
    ppermute x10, starting transfers between devices, swapped(): return lax.ppermute(value, axis, SWAP)  5.76 us
  transfers between devices with their start and end apart: 38, of which 19 were waited for; matrix products, arithmetic and copies ran while one was open for 4% of the time, Pallas kernels for 9%

profile of v2, /device:TPU:32, one launch (start us, length us, event | category | flops | bytes accessed | tf_op | source)
XLA Modules:
  0.0 210.1 jit_solution(1902346198928298282)
XLA Ops:
  0.6 1.9 collective-permute-start.5
  2.6 1.5 collective-permute-start.4
  4.1 2.8 %collective-permute-start.3 = (bf16[64,1024]{1,0:T(8,128)(2,1)}, bf16[64,1024]{1,0:T(8,128)(2,1)}, u32[]{:S(2)}, u32[]{:S(2)}) collective-permute-start(bf16[64,1024]{1,0:T(8,128)(2,1)} %bitcast.26), channel_id=1, source_target_pairs={{0,4},{4,8},{8,12},{12,0},{1,5},{5,9},{9,13},{13,1},{2,6},{6,10},{... | collective-permute-start | bytes 393224 | tf_op jit(solution)/shard_map/ppermute | solution.py:54
  6.9 3.2 %collective-permute-start.1 = (bf16[128,1024]{1,0:T(8,128)(2,1)}, bf16[128,1024]{1,0:T(8,128)(2,1)S(1)}, u32[]{:S(2)}, u32[]{:S(2)}) collective-permute-start(bf16[128,1024]{1,0:T(8,128)(2,1)} %a0.1), channel_id=1, source_target_pairs={{0,128},{64,192},{128,0},{192,64},{1,129},{65,193},{129,1},{193,65... | collective-permute-start | bytes 786440 | tf_op jit(solution)/shard_map/ppermute | solution.py:54
  12.3 7.1 %all-to-all-start = ((bf16[64,16,256]{2,1,0:T(8,128)(2,1)}), bf16[64,16,256]{2,1,0:T(8,128)(2,1)S(1)}, u32[]{:S(2)}, u32[]{:S(2)}) async-start(bf16[64,16,256]{2,1,0:T(8,128)(2,1)} %pad_maximum_fusion.1), calls=%async_computation | async-start | bytes 1048576 | tf_op jit(solution)/shard_map/all_to_all | solution.py:344
  20.5 2.8 %collective-permute-start.8 = (bf16[256,1024]{1,0:T(8,128)(2,1)S(1)}, bf16[256,1024]{1,0:T(8,128)(2,1)}, u32[]{:S(2)}, u32[]{:S(2)}) collective-permute-start(bf16[256,1024]{1,0:T(8,128)(2,1)S(1)} %pad_maximum_fusion.w0), channel_id=1, source_target_pairs={{0,48},{16,0},{32,16},{48,32},{1,49},{17,1},{33,17},{49,33},{2,50}... | collective-permute-start | bytes 1572872 | tf_op jit(solution)/shard_map/ppermute | solution.py:54
  25.0 1.5 collective-permute-start
  26.5 1.7 collective-permute-start.2
  28.3 7.0 %collective-permute-done.a1 = bf16[128,1024]{1,0:T(8,128)(2,1)} collective-permute-done((bf16[128,1024]{1,0:T(8,128)(2,1)S(1)}, bf16[128,1024]{1,0:T(8,128)(2,1)}, u32[]{:S(2)}, u32[]{:S(2)}) %collective-permute-start) | collective-permute-done | bytes 262176 | tf_op jit(solution)/shard_map/ppermute | solution.py:54
  35.4 3.0 %collective-permute-done.8.w3 = bf16[256,1024]{1,0:T(8,128)(2,1)} collective-permute-done((bf16[256,1024]{1,0:T(8,128)(2,1)S(1)}, bf16[256,1024]{1,0:T(8,128)(2,1)}, u32[]{:S(2)}, u32[]{:S(2)}) %collective-permute-start.8) | collective-permute-done | bytes 524320 | tf_op jit(solution)/shard_map/ppermute | solution.py:54
  38.3 3.3 %collective-permute-done.7.w2 = bf16[256,1024]{1,0:T(8,128)(2,1)} collective-permute-done((bf16[256,1024]{1,0:T(8,128)(2,1)S(1)}, bf16[256,1024]{1,0:T(8,128)(2,1)}, u32[]{:S(2)}, u32[]{:S(2)}) %collective-permute-start.7) | collective-permute-done | bytes 524320 | tf_op jit(solution)/shard_map/ppermute | solution.py:54
  41.6 9.2 %collective-permute-done.6.w1 = bf16[256,1024]{1,0:T(8,128)(2,1)} collective-permute-done((bf16[256,1024]{1,0:T(8,128)(2,1)S(1)}, bf16[256,1024]{1,0:T(8,128)(2,1)}, u32[]{:S(2)}, u32[]{:S(2)}) %collective-permute-start.6) | collective-permute-done | bytes 524320 | tf_op jit(solution)/shard_map/ppermute | solution.py:54
  50.8 5.3 %shard_map.179 = (f32[2,128,1024]{2,1,0:T(8,128)S(1)}, bf16[2,128,1024]{2,1,0:T(8,128)(2,1)}) custom-call(s32[5]{0:T(128)S(1)} %stack.26.pos, bf16[128,1024]{1,0:T(8,128)(2,1)S(1)} %copy-done.11, bf16[128,1024]{1,0:T(8,128)(2,1)} %collective-permute-done.a1, bf16[128,1024]{1,0:T(8,128)(2,1)S(1)} %collective-permute-done.1.a2, ...), custom_call_target="tpu_custom_call" | custom-call | flops 1073741824 | bytes 5242880 | tf_op jit(solution)/shard_map/pallas_call | solution.py:34
  57.5 1.3 shard_map.181
  58.8 4.9 %collective-permute-start.13 = (bf16[128,640]{1,0:T(8,128)(2,1)S(1)}, bf16[128,640]{1,0:T(8,128)(2,1)S(1)}, u32[]{:S(2)}, u32[]{:S(2)}) collective-permute-start(bf16[128,640]{1,0:T(8,128)(2,1)S(1)} %get-tuple-element.57.own), channel_id=1, source_target_pairs={{0,2},{2,0},{1,3},{3,1},{4,6},{6,4},{5,7},{7,5},{8,10},{10,8},{9,1... | collective-permute-start | bytes 491528 | tf_op jit(solution)/shard_map/ppermute | solution.py:58
  63.7 1.2 copy-done.6
  64.9 1.2 shard_map.180
  66.8 5.6 %collective-permute-start.11 = (bf16[128,1024]{1,0:T(8,128)(2,1)S(1)}, bf16[128,1024]{1,0:T(8,128)(2,1)S(1)}, u32[]{:S(2)}, u32[]{:S(2)}) collective-permute-start(bf16[128,1024]{1,0:T(8,128)(2,1)S(1)} %get-tuple-element.56), channel_id=1, source_target_pairs={{0,128},{1,192},{2,0},{3,64},{64,129},{65,193},{66,1},{67,65},{128... | collective-permute-start | bytes 786440 | tf_op jit(solution)/shard_map/ppermute | solution.py:372
  74.3 3.4 %shard_map.182 = (f32[4,128,640]{2,1,0:T(8,128)S(1)}, f32[128,384]{1,0:T(8,128)S(1)}, bf16[4,256,128]{2,1,0:T(8,128)(2,1)S(1)}, bf16[4,288,128]{2,1,0:T(8,128)(2,1)S(1)}, f32[3,128,1024]{2,1,0:T(8,128)S(1)}) custom-call(s32[5]{0:T(128)S(1)} %stack.26.pos, bf16[128,640]{1,0:T(8,128)(2,1)S(1)} %get-tuple-element.57.own, ...), custom_call_target="tpu_custom_call" | custom-call | flops 570425344 | bytes 9437184 | tf_op jit(solution)/shard_map/pallas_call | solution.py:34
  78.8 1.2 copy-done.4
  80.0 19.9 %collective-permute-done.11.second = bf16[128,1024]{1,0:T(8,128)(2,1)S(1)} collective-permute-done((bf16[128,1024]{1,0:T(8,128)(2,1)S(1)}, bf16[128,1024]{1,0:T(8,128)(2,1)S(1)}, u32[]{:S(2)}, u32[]{:S(2)}) %collective-permute-start.11) | collective-permute-done | bytes 262176 | tf_op jit(solution)/shard_map/ppermute | solution.py:372
  101.9 7.5 %collective-permute-done.16 = f32[8,128]{1,0:T(8,128)S(1)} collective-permute-done((f32[8,128]{1,0:T(8,128)S(1)}, f32[8,128]{1,0:T(8,128)S(1)}, u32[]{:S(2)}, u32[]{:S(2)}) %collective-permute-start.16) | collective-permute-done | bytes 4128 | tf_op jit(solution)/shard_map/ppermute | solution.py:58
  109.4 7.8 %shard_map.184 = (bf16[272,1024]{1,0:T(8,128)(2,1)S(1)}, bf16[272,1024]{1,0:T(8,128)(2,1)S(1)}, bf16[272,1024]{1,0:T(8,128)(2,1)S(1)}, bf16[272,1024]{1,0:T(8,12...) custom-call(s32[5]{0:T(128)S(1)} %stack.26.pos, ...), custom_call_target="tpu_custom_call" | custom-call | flops 1140850688 | bytes 15728640 | tf_op jit(solution)/shard_map/pallas_call | solution.py:34
  117.9 2.9 %collective-permute-start.19 = (bf16[272,1024]{1,0:T(8,128)(2,1)S(1)}, bf16[272,1024]{1,0:T(8,128)(2,1)S(1)}, u32[]{:S(2)}, u32[]{:S(2)}) collective-permute-start(bf16[272,1024]{1,0:T(8,128)(2,1)S(1)} %get-tuple-element.71), channel_id=1, source_target_pairs={{0,192},{64,0},{128,64},{192,128},{1,193},{65,1},{129,65},{193,129... | collective-permute-start | bytes 1671176 | tf_op jit(solution)/shard_map/ppermute | solution.py:54
  120.7 2.1 collective-permute-start.24
  122.8 21.1 %collective-permute-done.17.p1 = bf16[272,1024]{1,0:T(8,128)(2,1)S(1)} collective-permute-done((bf16[272,1024]{1,0:T(8,128)(2,1)S(1)}, bf16[272,1024]{1,0:T(8,128)(2,1)S(1)}, u32[]{:S(2)}, u32[]{:S(2)}) %collective-permute-start.17) | collective-permute-done | bytes 557088 | tf_op jit(solution)/shard_map/ppermute | solution.py:54
  146.7 1.7 shard_map.185
  148.4 1.4 collective-permute-start.20
  149.8 6.0 %collective-permute-done.35.got = bf16[128,640]{1,0:T(8,128)(2,1)S(1)} collective-permute-done((bf16[128,640]{1,0:T(8,128)(2,1)S(1)}, bf16[128,640]{1,0:T(8,128)(2,1)S(1)}, u32[]{:S(2)}, u32[]{:S(2)}) %collective-permute-start.35) | collective-permute-done | bytes 163872 | tf_op jit(solution)/shard_map/ppermute | solution.py:58
  155.9 2.1 %shard_map.190 = bf16[1024,256]{1,0:T(8,128)(2,1)} custom-call(s32[5]{0:T(128)S(1)} %stack.26.pos, f32[128,640]{1,0:T(8,128)S(1)} %get-tuple-element.94.keep, bf16[128,640]{1,0:T(8,128)(2,1)S(1)} %collective-permute-done.35.got, f32[4,128,640]{2,1,0:T(8,128)S(1)} %copy-done.2, f32[128,384]{1,0:T(8,128)S(1)} %get-tuple-element.96.scales, ...), custom_call_target="tpu_custom_call" | custom-call | flops 201326592 | bytes 2097152 | tf_op jit(solution)/shard_map/pallas_call | solution.py:34
  158.0 5.7 %all-to-all-start.1 = ((bf16[64,16,256]{2,1,0:T(8,128)(2,1)}), bf16[64,16,256]{2,1,0:T(8,128)(2,1)}, u32[]{:S(2)}, u32[]{:S(2)}) async-start(bf16[64,16,256]{2,1,0:T(8,128)(2,1)} %bitcast.13), calls=%async_computation.1 | async-start | bytes 1048576 | tf_op jit(solution)/shard_map/all_to_all | solution.py:420
  163.7 3.1 %collective-permute-start.21 = (bf16[80,1024]{1,0:T(8,128)(2,1)}, bf16[80,1024]{1,0:T(8,128)(2,1)S(1)}, u32[]{:S(2)}, u32[]{:S(2)}) collective-permute-start(bf16[80,1024]{1,0:T(8,128)(2,1)} %copy-done.13), channel_id=1, source_target_pairs={{0,32},{16,48},{32,0},{48,16},{1,33},{17,49},{33,1},{49,17},{2,34}... | collective-permute-start | bytes 491528 | tf_op jit(solution)/shard_map/ppermute | solution.py:54
  168.0 1.8 shard_map.186
  169.8 1.6 collective-permute-start.26
  171.4 2.9 %collective-permute-start.27 = (bf16[80,1024]{1,0:T(8,128)(2,1)S(1)}, bf16[80,1024]{1,0:T(8,128)(2,1)S(1)}, u32[]{:S(2)}, u32[]{:S(2)}) collective-permute-start(bf16[80,1024]{1,0:T(8,128)(2,1)S(1)} %get-tuple-element.82), channel_id=1, source_target_pairs={{0,128},{64,192},{128,0},{192,64},{1,129},{65,193},{129,1},{193,65... | collective-permute-start | bytes 491528 | tf_op jit(solution)/shard_map/ppermute | solution.py:54
  174.3 1.4 collective-permute-start.28
  175.6 2.9 %collective-permute-done.26.x1 = bf16[80,1024]{1,0:T(8,128)(2,1)S(1)} collective-permute-done((bf16[80,1024]{1,0:T(8,128)(2,1)S(1)}, bf16[80,1024]{1,0:T(8,128)(2,1)S(1)}, u32[]{:S(2)}, u32[]{:S(2)}) %collective-permute-start.26) | collective-permute-done | bytes 163872 | tf_op jit(solution)/shard_map/ppermute | solution.py:54
  178.5 1.8 collective-permute-done.27.x2
  181.1 1.4 collective-permute-start.29
  182.5 1.8 collective-permute-start.30
  185.3 4.2 %collective-permute-done.29.m1 = bf16[64,1024]{1,0:T(8,128)(2,1)S(1)} collective-permute-done((bf16[64,1024]{1,0:T(8,128)(2,1)S(1)}, bf16[64,1024]{1,0:T(8,128)(2,1)S(1)}, u32[]{:S(2)}, u32[]{:S(2)}) %collective-permute-start.29) | collective-permute-done | bytes 131104 | tf_op jit(solution)/shard_map/ppermute | solution.py:54
  189.5 1.4 collective-permute-done.30.m2
  190.9 2.1 %collective-permute-done.31.m3 = bf16[64,1024]{1,0:T(8,128)(2,1)S(1)} collective-permute-done((bf16[64,1024]{1,0:T(8,128)(2,1)S(1)}, bf16[64,1024]{1,0:T(8,128)(2,1)S(1)}, u32[]{:S(2)}, u32[]{:S(2)}) %collective-permute-start.31) | collective-permute-done | bytes 131104 | tf_op jit(solution)/shard_map/ppermute | solution.py:54
  193.0 1.2 shard_map.188
  194.2 1.2 collective-permute-done.32
  195.8 7.7 %collective-permute-done.33 = f32[8,1024]{1,0:T(8,128)S(1)} collective-permute-done((f32[8,1024]{1,0:T(8,128)S(1)}, f32[8,1024]{1,0:T(8,128)S(1)}, u32[]{:S(2)}, u32[]{:S(2)}) %collective-permute-start.33) | collective-permute-done | bytes 32800 | tf_op jit(solution)/shard_map/ppermute | solution.py:58
  205.2 2.4 %maximum_multiply_fusion = f32[3]{0:T(128)} fusion(f32[1]{0:T(128)} %bitcast.16, f32[1]{0:T(128)} %bitcast.15, f32[1]{0:T(128)} %bitcast.14), kind=kLoop, calls=%fused_computation.6 | loop fusion | flops 9 | bytes 24 | tf_op jit(solution)/shard_map/div | solution.py:455
  208.1 1.9 reshape.40
  (100 shorter events, 21.0 us)
Async XLA Ops:
  0.6 18.8 %collective-permute-start.5 = (bf16[64,1024]{1,0:T(8,128)(2,1)}, bf16[64,1024]{1,0:T(8,128)(2,1)}, u32[]{:S(2)}, u32[]{:S(2)}) collective-permute-start(bf16[64,1024]{1,0:T(8,128)(2,1)} %bitcast.24), channel_id=1, source_target_pairs={{0,12},{4,0},{8,4},{12,8},{1,13},{5,1},{9,5},{13,9},{2,14},{6,2},{... | collective-permute-start | bytes 393224 | tf_op jit(solution)/shard_map/ppermute | solution.py:54
  2.6 16.9 %collective-permute-start.4 = (bf16[64,1024]{1,0:T(8,128)(2,1)}, bf16[64,1024]{1,0:T(8,128)(2,1)}, u32[]{:S(2)}, u32[]{:S(2)}) collective-permute-start(bf16[64,1024]{1,0:T(8,128)(2,1)} %bitcast.25), channel_id=1, source_target_pairs={{0,8},{4,12},{8,0},{12,4},{1,9},{5,13},{9,1},{13,5},{2,10},{6,14},... | collective-permute-start | bytes 393224 | tf_op jit(solution)/shard_map/ppermute | solution.py:54
  4.1 15.3 %collective-permute-start.3 = (bf16[64,1024]{1,0:T(8,128)(2,1)}, bf16[64,1024]{1,0:T(8,128)(2,1)}, u32[]{:S(2)}, u32[]{:S(2)}) collective-permute-start(bf16[64,1024]{1,0:T(8,128)(2,1)} %bitcast.26), channel_id=1, source_target_pairs={{0,4},{4,8},{8,12},{12,0},{1,5},{5,9},{9,13},{13,1},{2,6},{6,10},{... | collective-permute-start | bytes 393224 | tf_op jit(solution)/shard_map/ppermute | solution.py:54
  6.9 19.6 %collective-permute-start.1 = (bf16[128,1024]{1,0:T(8,128)(2,1)}, bf16[128,1024]{1,0:T(8,128)(2,1)S(1)}, u32[]{:S(2)}, u32[]{:S(2)}) collective-permute-start(bf16[128,1024]{1,0:T(8,128)(2,1)} %a0.1), channel_id=1, source_target_pairs={{0,128},{64,192},{128,0},{192,64},{1,129},{65,193},{129,1},{193,65... | collective-permute-start | bytes 786440 | tf_op jit(solution)/shard_map/ppermute | solution.py:54
  11.2 13.8 %copy-start.11 = (bf16[128,1024]{1,0:T(8,128)(2,1)S(1)}, bf16[128,1024]{1,0:T(8,128)(2,1)}, u32[]{:S(2)}) copy-start(bf16[128,1024]{1,0:T(8,128)(2,1)} %a0.1) | copy-start | bytes 786436
  12.3 45.2 %all-to-all-start = ((bf16[64,16,256]{2,1,0:T(8,128)(2,1)}), bf16[64,16,256]{2,1,0:T(8,128)(2,1)S(1)}, u32[]{:S(2)}, u32[]{:S(2)}) async-start(bf16[64,16,256]{2,1,0:T(8,128)(2,1)} %pad_maximum_fusion.1), calls=%async_computation | async-start | bytes 1048576 | tf_op jit(solution)/shard_map/all_to_all | solution.py:344
  20.5 17.8 %collective-permute-start.8 = (bf16[256,1024]{1,0:T(8,128)(2,1)S(1)}, bf16[256,1024]{1,0:T(8,128)(2,1)}, u32[]{:S(2)}, u32[]{:S(2)}) collective-permute-start(bf16[256,1024]{1,0:T(8,128)(2,1)S(1)} %pad_maximum_fusion.w0), channel_id=1, source_target_pairs={{0,48},{16,0},{32,16},{48,32},{1,49},{17,1},{33,17},{49,33},{2,50}... | collective-permute-start | bytes 1572872 | tf_op jit(solution)/shard_map/ppermute | solution.py:54
  23.3 18.3 %collective-permute-start.7 = (bf16[256,1024]{1,0:T(8,128)(2,1)S(1)}, bf16[256,1024]{1,0:T(8,128)(2,1)}, u32[]{:S(2)}, u32[]{:S(2)}) collective-permute-start(bf16[256,1024]{1,0:T(8,128)(2,1)S(1)} %pad_maximum_fusion.w0), channel_id=1, source_target_pairs={{0,32},{16,48},{32,0},{48,16},{1,33},{17,49},{33,1},{49,17},{2,34}... | collective-permute-start | bytes 1572872 | tf_op jit(solution)/shard_map/ppermute | solution.py:54
  24.2 26.7 %collective-permute-start.6 = (bf16[256,1024]{1,0:T(8,128)(2,1)S(1)}, bf16[256,1024]{1,0:T(8,128)(2,1)}, u32[]{:S(2)}, u32[]{:S(2)}) collective-permute-start(bf16[256,1024]{1,0:T(8,128)(2,1)S(1)} %pad_maximum_fusion.w0), channel_id=1, source_target_pairs={{0,16},{16,32},{32,48},{48,0},{1,17},{17,33},{33,49},{49,1},{2,18}... | collective-permute-start | bytes 1572872 | tf_op jit(solution)/shard_map/ppermute | solution.py:54
  25.0 10.3 %collective-permute-start = (bf16[128,1024]{1,0:T(8,128)(2,1)S(1)}, bf16[128,1024]{1,0:T(8,128)(2,1)}, u32[]{:S(2)}, u32[]{:S(2)}) collective-permute-start(bf16[128,1024]{1,0:T(8,128)(2,1)S(1)} %copy-done.11), channel_id=1, source_target_pairs={{0,64},{64,128},{128,192},{192,0},{1,65},{65,129},{129,193},{193,1... | collective-permute-start | bytes 786440 | tf_op jit(solution)/shard_map/ppermute | solution.py:54
  26.5 8.8 %collective-permute-start.2 = (bf16[128,1024]{1,0:T(8,128)(2,1)S(1)}, bf16[128,1024]{1,0:T(8,128)(2,1)}, u32[]{:S(2)}, u32[]{:S(2)}) collective-permute-start(bf16[128,1024]{1,0:T(8,128)(2,1)S(1)} %copy-done.11), channel_id=1, source_target_pairs={{0,192},{64,0},{128,64},{192,128},{1,193},{65,1},{129,65},{193,129... | collective-permute-start | bytes 786440 | tf_op jit(solution)/shard_map/ppermute | solution.py:54
  28.3 29.0 %copy-start.15 = (s32[128,3]{0,1:T(4,128)S(1)}, s32[128,3]{0,1:T(4,128)}, u32[]{:S(2)}) copy-start(s32[128,3]{0,1:T(4,128)} %param.23) | copy-start | bytes 4612
  57.2 15.7 %copy-start.17 = (f32[384]{0:T(512)S(1)}, f32[384]{0:T(512)}, u32[]{:S(2)}) copy-start(f32[384]{0:T(512)} %param.20) | copy-start | bytes 4612
  57.2 15.7 %copy-start.16 = (f32[768]{0:T(1024)S(1)}, f32[768]{0:T(1024)}, u32[]{:S(2)}) copy-start(f32[768]{0:T(1024)} %param.21) | copy-start | bytes 9220
  57.2 17.1 %copy-start.3 = (bf16[384,1024]{1,0:T(8,128)(2,1)S(1)}, bf16[384,1024]{1,0:T(8,128)(2,1)}, u32[]{:S(2)}) copy-start(bf16[384,1024]{1,0:T(8,128)(2,1)} %head_s.3) | copy-start | bytes 2359300
  57.2 17.1 %copy-start.9 = (f32[1024]{0:T(1024)S(1)}, f32[1024]{0:T(1024)}, u32[]{:S(2)}) copy-start(f32[1024]{0:T(1024)} %param.22) | copy-start | bytes 12292
  57.2 6.5 %collective-permute-start.9 = (bf16[2,128,1024]{2,1,0:T(8,128)(2,1)}, bf16[2,128,1024]{2,1,0:T(8,128)(2,1)}, u32[]{:S(2)}, u32[]{:S(2)}) collective-permute-start(bf16[2,128,1024]{2,1,0:T(8,128)(2,1)} %get-tuple-element.54), channel_id=1, source_target_pairs={{0,1},{1,0},{2,3},{3,2},{4,5},{5,4},{6,7},{7,6},{8,9},{9,8},{10,11... | collective-permute-start | bytes 1572872 | tf_op jit(solution)/shard_map/ppermute | solution.py:58
  58.8 14.1 %collective-permute-start.13 = (bf16[128,640]{1,0:T(8,128)(2,1)S(1)}, bf16[128,640]{1,0:T(8,128)(2,1)S(1)}, u32[]{:S(2)}, u32[]{:S(2)}) collective-permute-start(bf16[128,640]{1,0:T(8,128)(2,1)S(1)} %get-tuple-element.57.own), channel_id=1, source_target_pairs={{0,2},{2,0},{1,3},{3,1},{4,6},{6,4},{5,7},{7,5},{8,10},{10,8},{9,1... | collective-permute-start | bytes 491528 | tf_op jit(solution)/shard_map/ppermute | solution.py:58
  66.1 13.9 %collective-permute-start.10 = (bf16[128,1024]{1,0:T(8,128)(2,1)S(1)}, bf16[128,1024]{1,0:T(8,128)(2,1)S(1)}, u32[]{:S(2)}, u32[]{:S(2)}) collective-permute-start(bf16[128,1024]{1,0:T(8,128)(2,1)S(1)} %get-tuple-element.55), channel_id=1, source_target_pairs={{0,0},{1,64},{2,128},{3,192},{64,1},{65,65},{66,129},{67,193},{128... | collective-permute-start | bytes 786440 | tf_op jit(solution)/shard_map/ppermute | solution.py:372
  66.8 33.1 %collective-permute-start.11 = (bf16[128,1024]{1,0:T(8,128)(2,1)S(1)}, bf16[128,1024]{1,0:T(8,128)(2,1)S(1)}, u32[]{:S(2)}, u32[]{:S(2)}) collective-permute-start(bf16[128,1024]{1,0:T(8,128)(2,1)S(1)} %get-tuple-element.56), channel_id=1, source_target_pairs={{0,128},{1,192},{2,0},{3,64},{64,129},{65,193},{66,1},{67,65},{128... | collective-permute-start | bytes 786440 | tf_op jit(solution)/shard_map/ppermute | solution.py:372
  72.4 1.4 collective-permute-start.12
  72.9 1.4 collective-permute-start.14
  74.3 25.6 %copy-start.8 = (bf16[128,1024]{1,0:T(8,128)(2,1)S(1)}, bf16[128,1024]{1,0:T(8,128)(2,1)}, u32[]{:S(2)}) copy-start(bf16[128,1024]{1,0:T(8,128)(2,1)} %residual.1) | copy-start | bytes 786436
  74.3 35.1 %copy-start.10 = (f32[1024]{0:T(1024)S(1)}, f32[1024]{0:T(1024)}, u32[]{:S(2)}) copy-start(f32[1024]{0:T(1024)} %param.15) | copy-start | bytes 12292
  100.6 1.2 collective-permute-start.15
  101.8 7.5 %collective-permute-start.16 = (f32[8,128]{1,0:T(8,128)S(1)}, f32[8,128]{1,0:T(8,128)S(1)}, u32[]{:S(2)}, u32[]{:S(2)}) collective-permute-start(f32[8,128]{1,0:T(8,128)S(1)} %add.28), channel_id=1, source_target_pairs={{0,2},{2,0},{1,3},{3,1},{4,6},{6,4},{5,7},{7,5},{8,10},{10,8},{9,1... | collective-permute-start | bytes 12296 | tf_op jit(solution)/shard_map/ppermute | solution.py:58
  117.1 38.8 %copy-start.2 = (f32[4,128,640]{2,1,0:T(8,128)S(1)}, f32[4,128,640]{2,1,0:T(8,128)}, u32[]{:S(2)}) copy-start(f32[4,128,640]{2,1,0:T(8,128)} %copy-done.1) | copy-start | bytes 3932164
  117.1 26.7 %collective-permute-start.17 = (bf16[272,1024]{1,0:T(8,128)(2,1)S(1)}, bf16[272,1024]{1,0:T(8,128)(2,1)S(1)}, u32[]{:S(2)}, u32[]{:S(2)}) collective-permute-start(bf16[272,1024]{1,0:T(8,128)(2,1)S(1)} %get-tuple-element.69), channel_id=1, source_target_pairs={{0,64},{64,128},{128,192},{192,0},{1,65},{65,129},{129,193},{193,1... | collective-permute-start | bytes 1671176 | tf_op jit(solution)/shard_map/ppermute | solution.py:54
  117.9 2.9 %collective-permute-start.34 = (bf16[2,128,640]{2,1,0:T(8,128)(2,1)S(1)}, bf16[2,128,640]{2,1,0:T(8,128)(2,1)S(1)}, u32[]{:S(2)}, u32[]{:S(2)}) collective-permute-start(bf16[2,128,640]{2,1,0:T(8,128)(2,1)S(1)} %get-tuple-element.93), channel_id=1, source_target_pairs={{0,1},{1,0},{2,3},{3,2},{4,5},{5,4},{6,7},{7,6},{8,9},{9,8},{10,11... | collective-permute-start | bytes 983048 | tf_op jit(solution)/shard_map/ppermute | solution.py:58
  117.9 28.5 %collective-permute-start.18 = (bf16[272,1024]{1,0:T(8,128)(2,1)S(1)}, bf16[272,1024]{1,0:T(8,128)(2,1)S(1)}, u32[]{:S(2)}, u32[]{:S(2)}) collective-permute-start(bf16[272,1024]{1,0:T(8,128)(2,1)S(1)} %get-tuple-element.70), channel_id=1, source_target_pairs={{0,128},{64,192},{128,0},{192,64},{1,129},{65,193},{129,1},{193,65... | collective-permute-start | bytes 1671176 | tf_op jit(solution)/shard_map/ppermute | solution.py:54
  117.9 28.8 %collective-permute-start.19 = (bf16[272,1024]{1,0:T(8,128)(2,1)S(1)}, bf16[272,1024]{1,0:T(8,128)(2,1)S(1)}, u32[]{:S(2)}, u32[]{:S(2)}) collective-permute-start(bf16[272,1024]{1,0:T(8,128)(2,1)S(1)} %get-tuple-element.71), channel_id=1, source_target_pairs={{0,192},{64,0},{128,64},{192,128},{1,193},{65,1},{129,65},{193,129... | collective-permute-start | bytes 1671176 | tf_op jit(solution)/shard_map/ppermute | solution.py:54
  120.7 46.1 %collective-permute-start.23 = (bf16[288,1024]{1,0:T(8,128)(2,1)}, bf16[288,1024]{1,0:T(8,128)(2,1)S(1)}, u32[]{:S(2)}, u32[]{:S(2)}) collective-permute-start(bf16[288,1024]{1,0:T(8,128)(2,1)} %get-tuple-element.77), channel_id=1, source_target_pairs={{0,16},{16,32},{32,48},{48,0},{1,17},{17,33},{33,49},{49,1},{2,18}... | collective-permute-start | bytes 1769480 | tf_op jit(solution)/shard_map/ppermute | solution.py:54
  120.7 47.2 %collective-permute-start.24 = (bf16[288,1024]{1,0:T(8,128)(2,1)}, bf16[288,1024]{1,0:T(8,128)(2,1)}, u32[]{:S(2)}, u32[]{:S(2)}) collective-permute-start(bf16[288,1024]{1,0:T(8,128)(2,1)} %get-tuple-element.78), channel_id=1, source_target_pairs={{0,32},{16,48},{32,0},{48,16},{1,33},{17,49},{33,1},{49,17},{2,34}... | collective-permute-start | bytes 1769480 | tf_op jit(solution)/shard_map/ppermute | solution.py:54
  143.8 24.1 %collective-permute-start.25 = (bf16[288,1024]{1,0:T(8,128)(2,1)}, bf16[288,1024]{1,0:T(8,128)(2,1)}, u32[]{:S(2)}, u32[]{:S(2)}) collective-permute-start(bf16[288,1024]{1,0:T(8,128)(2,1)} %get-tuple-element.79), channel_id=1, source_target_pairs={{0,48},{16,0},{32,16},{48,32},{1,49},{17,1},{33,17},{49,33},{2,50}... | collective-permute-start | bytes 1769480 | tf_op jit(solution)/shard_map/ppermute | solution.py:54
  146.4 9.5 %collective-permute-start.35 = (bf16[128,640]{1,0:T(8,128)(2,1)S(1)}, bf16[128,640]{1,0:T(8,128)(2,1)S(1)}, u32[]{:S(2)}, u32[]{:S(2)}) collective-permute-start(bf16[128,640]{1,0:T(8,128)(2,1)S(1)} %get-tuple-element.95), channel_id=1, source_target_pairs={{0,2},{2,0},{1,3},{3,1},{4,6},{6,4},{5,7},{7,5},{8,10},{10,8},{9,1... | collective-permute-start | bytes 491528 | tf_op jit(solution)/shard_map/ppermute | solution.py:58
  148.4 9.6 %copy-start.13 = (bf16[80,1024]{1,0:T(8,128)(2,1)}, bf16[80,1024]{1,0:T(8,128)(2,1)S(1)}, u32[]{:S(2)}) copy-start(bf16[80,1024]{1,0:T(8,128)(2,1)S(1)} %get-tuple-element.74) | copy-start | bytes 491524
  148.4 25.8 %collective-permute-start.20 = (bf16[80,1024]{1,0:T(8,128)(2,1)}, bf16[80,1024]{1,0:T(8,128)(2,1)S(1)}, u32[]{:S(2)}, u32[]{:S(2)}) collective-permute-start(bf16[80,1024]{1,0:T(8,128)(2,1)} %get-tuple-element.73), channel_id=1, source_target_pairs={{0,16},{16,32},{32,48},{48,0},{1,17},{17,33},{33,49},{49,1},{2,18}... | collective-permute-start | bytes 491528 | tf_op jit(solution)/shard_map/ppermute | solution.py:54
  158.0 50.1 %all-to-all-start.1 = ((bf16[64,16,256]{2,1,0:T(8,128)(2,1)}), bf16[64,16,256]{2,1,0:T(8,128)(2,1)}, u32[]{:S(2)}, u32[]{:S(2)}) async-start(bf16[64,16,256]{2,1,0:T(8,128)(2,1)} %bitcast.13), calls=%async_computation.1 | async-start | bytes 1048576 | tf_op jit(solution)/shard_map/all_to_all | solution.py:420
  163.7 11.9 %collective-permute-start.21 = (bf16[80,1024]{1,0:T(8,128)(2,1)}, bf16[80,1024]{1,0:T(8,128)(2,1)S(1)}, u32[]{:S(2)}, u32[]{:S(2)}) collective-permute-start(bf16[80,1024]{1,0:T(8,128)(2,1)} %copy-done.13), channel_id=1, source_target_pairs={{0,32},{16,48},{32,0},{48,16},{1,33},{17,49},{33,1},{49,17},{2,34}... | collective-permute-start | bytes 491528 | tf_op jit(solution)/shard_map/ppermute | solution.py:54
  166.8 8.8 %collective-permute-start.22 = (bf16[80,1024]{1,0:T(8,128)(2,1)}, bf16[80,1024]{1,0:T(8,128)(2,1)S(1)}, u32[]{:S(2)}, u32[]{:S(2)}) collective-permute-start(bf16[80,1024]{1,0:T(8,128)(2,1)} %copy-done.12), channel_id=1, source_target_pairs={{0,48},{16,0},{32,16},{48,32},{1,49},{17,1},{33,17},{49,33},{2,50}... | collective-permute-start | bytes 491528 | tf_op jit(solution)/shard_map/ppermute | solution.py:54
  169.8 8.7 %collective-permute-start.26 = (bf16[80,1024]{1,0:T(8,128)(2,1)S(1)}, bf16[80,1024]{1,0:T(8,128)(2,1)S(1)}, u32[]{:S(2)}, u32[]{:S(2)}) collective-permute-start(bf16[80,1024]{1,0:T(8,128)(2,1)S(1)} %get-tuple-element.81), channel_id=1, source_target_pairs={{0,64},{64,128},{128,192},{192,0},{1,65},{65,129},{129,193},{193,1... | collective-permute-start | bytes 491528 | tf_op jit(solution)/shard_map/ppermute | solution.py:54
  171.4 8.9 %collective-permute-start.27 = (bf16[80,1024]{1,0:T(8,128)(2,1)S(1)}, bf16[80,1024]{1,0:T(8,128)(2,1)S(1)}, u32[]{:S(2)}, u32[]{:S(2)}) collective-permute-start(bf16[80,1024]{1,0:T(8,128)(2,1)S(1)} %get-tuple-element.82), channel_id=1, source_target_pairs={{0,128},{64,192},{128,0},{192,64},{1,129},{65,193},{129,1},{193,65... | collective-permute-start | bytes 491528 | tf_op jit(solution)/shard_map/ppermute | solution.py:54
  174.3 6.0 %collective-permute-start.28 = (bf16[80,1024]{1,0:T(8,128)(2,1)S(1)}, bf16[80,1024]{1,0:T(8,128)(2,1)S(1)}, u32[]{:S(2)}, u32[]{:S(2)}) collective-permute-start(bf16[80,1024]{1,0:T(8,128)(2,1)S(1)} %get-tuple-element.83), channel_id=1, source_target_pairs={{0,192},{64,0},{128,64},{192,128},{1,193},{65,1},{129,65},{193,129... | collective-permute-start | bytes 491528 | tf_op jit(solution)/shard_map/ppermute | solution.py:54
  181.1 8.4 %collective-permute-start.29 = (bf16[64,1024]{1,0:T(8,128)(2,1)S(1)}, bf16[64,1024]{1,0:T(8,128)(2,1)S(1)}, u32[]{:S(2)}, u32[]{:S(2)}) collective-permute-start(bf16[64,1024]{1,0:T(8,128)(2,1)S(1)} %get-tuple-element.85), channel_id=1, source_target_pairs={{0,4},{4,8},{8,12},{12,0},{1,5},{5,9},{9,13},{13,1},{2,6},{6,10},{... | collective-permute-start | bytes 393224 | tf_op jit(solution)/shard_map/ppermute | solution.py:54
  182.5 8.4 %collective-permute-start.30 = (bf16[64,1024]{1,0:T(8,128)(2,1)S(1)}, bf16[64,1024]{1,0:T(8,128)(2,1)S(1)}, u32[]{:S(2)}, u32[]{:S(2)}) collective-permute-start(bf16[64,1024]{1,0:T(8,128)(2,1)S(1)} %get-tuple-element.86), channel_id=1, source_target_pairs={{0,8},{4,12},{8,0},{12,4},{1,9},{5,13},{9,1},{13,5},{2,10},{6,14},... | collective-permute-start | bytes 393224 | tf_op jit(solution)/shard_map/ppermute | solution.py:54
  184.3 8.7 %collective-permute-start.31 = (bf16[64,1024]{1,0:T(8,128)(2,1)S(1)}, bf16[64,1024]{1,0:T(8,128)(2,1)S(1)}, u32[]{:S(2)}, u32[]{:S(2)}) collective-permute-start(bf16[64,1024]{1,0:T(8,128)(2,1)S(1)} %get-tuple-element.87), channel_id=1, source_target_pairs={{0,12},{4,0},{8,4},{12,8},{1,13},{5,1},{9,5},{13,9},{2,14},{6,2},{... | collective-permute-start | bytes 393224 | tf_op jit(solution)/shard_map/ppermute | solution.py:54
  194.2 1.2 collective-permute-start.32
  195.5 8.1 %collective-permute-start.33 = (f32[8,1024]{1,0:T(8,128)S(1)}, f32[8,1024]{1,0:T(8,128)S(1)}, u32[]{:S(2)}, u32[]{:S(2)}) collective-permute-start(f32[8,1024]{1,0:T(8,128)S(1)} %add.30), channel_id=1, source_target_pairs={{0,2},{2,0},{1,3},{3,1},{4,6},{6,4},{5,7},{7,5},{8,10},{10,8},{9,1... | collective-permute-start | bytes 98312 | tf_op jit(solution)/shard_map/ppermute | solution.py:58
  (8 other events, 33.9 us)

commit v3 on v2

v3 whole, which is shorter than its diff:
```python
import functools
import math

import jax
import jax.numpy as jnp
from jax import lax
from jax.experimental import pallas as pl
from jax.experimental.pallas import tpu as pltpu
from jax.sharding import Mesh
from jax.sharding import PartitionSpec as P

D = 4096
TOKENS = 8192
ROWS = 128
SHARDS = 64
CAP = 14
SLOT = 16
GROUPS = (12, 20, 32)
WIDTHS = (384, 768, 1024)
QUARTERS = (96, 192, 256)
OFFSETS = (512, 256, 0)
BLOCK = 640
LINES = (448, 256, 0)
SPARE = 448
ROOT = math.sqrt(TOKENS)
F32 = jnp.float32
BF16 = jnp.bfloat16
SWAP = [(0, 1), (1, 0)]
MIB = 1024 * 1024


def call(body, outs, *args, scratch=(), flops=0, moved=0, room=8):
    specs = [pl.BlockSpec(memory_space=pltpu.SMEM)]
    specs += [pl.BlockSpec(memory_space=pltpu.VMEM)] * (len(args) - 1)
    return pl.pallas_call(
        body,
        out_shape=[jax.ShapeDtypeStruct(shape, dtype) for shape, dtype in outs],
        in_specs=specs,
        out_specs=[pl.BlockSpec(memory_space=pltpu.VMEM)] * len(outs),
        scratch_shapes=[pltpu.VMEM(shape, dtype) for shape, dtype in scratch],
        compiler_params=pltpu.CompilerParams(vmem_limit_bytes=room * MIB),
        cost_estimate=pl.CostEstimate(flops=flops, bytes_accessed=moved, transcendentals=0),
    )(*args)


def dot(a, b):
    return jnp.dot(a, b, preferred_element_type=F32)


def dot_t(a, b):
    return lax.dot_general(a, b, (((1,), (1,)), ((), ())), preferred_element_type=F32)


def shifted(value, axis, step):
    return lax.ppermute(value, axis, [(i, (i + step) % 4) for i in range(4)])


def swapped(value, axis):
    return lax.ppermute(value, axis, SWAP)


def split_sum(value):
    high = value.astype(BF16)
    return high, (value - high.astype(F32)).astype(BF16)


Y, X, ZL, ZH, C = range(5)


def teacher_kernel(pos, a0, a1, a2, a3, w0, w1, w2, w3, mine, other, rows, weights):
    y, x, zl, c = pos[Y], pos[X], pos[ZL], pos[C]
    for step, part in enumerate((a0, a1, a2, a3)):
        index = lax.rem(y + 4 - step, 4)
        place = 2 * lax.rem(index + c, 2) + lax.div(index, 2)
        rows[pl.ds(pl.multiple_of(place * ROWS, ROWS), ROWS), :] = part[...]
    for step, part in enumerate((w0, w1, w2, w3)):
        first = lax.rem(x + 4 - step, 4) * 256
        for turn in range(4):
            start = pl.multiple_of(first + lax.rem(zl + 4 - turn, 4) * 64, 64)
            weights[pl.ds(start, 64), :] = part[turn * 64 : turn * 64 + 64, :]
    product = dot_t(rows[...], weights[...]).astype(BF16)
    for half in range(2):
        mine[half] = product[half * ROWS : half * ROWS + ROWS]
        other[half] = product[(half + 2) * ROWS : (half + 3) * ROWS]


def pair_kernel(pos, mine, got, first, second):
    zh = pos[ZH]
    first[...] = (mine[zh].astype(F32) + got[zh].astype(F32)).astype(BF16)
    second[...] = (mine[1 - zh].astype(F32) + got[1 - zh].astype(F32)).astype(BF16)


def hidden_kernel(pos, first, second, residual, hidden, sums):
    value = residual[...].astype(F32) + (first[...].astype(F32) + second[...].astype(F32))
    hidden[...] = value
    lane = lax.broadcasted_iota(jnp.int32, (ROWS, 128), 1)
    total = jnp.sum(value, axis=1, keepdims=True)
    square = jnp.sum(value * value, axis=1, keepdims=True)
    both = jnp.where(lane == 0, total, jnp.where(lane == 1, square, 0.0))
    sums[...] = jnp.transpose(both)[0:8]


def place_kernel(pos, shard, shard_t, got, block, place_t, weights):
    token = lax.broadcasted_iota(jnp.int32, (ROWS, ROWS), 0)
    token_t = lax.broadcasted_iota(jnp.int32, (ROWS, ROWS), 1)
    slot = lax.broadcasted_iota(jnp.int32, (ROWS, SHARDS * SLOT), 1)
    spare = lax.broadcasted_iota(jnp.int32, (8, SHARDS * SLOT), 1)
    lane = lax.broadcasted_iota(jnp.int32, (ROWS, 256), 1)
    counts = dot((lax.rem(spare, SLOT) == CAP).astype(F32).astype(BF16), got[...])[0:1]
    block[...] = jnp.zeros_like(block)
    place_t[...] = jnp.zeros_like(place_t)
    for i in range(3):
        column = shard[:, i : i + 1]
        row = shard_t[i : i + 1, :]
        same = column == row
        rank = jnp.sum(jnp.where(same & (token_t < token), 1, 0), axis=1, keepdims=True)
        rank_t = jnp.sum(jnp.where(same & (token < token_t), 1, 0), axis=0, keepdims=True)
        place_t[i : i + 1, :] = row * SLOT + rank_t
        select = (slot == column * SLOT + rank).astype(F32).astype(BF16)
        value = dot(select, got[...]).astype(BF16)
        block[:, OFFSETS[i] : OFFSETS[i] + QUARTERS[i]] = value[:, : QUARTERS[i]]
        owned = jnp.sum(jnp.where(lane == column + 64 * i, counts, 0.0), axis=1, keepdims=True)
        weights[:, 128 * i : 128 * i + 128] = jnp.broadcast_to(
            TOKENS / (GROUPS[i] * owned), (ROWS, 128)
        )


def student_kernel(
    pos, own, own_c, own_z, own_zc, gain_s, gain_b, gain_l, head_s, head_b, head_l,
    xhat, scales, outs, n0, n1, n2, n3, blocks, lines,
):
    y, zh, c = pos[Y], pos[ZH], pos[C]
    blocks[2 * zh + c] = own[...]
    blocks[2 * zh + 1 - c] = own_c[...]
    blocks[2 * (1 - zh) + c] = own_z[...]
    blocks[2 * (1 - zh) + 1 - c] = own_zc[...]
    xhat[...] = jnp.zeros_like(xhat)
    for i, (gain, head) in enumerate(((gain_s, head_s), (gain_b, head_b), (gain_l, head_l))):
        wide, first, first_line = QUARTERS[i], OFFSETS[i], LINES[i]
        parts = [blocks[b, :, first : first + wide].astype(F32) for b in range(4)]
        total = sum(jnp.sum(p, axis=1, keepdims=True) for p in parts)
        square = sum(jnp.sum(p * p, axis=1, keepdims=True) for p in parts)
        center = total / WIDTHS[i]
        scale = lax.rsqrt(square / WIDTHS[i] - center * center + 1e-06)
        scales[:, 128 * i : 128 * i + 128] = jnp.broadcast_to(scale, (ROWS, 128))
        out = jnp.zeros((ROWS, 1024), F32)
        for b in range(4):
            value = (parts[b] - center) * scale
            xhat[b, :, first : first + wide] = value
            normed = value * gain[:, b * wide : b * wide + wide]
            out = out + dot(normed.astype(BF16), head[b * wide : b * wide + wide, :])
            lines[b, first_line : first_line + wide, :] = jnp.transpose(normed).astype(BF16)
        outs[i] = out
    for step, out in enumerate((n0, n1, n2, n3)):
        out[...] = lines[lax.rem(y + step, 4)]


def error_kernel(
    pos, hidden, sums, teacher_gain, outs, weights, xhat,
    gain_s, gain_b, gain_l, head_s, head_b, head_l,
    errors, mine, other, backs,
):
    c = pos[C]
    stats = jnp.transpose(jnp.concatenate([sums[...], jnp.zeros((120, 128), F32)], axis=0))
    center = stats[:, 0:1] / D
    spread = stats[:, 1:2] / D - center * center
    target = (hidden[...] - center) * lax.rsqrt(spread + 1e-06) * teacher_gain[...]
    target = target.astype(BF16).astype(F32)
    lane = lax.broadcasted_iota(jnp.int32, (ROWS, 64), 1)
    moments = jnp.zeros((ROWS, 64), F32)
    for i, (gain, head) in enumerate(((gain_s, head_s), (gain_b, head_b), (gain_l, head_l))):
        wide, first = QUARTERS[i], OFFSETS[i]
        weight = weights[:, 128 * i : 128 * i + 1]
        diff = outs[i] - target
        error = (weight * diff).astype(BF16)
        errors[i] = error
        loss = weight * jnp.sum(diff * diff, axis=1, keepdims=True)
        one = jnp.zeros((ROWS, 1), F32)
        two = jnp.zeros((ROWS, 1), F32)
        for b in range(4):
            back = dot_t(error, head[b * wide : b * wide + wide, :])
            value = xhat[b, :, first : first + wide]
            upper = back * gain[:, b * wide : b * wide + wide]
            one = one + jnp.sum(upper, axis=1, keepdims=True)
            two = two + jnp.sum(upper * value, axis=1, keepdims=True)
            backs[b, :, first : first + wide] = back
        moments = jnp.where(lane == 3 * i, one, jnp.where(lane == 3 * i + 1, two, moments))
        moments = jnp.where(lane == 3 * i + 2, loss, moments)
    high, low = split_sum(moments)
    turned = jnp.concatenate([high.astype(F32)[:, :32], low.astype(F32)[:, :32]], axis=1)
    zeros = jnp.zeros((ROWS, 32), F32)
    for half in range(2):
        mine[half] = backs[2 * half + c]
        mine[half, :, SPARE : SPARE + 64] = moments
        mine[half, :, BLOCK - 32 : BLOCK] = zeros
        other[half] = backs[2 * half + 1 - c].astype(BF16)
        other[half, :, SPARE : SPARE + 64] = turned.astype(BF16)
        other[half, :, BLOCK - 32 : BLOCK] = zeros.astype(BF16)


def grads_kernel(
    pos, n0, n1, n2, n3, e0, e1, e2, e3, keep, m1, m2, m3, total
):
    x = pos[X]
    for i in range(3):
        wide, first = QUARTERS[i], LINES[i]
        lines = jnp.concatenate([n[first : first + wide, :] for n in (n0, n1, n2, n3)], axis=1)
        errors = jnp.concatenate([e[i] for e in (e0, e1, e2, e3)], axis=0)
        total[first : first + wide, :] = dot(lines, errors)

    def piece(index):
        return (
            total[pl.ds(pl.multiple_of(index * 64, 8), 64), :],
            total[pl.ds(pl.multiple_of(256 + index * 48, 8), 48), :],
            total[pl.ds(pl.multiple_of(448 + index * 24, 8), 24), :],
        )

    keep[0:64, :], keep[64:112, :], keep[112:136, :] = piece(x)
    for step, out in ((1, m1), (2, m2), (3, m3)):
        large, base, small = piece(lax.rem(x + step, 4))
        out[0:64, :] = large.astype(BF16)
        out[64:112, :] = base.astype(BF16)
        out[112:144, :] = jnp.concatenate([small, jnp.zeros((8, 1024), F32)], axis=0).astype(BF16)


def back_kernel(pos, mine, got, keep, send, both):
    zh = pos[ZH]
    for half in range(2):
        both[half] = mine[half] + got[half].astype(F32)
    keep[...] = both[zh]
    send[...] = both[1 - zh].astype(BF16)
    value = both[0, :, SPARE : SPARE + 64]
    moments = value[:, 0:32] + value[:, 32:64]
    high, low = split_sum(moments)
    keep[:, SPARE : SPARE + 64] = jnp.concatenate([moments, jnp.zeros((ROWS, 32), F32)], axis=1)
    send[:, SPARE : SPARE + 64] = jnp.concatenate(
        [high.astype(F32), low.astype(F32)], axis=1
    ).astype(BF16)


def pieces_kernel(pos, keep, got, xhat, pieces):
    t = 2 * pos[ZH] + pos[C]
    back = keep[...] + got[...].astype(F32)
    moments = back[:, SPARE : SPARE + 32] + back[:, SPARE + 32 : SPARE + 64]
    terms = jnp.sum(back * xhat[t], axis=0, keepdims=True)
    pieces[...] = jnp.zeros_like(pieces)
    for j in range(5):
        pieces[j : j + 1, :] = terms[:, 128 * j : 128 * j + 128]
    pieces[5:6, 0:32] = jnp.sum(moments, axis=0, keepdims=True)


def rows_kernel(
    pos, keep, got, xhat, scales, place_t, gain_s, gain_b, gain_l, piece, piece_z, slots, gains
):
    t = 2 * pos[ZH] + pos[C]
    back = keep[...] + got[...].astype(F32)
    moments = back[:, SPARE : SPARE + 32] + back[:, SPARE + 32 : SPARE + 64]
    value = xhat[t]
    for i, gain in enumerate((gain_s, gain_b, gain_l)):
        wide = QUARTERS[i]
        for b in range(4):
            gains[b : b + 1, OFFSETS[i] : OFFSETS[i] + wide] = gain[:, b * wide : b * wide + wide]
    gain_row = gains[pl.ds(t, 1), :]
    pair = piece[...] + piece_z[...]
    high, low = split_sum(pair[5:6, 0:32])
    tail = jnp.concatenate(
        [pair[4:5], high.astype(F32), low.astype(F32), jnp.zeros((1, 64), F32)], axis=1
    )
    even = jnp.concatenate([jnp.concatenate([pair[0:1], pair[1:2]], axis=1), tail], axis=0)
    odd = jnp.concatenate([pair[2:3], pair[3:4]], axis=1)
    odd = jnp.concatenate([odd, jnp.zeros((1, 256), F32)], axis=0)
    spare = jnp.where(lax.rem(pos[ZL], 2) == 0, even, odd)
    spare = jnp.concatenate([spare, jnp.zeros((6, 256), F32)], axis=0)
    at = lax.broadcasted_iota(jnp.int32, (SHARDS * SLOT, 8), 0)
    kind = lax.broadcasted_iota(jnp.int32, (SHARDS * SLOT, 8), 1)
    ride = (lax.rem(at, SLOT) == CAP + kind).astype(F32).astype(BF16)
    slot = lax.broadcasted_iota(jnp.int32, (SHARDS * SLOT, ROWS), 0)
    total = dot(ride, spare.astype(BF16))
    for i in range(3):
        first, wide = OFFSETS[i], QUARTERS[i]
        hat = value[:, first : first + wide]
        upper = back[:, first : first + wide] * gain_row[:, first : first + wide]
        one = moments[:, 3 * i : 3 * i + 1] / WIDTHS[i]
        two = moments[:, 3 * i + 1 : 3 * i + 2] / WIDTHS[i]
        rows = scales[:, 128 * i : 128 * i + 1] * (upper - one - hat * two)
        if wide < 256:
            rows = jnp.concatenate([rows, jnp.zeros((ROWS, 256 - wide), F32)], axis=1)
        select = (slot == place_t[i : i + 1, :]).astype(F32).astype(BF16)
        total = total + dot(select, rows.astype(BF16))
    slots[...] = total.astype(BF16)


def third_kernel(pos, kept, p1, p2, p3, keep, m1, m2, m3, parts):
    zl = pos[ZL]
    total = kept[...] + sum(p[...].astype(F32)[0:136] for p in (p1, p2, p3))
    for i in range(4):
        parts[i, 0:16, :] = total[16 * i : 16 * i + 16]
        parts[i, 16:28, :] = total[64 + 12 * i : 64 + 12 * i + 12]
        parts[i, 28:34, :] = total[112 + 6 * i : 112 + 6 * i + 6]
        parts[i, 34:48, :] = jnp.zeros((14, 1024), F32)
    keep[...] = parts[zl]
    for step, out in ((1, m1), (2, m2), (3, m3)):
        out[...] = parts[lax.rem(zl + step, 4)].astype(BF16)


def last_kernel(pos, keep, m1, m2, m3, small, base, large):
    total = keep[...] + sum(p[...].astype(F32) for p in (m1, m2, m3))
    total = total / ROOT
    large[...] = total[0:16]
    base[...] = total[16:28]
    small[...] = total[28:34]


def sums_kernel(pos, got, gain_s, gain_b, gain_l, losses):
    slot = lax.broadcasted_iota(jnp.int32, (8, SHARDS * SLOT), 1)
    row = lax.broadcasted_iota(jnp.int32, (8, SHARDS * SLOT), 0)
    kind = 2 * lax.rem(lax.div(slot, SLOT), 2) + lax.rem(slot, SLOT) - CAP
    select = (lax.rem(slot, SLOT) >= CAP) & (kind == row)
    total = dot(select.astype(F32).astype(BF16), got[...])
    gain_l[...] = total[0:1] / ROOT
    gain_s[...] = total[1:2, 0:96] / ROOT
    gain_b[...] = total[2:3, 0:192] / ROOT
    loss = (total[1:2, 128:160] + total[1:2, 160:192]) / (2.0 * D * TOKENS)
    lane = lax.broadcasted_iota(jnp.int32, (1, 3), 1)
    losses[...] = jnp.where(
        lane == 0, loss[:, 2:3], jnp.where(lane == 1, loss[:, 5:6], loss[:, 8:9])
    )


def per_device(
    attn_out,
    out_proj,
    residual,
    teacher_gain,
    student_feats,
    head_small,
    head_base,
    head_large,
    gain_small,
    gain_base,
    gain_large,
    row_shard,
):
    pos = jnp.stack([lax.axis_index(a).astype(jnp.int32) for a in ("y", "x", "zl", "zh", "c")])
    tensor = 2 * pos[ZH] + pos[C]
    heads = (head_small, head_base, head_large)
    gains = (gain_small[None, :], gain_base[None, :], gain_large[None, :])

    own = out_proj.T
    early = [own] + [shifted(own, "zl", s) for s in (1, 2, 3)]
    weights = jnp.concatenate(early, axis=0)
    rows = [attn_out] + [shifted(attn_out, "y", s) for s in (1, 2, 3)]
    weights = [weights] + [shifted(weights, "x", s) for s in (1, 2, 3)]

    shard_t = jnp.pad(row_shard.T, ((0, 5), (0, 0)))
    shard_ids = jnp.arange(SHARDS, dtype=jnp.int32)
    named = (row_shard.T[:, :, None] == shard_ids[None, None, :]).astype(F32)
    own_counts = jnp.sum(named, axis=1).reshape(3 * SHARDS)
    feats = lax.dynamic_slice(student_feats, (0, tensor * 256), (SHARDS * CAP, 256))
    counts_row = jnp.pad(own_counts.astype(BF16), (0, 64))
    ride = jnp.broadcast_to(counts_row[None, None, :], (SHARDS, 2, 256))
    sent = jnp.concatenate([feats.reshape(SHARDS, CAP, 256), ride], axis=1)
    got = lax.all_to_all(sent, ("y", "x", "zl"), 0, 0, tiled=True).reshape(SHARDS * SLOT, 256)
    block, place_t, token_weights = call(
        place_kernel,
        [((ROWS, BLOCK), BF16), ((8, ROWS), jnp.int32), ((ROWS, 384), F32)],
        pos, row_shard, shard_t, got,
        flops=3 * 2 * 128 * 1024 * 256, moved=1 << 20,
    )
    block_c = swapped(block, "c")
    block_z = swapped(block, "zh")

    mine, other = call(
        teacher_kernel,
        [((2, ROWS, 1024), BF16)] * 2,
        pos, *rows, *weights,
        scratch=[((512, 1024), BF16), ((1024, 1024), BF16)],
        flops=2 * 512 * 1024 * 1024, moved=5 << 20, room=16,
    )
    first, second = call(
        pair_kernel, [((ROWS, 1024), BF16)] * 2, pos, mine, swapped(other, "c"), moved=2 << 20
    )
    parts = []
    for k, value in enumerate((first, second)):
        links = []
        for py in range(4):
            for pzh in range(2):
                for pc in range(2):
                    links.append(((py * 2 + pzh) * 2 + pc, (pc + 2 * ((pzh + k) % 2)) * 4 + py))
        parts.append(lax.ppermute(value, ("y", "zh", "c"), links))


    hidden, sums = call(
        hidden_kernel, [((ROWS, 1024), F32), ((8, ROWS), F32)], pos, *parts, residual, moved=1 << 20
    )
    block_z, hidden = lax.optimization_barrier((block_z, hidden))
    block_zc = swapped(block_z, "c")
    xhat, scales, outs, *lines = call(
        student_kernel,
        [
            ((4, ROWS, BLOCK), F32),
            ((ROWS, 384), F32),
            ((3, ROWS, 1024), F32),
        ]
        + [((544, ROWS), BF16)] * 4,
        pos, block, block_c, block_z, block_zc, *gains, *heads,
        scratch=[((4, ROWS, BLOCK), BF16), ((4, 544, ROWS), BF16)],
        flops=2 * 128 * 2176 * 1024, moved=9 << 20, room=20,
    )
    sums = sums + swapped(sums, "c")
    sums = sums + swapped(sums, "zh")

    lines = [lines[0]] + [shifted(lines[s], "y", s) for s in (1, 2, 3)]
    sums, lines = lax.optimization_barrier((sums, lines))
    errors, mine, other = call(
        error_kernel,
        [((3, ROWS, 1024), BF16), ((2, ROWS, BLOCK), F32), ((2, ROWS, BLOCK), BF16)],
        pos, hidden, sums, teacher_gain[None, :], outs, token_weights, xhat,
        *gains, *heads,
        scratch=[((4, ROWS, BLOCK), F32)],
        flops=4 * 128 * 2176 * 1024, moved=15 << 20, room=28,
    )
    errors = [errors] + [shifted(errors, "y", s) for s in (1, 2, 3)]

    got = swapped(other, "c")
    keep, send = call(
        back_kernel,
        [((ROWS, BLOCK), F32), ((ROWS, BLOCK), BF16)],
        pos, mine, got,
        scratch=[((2, ROWS, BLOCK), F32)], moved=2 << 20,
    )
    got = swapped(send, "zh")
    (pieces,) = call(pieces_kernel, [((8, 128), F32)], pos, keep, got, xhat, moved=1 << 20)
    pieces_z = lax.ppermute(pieces, "zl", [(0, 1), (1, 0), (2, 3), (3, 2)])
    (slots,) = call(
        rows_kernel,
        [((SHARDS * SLOT, 256), BF16)],
        pos, keep, got, xhat, scales, place_t, *gains, pieces, pieces_z,
        scratch=[((8, BLOCK), F32)],
        flops=3 * 2 * 128 * 1024 * 256, moved=2 << 20,
    )
    got = lax.all_to_all(slots.reshape(SHARDS, SLOT, 256), ("y", "x", "zl"), 0, 0, tiled=True)
    token_gradient = got[:, :CAP].reshape(SHARDS * CAP, 256)
    gain_s, gain_b, gain_l, losses = call(
        sums_kernel,
        [((1, n), F32) for n in (96, 192, 256, 3)],
        pos, got.reshape(SHARDS * SLOT, 256), moved=1 << 19,
    )

    keep, *sent = call(
        grads_kernel,
        [((136, 1024), F32)] + [((144, 1024), BF16)] * 3,
        pos, *lines, *errors,
        scratch=[((544, 1024), F32)], flops=2 * 512 * 544 * 1024, moved=5 << 20, room=16,
    )
    keep, *sent = call(
        third_kernel,
        [((48, 1024), F32)] + [((48, 1024), BF16)] * 3,
        pos, keep, *[shifted(sent[s - 1], "x", s) for s in (1, 2, 3)],
        scratch=[((4, 48, 1024), F32)], moved=2 << 20,
    )
    sent = [shifted(sent[s - 1], "zl", s) for s in (1, 2, 3)]
    sent, token_gradient, gain_s, gain_b, gain_l, losses = lax.optimization_barrier(
        (sent, token_gradient, gain_s, gain_b, gain_l, losses)
    )
    grad_small, grad_base, grad_large = call(
        last_kernel,
        [((6, 1024), F32), ((12, 1024), F32), ((16, 1024), F32)],
        pos, keep, *sent,
        moved=1 << 20,
    )
    return (
        grad_small,
        grad_base,
        grad_large,
        gain_s[0],
        gain_b[0],
        gain_l[0],
        token_gradient,
        losses[0],
    )


def solution(mesh):
    fine = Mesh(mesh.devices.reshape(4, 4, 4, 2, 2), ("y", "x", "zl", "zh", "c"))
    dp = ("y", "x", "zl")
    tp = ("zh", "c")
    return jax.shard_map(
        per_device,
        mesh=fine,
        in_specs=(
            P(dp, tp),
            P(tp, dp),
            P(dp, tp),
            P(tp),
            P(dp, None),
            P(None, tp),
            P(None, tp),
            P(None, tp),
            P(),
            P(),
            P(),
            P(dp, None),
        ),
        out_specs=(
            P(dp, tp),
            P(dp, tp),
            P(dp, tp),
            P(tp),
            P(tp),
            P(tp),
            P(dp, tp),
            P(),
        ),
        check_vma=False,
    )
```

time: 211 us -> 198 us (0.938)
  waiting for transfers between devices: 101 us -> 87.5 us
  starting transfers between devices: 63.9 us -> 72.8 us
  Pallas kernels: 28.3 us -> 22.4 us
    ppermute x10 -> x8, waiting for transfers between devices: 25.5 us -> 12.7 us  [swapped(): return lax.ppermute(value, axis, SWAP)]
    ppermute x24 -> x21, waiting for transfers between devices: 55.9 us -> 46.6 us  [shifted(): return lax.ppermute(value, axis, [(i, (i + step) % 4) for i in range(4)])]
    pallas_call x12 -> x13, Pallas kernels: 28.3 us -> 22.4 us  [call(): pl.pallas_call(body, out_shape=[jax.ShapeDtypeStruct(shape, dtype) for sh...]
    ppermute x24 -> x21, starting transfers between devices: 39.1 us -> 33.5 us  [shifted(): return lax.ppermute(value, axis, [(i, (i + step) % 4) for i in range(4)])]
    ppermute x10 -> x8, starting transfers between devices: 5.76 us -> 10.6 us  [swapped(): return lax.ppermute(value, axis, SWAP)]
    ppermute x2, waiting for transfers between devices: 19.9 us -> 24.6 us  [per_device(): parts.append(lax.ppermute(value, ('y', 'zh', 'c'), links))]
    ppermute x2, starting transfers between devices: 6.25 us -> 10.7 us  [per_device(): parts.append(lax.ppermute(value, ('y', 'zh', 'c'), links))]
    ppermute x0 -> x1, waiting for transfers between devices: none -> 3.59 us  [per_device(): pieces_z = lax.ppermute(pieces, 'zl', [(0, 1), (1, 0), (2, 3), (3, 2)])]
  transfers between devices with their start and end apart: 38 -> 34, of which waited for: 19 -> 18; matrix products, arithmetic and copies ran while one was open for 4% -> 4% of each run, Pallas kernels for 9% -> 8%
where the time goes in v3:
time: 198 us; the launch traced here: 197 us
  waiting for transfers between devices  87.5 us (44%)
  starting transfers between devices  72.8 us (37%)
  Pallas kernels  22.4 us (11%)
  local copies, waits for them, and re-layouts  9.39 us (5%)
  other arithmetic  3.73 us (2%)
    ppermute x21, waiting for transfers between devices, shifted(): return lax.ppermute(value, axis, [(i, (i + step) % 4) for i in range(4)])  46.6 us
    ppermute x21, starting transfers between devices, shifted(): return lax.ppermute(value, axis, [(i, (i + step) % 4) for i in range(4)])  33.5 us
    ppermute x2, waiting for transfers between devices, per_device(): parts.append(lax.ppermute(value, ('y', 'zh', 'c'), links))  24.6 us
    pallas_call x13, Pallas kernels, call(): pl.pallas_call(body, out_shape=[jax.ShapeDtypeStruct(shape, dtype) for sh...  22.4 us
    ppermute x8, waiting for transfers between devices, swapped(): return lax.ppermute(value, axis, SWAP)  12.7 us
    ppermute x2, starting transfers between devices, per_device(): parts.append(lax.ppermute(value, ('y', 'zh', 'c'), links))  10.7 us
    ppermute x8, starting transfers between devices, swapped(): return lax.ppermute(value, axis, SWAP)  10.6 us
    all_to_all x1, starting transfers between devices, per_device(): lax.all_to_all(sent, ('y', 'x', 'zl'), 0, 0, tiled=True)  10.3 us
  transfers between devices with their start and end apart: 34, of which 18 were waited for; matrix products, arithmetic and copies ran while one was open for 4% of the time, Pallas kernels for 8%

profile of v3, /device:TPU:32, one launch (start us, length us, event | category | flops | bytes accessed | tf_op | source)
XLA Modules:
  0.0 196.7 jit_solution(12181401406802348433)
XLA Ops:
  0.6 1.9 collective-permute-start.5
  2.6 1.5 collective-permute-start.4
  4.1 2.8 %collective-permute-start.3 = (bf16[64,1024]{1,0:T(8,128)(2,1)}, bf16[64,1024]{1,0:T(8,128)(2,1)S(1)}, u32[]{:S(2)}, u32[]{:S(2)}) collective-permute-start(bf16[64,1024]{1,0:T(8,128)(2,1)} %bitcast.25), channel_id=1, source_target_pairs={{0,4},{4,8},{8,12},{12,0},{1,5},{5,9},{9,13},{13,1},{2,6},{6,10},{... | collective-permute-start | bytes 393224 | tf_op jit(solution)/shard_map/ppermute | solution.py:55
  6.9 3.2 %collective-permute-start.1 = (bf16[128,1024]{1,0:T(8,128)(2,1)}, bf16[128,1024]{1,0:T(8,128)(2,1)}, u32[]{:S(2)}, u32[]{:S(2)}) collective-permute-start(bf16[128,1024]{1,0:T(8,128)(2,1)} %a0.1), channel_id=1, source_target_pairs={{0,128},{64,192},{128,0},{192,64},{1,129},{65,193},{129,1},{193,65... | collective-permute-start | bytes 786440 | tf_op jit(solution)/shard_map/ppermute | solution.py:55
  11.0 2.7 %collective-permute-done.4 = bf16[64,1024]{1,0:T(8,128)(2,1)S(1)} collective-permute-done((bf16[64,1024]{1,0:T(8,128)(2,1)}, bf16[64,1024]{1,0:T(8,128)(2,1)S(1)}, u32[]{:S(2)}, u32[]{:S(2)}) %collective-permute-start.4) | collective-permute-done | bytes 131104 | tf_op jit(solution)/shard_map/ppermute | solution.py:55
  13.7 1.9 collective-permute-done.3
  16.6 2.8 %collective-permute-start.8 = (bf16[256,1024]{1,0:T(8,128)(2,1)S(1)}, bf16[256,1024]{1,0:T(8,128)(2,1)S(1)}, u32[]{:S(2)}, u32[]{:S(2)}) collective-permute-start(bf16[256,1024]{1,0:T(8,128)(2,1)S(1)} %pad_maximum_fusion.w0), channel_id=1, source_target_pairs={{0,48},{16,0},{32,16},{48,32},{1,49},{17,1},{33,17},{49,33},{2,50}... | collective-permute-start | bytes 1572872 | tf_op jit(solution)/shard_map/ppermute | solution.py:55
  21.9 2.0 %reshape.35 = bf16[64,14,256]{2,1,0:T(8,128)(2,1)} reshape(bf16[896,256]{1,0:T(8,128)(2,1)} %constant_dynamic-slice_fusion) | data formatting | bytes 917504 | tf_op jit(solution)/shard_map/reshape | solution.py:362
  23.9 2.0 %pad_maximum_fusion.1 = bf16[64,16,256]{2,1,0:T(8,128)(2,1)} fusion(bf16[64,2,256]{2,1,0:T(2,128)(2,1)S(1)} %broadcast_in_dim.20, bf16[64,14,256]{2,1,0:T(8,128)(2,1)} %reshape.35), kind=kLoop, calls=%fused_computation.1 | loop fusion | flops 1048576 | bytes 1048576 | tf_op jit(solution)/shard_map/concatenate | solution.py:362
  25.9 10.3 %all-to-all-start = ((bf16[64,16,256]{2,1,0:T(8,128)(2,1)}), bf16[64,16,256]{2,1,0:T(8,128)(2,1)}, u32[]{:S(2)}, u32[]{:S(2)}) async-start(bf16[64,16,256]{2,1,0:T(8,128)(2,1)} %pad_maximum_fusion.1), calls=%async_computation | async-start | bytes 1048576 | tf_op jit(solution)/shard_map/all_to_all | solution.py:363
  36.2 1.5 collective-permute-start
  37.8 1.8 collective-permute-start.2
  39.6 7.5 %collective-permute-done.a1 = bf16[128,1024]{1,0:T(8,128)(2,1)} collective-permute-done((bf16[128,1024]{1,0:T(8,128)(2,1)}, bf16[128,1024]{1,0:T(8,128)(2,1)}, u32[]{:S(2)}, u32[]{:S(2)}) %collective-permute-start) | collective-permute-done | bytes 262176 | tf_op jit(solution)/shard_map/ppermute | solution.py:55
  47.6 2.1 %collective-permute-done.6.w1 = bf16[256,1024]{1,0:T(8,128)(2,1)} collective-permute-done((bf16[256,1024]{1,0:T(8,128)(2,1)S(1)}, bf16[256,1024]{1,0:T(8,128)(2,1)}, u32[]{:S(2)}, u32[]{:S(2)}) %collective-permute-start.6) | collective-permute-done | bytes 524320 | tf_op jit(solution)/shard_map/ppermute | solution.py:55
  50.6 2.8 %shard_map.179 = (bf16[2,128,1024]{2,1,0:T(8,128)(2,1)S(1)}, bf16[2,128,1024]{2,1,0:T(8,128)(2,1)S(1)}) custom-call(s32[5]{0:T(128)S(1)} %stack.23.pos, bf16[128,1024]{1,0:T(8,128)(2,1)S(1)} %copy-done.14, bf16[128,1024]{1,0:T(8,128)(2,1)} %collective-permute-done.a1, bf16[128,1024]{1,0:T(8,128)(2,1)} %collective-permute-done.1.a2, ...), custom_call_target="tpu_custom_call" | custom-call | flops 1073741824 | bytes 5242880 | tf_op jit(solution)/shard_map/pallas_call | solution.py:35
  53.5 1.9 collective-permute-done.9.got
  55.4 1.4 shard_map.180
  56.8 3.6 %collective-permute-start.10 = (bf16[128,1024]{1,0:T(8,128)(2,1)}, bf16[128,1024]{1,0:T(8,128)(2,1)}, u32[]{:S(2)}, u32[]{:S(2)}) collective-permute-start(bf16[128,1024]{1,0:T(8,128)(2,1)} %get-tuple-element.61), channel_id=1, source_target_pairs={{0,0},{1,64},{2,128},{3,192},{64,1},{65,65},{66,129},{67,193},{128... | collective-permute-start | bytes 786440 | tf_op jit(solution)/shard_map/ppermute | solution.py:390
  60.4 7.1 %collective-permute-start.11 = (bf16[128,1024]{1,0:T(8,128)(2,1)}, bf16[128,1024]{1,0:T(8,128)(2,1)}, u32[]{:S(2)}, u32[]{:S(2)}) collective-permute-start(bf16[128,1024]{1,0:T(8,128)(2,1)} %get-tuple-element.62), channel_id=1, source_target_pairs={{0,128},{1,192},{2,0},{3,64},{64,129},{65,193},{66,1},{67,65},{128... | collective-permute-start | bytes 786440 | tf_op jit(solution)/shard_map/ppermute | solution.py:390
  67.7 1.8 shard_map.182
  69.9 24.6 %collective-permute-done.11.second = bf16[128,1024]{1,0:T(8,128)(2,1)} collective-permute-done((bf16[128,1024]{1,0:T(8,128)(2,1)}, bf16[128,1024]{1,0:T(8,128)(2,1)}, u32[]{:S(2)}, u32[]{:S(2)}) %collective-permute-start.11) | collective-permute-done | bytes 262176 | tf_op jit(solution)/shard_map/ppermute | solution.py:390
  95.4 1.3 shard_map.181
  97.8 1.4 collective-permute-done.16.own_zc
  99.2 1.6 copy-done.1
  100.7 1.9 shard_map.183
  103.9 2.1 %collective-permute-start.19 = (bf16[544,128]{1,0:T(8,128)(2,1)S(1)}, bf16[544,128]{1,0:T(8,128)(2,1)S(1)}, u32[]{:S(2)}, u32[]{:S(2)}) collective-permute-start(bf16[544,128]{1,0:T(8,128)(2,1)S(1)} %get-tuple-element.70), channel_id=1, source_target_pairs={{0,192},{64,0},{128,64},{192,128},{1,193},{65,1},{129,65},{193,129... | collective-permute-start | bytes 417800 | tf_op jit(solution)/shard_map/ppermute | solution.py:55
  106.0 1.2 collective-permute-done.12
  107.2 5.8 %collective-permute-start.13 = (f32[8,128]{1,0:T(8,128)S(1)}, f32[8,128]{1,0:T(8,128)S(1)}, u32[]{:S(2)}, u32[]{:S(2)}) collective-permute-start(f32[8,128]{1,0:T(8,128)S(1)} %add.16), channel_id=1, source_target_pairs={{0,2},{2,0},{1,3},{3,1},{4,6},{6,4},{5,7},{7,5},{8,10},{10,8},{9,1... | collective-permute-start | bytes 12296 | tf_op jit(solution)/shard_map/ppermute | solution.py:59
  113.0 1.7 collective-permute-done.13
  114.8 3.4 %shard_map.184 = (bf16[3,128,1024]{2,1,0:T(8,128)(2,1)}, f32[2,128,640]{2,1,0:T(8,128)S(1)}, bf16[2,128,640]{2,1,0:T(8,128)(2,1)S(1)}) custom-call(s32[5]{0:T(128)S(1)} %stack.23.pos, f32[128,1024]{1,0:T(8,128)S(1)} %get-tuple-element.75.hidden, f32[8,128]{1,0:T(8,128)S(1)} %add.17.sums, f32[1,1024]{1,0:T(1,128)S(1)} %bitcast.22, ...), custom_call_target="tpu_custom_call" | custom-call | flops 1140850688 | bytes 15728640 | tf_op jit(solution)/shard_map/pallas_call | solution.py:35
  118.3 1.2 collective-permute-start.22
  119.4 1.9 collective-permute-start.21
  121.3 1.3 collective-permute-start.20
  123.5 4.2 %collective-permute-start.30 = (bf16[128,640]{1,0:T(8,128)(2,1)S(1)}, bf16[128,640]{1,0:T(8,128)(2,1)S(1)}, u32[]{:S(2)}, u32[]{:S(2)}) collective-permute-start(bf16[128,640]{1,0:T(8,128)(2,1)S(1)} %get-tuple-element.92), channel_id=1, source_target_pairs={{0,2},{2,0},{1,3},{3,1},{4,6},{6,4},{5,7},{7,5},{8,10},{10,8},{9,1... | collective-permute-start | bytes 491528 | tf_op jit(solution)/shard_map/ppermute | solution.py:59
  127.7 5.5 %collective-permute-done.30.got = bf16[128,640]{1,0:T(8,128)(2,1)S(1)} collective-permute-done((bf16[128,640]{1,0:T(8,128)(2,1)S(1)}, bf16[128,640]{1,0:T(8,128)(2,1)S(1)}, u32[]{:S(2)}, u32[]{:S(2)}) %collective-permute-start.30) | collective-permute-done | bytes 163872 | tf_op jit(solution)/shard_map/ppermute | solution.py:59
  134.0 3.6 %collective-permute-done.31.piece_z = f32[8,128]{1,0:T(8,128)S(1)} collective-permute-done((f32[8,128]{1,0:T(8,128)S(1)}, f32[8,128]{1,0:T(8,128)S(1)}, u32[]{:S(2)}, u32[]{:S(2)}) %collective-permute-start.31) | collective-permute-done | bytes 4128 | tf_op jit(solution)/shard_map/ppermute | solution.py:434
  137.5 2.2 %shard_map.189 = bf16[1024,256]{1,0:T(8,128)(2,1)} custom-call(s32[5]{0:T(128)S(1)} %stack.23.pos, f32[128,640]{1,0:T(8,128)S(1)} %get-tuple-element.91.keep, bf16[128,640]{1,0:T(8,128)(2,1)S(1)} %collective-permute-done.30.got, f32[4,128,640]{2,1,0:T(8,128)S(1)} %get-tuple-element.79.xhat, f32[128,384]{1,0:T(8,128)S(1)} %get-tuple-element.93.scales, ...), custom_call_target="tpu_custom_call" | custom-call | flops 201326592 | bytes 2097152 | tf_op jit(solution)/shard_map/pallas_call | solution.py:35
  139.7 7.7 %all-to-all-start.1 = ((bf16[64,16,256]{2,1,0:T(8,128)(2,1)}), bf16[64,16,256]{2,1,0:T(8,128)(2,1)S(1)}, u32[]{:S(2)}, u32[]{:S(2)}) async-start(bf16[64,16,256]{2,1,0:T(8,128)(2,1)} %bitcast.10), calls=%async_computation.1 | async-start | bytes 1048576 | tf_op jit(solution)/shard_map/all_to_all | solution.py:442
  147.5 15.6 %collective-permute-done.20.e1 = bf16[3,128,1024]{2,1,0:T(8,128)(2,1)} collective-permute-done((bf16[3,128,1024]{2,1,0:T(8,128)(2,1)}, bf16[3,128,1024]{2,1,0:T(8,128)(2,1)}, u32[]{:S(2)}, u32[]{:S(2)}) %collective-permute-start.20) | collective-permute-done | bytes 786464 | tf_op jit(solution)/shard_map/ppermute | solution.py:55
  164.9 2.6 %shard_map.185 = (f32[136,1024]{1,0:T(8,128)S(1)}, bf16[144,1024]{1,0:T(8,128)(2,1)S(1)}, bf16[144,1024]{1,0:T(8,128)(2,1)S(1)}, bf16[144,1024]{1,0:T(8,128)(2,1)S(1)}) custom-call(s32[5]{0:T(128)S(1)} %stack.23.pos, bf16[544,128]{1,0:T(8,128)(2,1)S(1)} %get-tuple-element.71.n0, bf16[544,128]{1,0:T(8,128)(2,1)S(1)} %copy-done.7, ...), custom_call_target="tpu_custom_call" | custom-call | flops 570425344 | bytes 5242880 | tf_op jit(solution)/shard_map/pallas_call | solution.py:35
  167.7 2.4 %collective-permute-start.24 = (bf16[144,1024]{1,0:T(8,128)(2,1)S(1)}, bf16[144,1024]{1,0:T(8,128)(2,1)S(1)}, u32[]{:S(2)}, u32[]{:S(2)}) collective-permute-start(bf16[144,1024]{1,0:T(8,128)(2,1)S(1)} %get-tuple-element.83), channel_id=1, source_target_pairs={{0,32},{16,48},{32,0},{48,16},{1,33},{17,49},{33,1},{49,17},{2,34}... | collective-permute-start | bytes 884744 | tf_op jit(solution)/shard_map/ppermute | solution.py:55
  170.1 1.6 collective-permute-start.25
  171.7 12.2 %collective-permute-done.23.p1 = bf16[144,1024]{1,0:T(8,128)(2,1)S(1)} collective-permute-done((bf16[144,1024]{1,0:T(8,128)(2,1)S(1)}, bf16[144,1024]{1,0:T(8,128)(2,1)S(1)}, u32[]{:S(2)}, u32[]{:S(2)}) %collective-permute-start.23) | collective-permute-done | bytes 294944 | tf_op jit(solution)/shard_map/ppermute | solution.py:55
  185.4 2.7 %collective-permute-start.26 = (bf16[48,1024]{1,0:T(8,128)(2,1)S(1)}, bf16[48,1024]{1,0:T(8,128)(2,1)S(1)}, u32[]{:S(2)}, u32[]{:S(2)}) collective-permute-start(bf16[48,1024]{1,0:T(8,128)(2,1)S(1)} %get-tuple-element.86), channel_id=1, source_target_pairs={{0,4},{4,8},{8,12},{12,0},{1,5},{5,9},{9,13},{13,1},{2,6},{6,10},{... | collective-permute-start | bytes 294920 | tf_op jit(solution)/shard_map/ppermute | solution.py:55
  188.2 1.6 collective-permute-start.28
  189.7 1.4 shard_map.190
  192.0 2.5 %collective-permute-done.26.m1 = bf16[48,1024]{1,0:T(8,128)(2,1)S(1)} collective-permute-done((bf16[48,1024]{1,0:T(8,128)(2,1)S(1)}, bf16[48,1024]{1,0:T(8,128)(2,1)S(1)}, u32[]{:S(2)}, u32[]{:S(2)}) %collective-permute-start.26) | collective-permute-done | bytes 98336 | tf_op jit(solution)/shard_map/ppermute | solution.py:55
  195.5 1.2 shard_map.191
  (85 shorter events, 16.8 us)
Async XLA Ops:
  0.6 20.5 %copy-start = (bf16[896,1024]{1,0:T(8,128)(2,1)S(1)}, bf16[896,1024]{1,0:T(8,128)(2,1)}, u32[]{:S(2)}) copy-start(bf16[896,1024]{1,0:T(8,128)(2,1)} %param.16) | copy-start | bytes 5505028
  0.6 10.3 %collective-permute-start.5 = (bf16[64,1024]{1,0:T(8,128)(2,1)}, bf16[64,1024]{1,0:T(8,128)(2,1)S(1)}, u32[]{:S(2)}, u32[]{:S(2)}) collective-permute-start(bf16[64,1024]{1,0:T(8,128)(2,1)} %bitcast.23), channel_id=1, source_target_pairs={{0,12},{4,0},{8,4},{12,8},{1,13},{5,1},{9,5},{13,9},{2,14},{6,2},{... | collective-permute-start | bytes 393224 | tf_op jit(solution)/shard_map/ppermute | solution.py:55
  2.6 11.1 %collective-permute-start.4 = (bf16[64,1024]{1,0:T(8,128)(2,1)}, bf16[64,1024]{1,0:T(8,128)(2,1)S(1)}, u32[]{:S(2)}, u32[]{:S(2)}) collective-permute-start(bf16[64,1024]{1,0:T(8,128)(2,1)} %bitcast.24), channel_id=1, source_target_pairs={{0,8},{4,12},{8,0},{12,4},{1,9},{5,13},{9,1},{13,5},{2,10},{6,14},... | collective-permute-start | bytes 393224 | tf_op jit(solution)/shard_map/ppermute | solution.py:55
  4.1 11.5 %collective-permute-start.3 = (bf16[64,1024]{1,0:T(8,128)(2,1)}, bf16[64,1024]{1,0:T(8,128)(2,1)S(1)}, u32[]{:S(2)}, u32[]{:S(2)}) collective-permute-start(bf16[64,1024]{1,0:T(8,128)(2,1)} %bitcast.25), channel_id=1, source_target_pairs={{0,4},{4,8},{8,12},{12,0},{1,5},{5,9},{9,13},{13,1},{2,6},{6,10},{... | collective-permute-start | bytes 393224 | tf_op jit(solution)/shard_map/ppermute | solution.py:55
  6.9 30.8 %collective-permute-start.1 = (bf16[128,1024]{1,0:T(8,128)(2,1)}, bf16[128,1024]{1,0:T(8,128)(2,1)}, u32[]{:S(2)}, u32[]{:S(2)}) collective-permute-start(bf16[128,1024]{1,0:T(8,128)(2,1)} %a0.1), channel_id=1, source_target_pairs={{0,128},{64,192},{128,0},{192,64},{1,129},{65,193},{129,1},{193,65... | collective-permute-start | bytes 786440 | tf_op jit(solution)/shard_map/ppermute | solution.py:55
  16.6 31.0 %collective-permute-start.8 = (bf16[256,1024]{1,0:T(8,128)(2,1)S(1)}, bf16[256,1024]{1,0:T(8,128)(2,1)S(1)}, u32[]{:S(2)}, u32[]{:S(2)}) collective-permute-start(bf16[256,1024]{1,0:T(8,128)(2,1)S(1)} %pad_maximum_fusion.w0), channel_id=1, source_target_pairs={{0,48},{16,0},{32,16},{48,32},{1,49},{17,1},{33,17},{49,33},{2,50}... | collective-permute-start | bytes 1572872 | tf_op jit(solution)/shard_map/ppermute | solution.py:55
  19.4 28.2 %collective-permute-start.7 = (bf16[256,1024]{1,0:T(8,128)(2,1)S(1)}, bf16[256,1024]{1,0:T(8,128)(2,1)S(1)}, u32[]{:S(2)}, u32[]{:S(2)}) collective-permute-start(bf16[256,1024]{1,0:T(8,128)(2,1)S(1)} %pad_maximum_fusion.w0), channel_id=1, source_target_pairs={{0,32},{16,48},{32,0},{48,16},{1,33},{17,49},{33,1},{49,17},{2,34}... | collective-permute-start | bytes 1572872 | tf_op jit(solution)/shard_map/ppermute | solution.py:55
  20.2 29.5 %collective-permute-start.6 = (bf16[256,1024]{1,0:T(8,128)(2,1)S(1)}, bf16[256,1024]{1,0:T(8,128)(2,1)}, u32[]{:S(2)}, u32[]{:S(2)}) collective-permute-start(bf16[256,1024]{1,0:T(8,128)(2,1)S(1)} %pad_maximum_fusion.w0), channel_id=1, source_target_pairs={{0,16},{16,32},{32,48},{48,0},{1,17},{17,33},{33,49},{49,1},{2,18}... | collective-permute-start | bytes 1572872 | tf_op jit(solution)/shard_map/ppermute | solution.py:55
  25.9 41.7 %all-to-all-start = ((bf16[64,16,256]{2,1,0:T(8,128)(2,1)}), bf16[64,16,256]{2,1,0:T(8,128)(2,1)}, u32[]{:S(2)}, u32[]{:S(2)}) async-start(bf16[64,16,256]{2,1,0:T(8,128)(2,1)} %pad_maximum_fusion.1), calls=%async_computation | async-start | bytes 1048576 | tf_op jit(solution)/shard_map/all_to_all | solution.py:363
  36.2 10.9 %collective-permute-start = (bf16[128,1024]{1,0:T(8,128)(2,1)}, bf16[128,1024]{1,0:T(8,128)(2,1)}, u32[]{:S(2)}, u32[]{:S(2)}) collective-permute-start(bf16[128,1024]{1,0:T(8,128)(2,1)} %a0.1), channel_id=1, source_target_pairs={{0,64},{64,128},{128,192},{192,0},{1,65},{65,129},{129,193},{193,1... | collective-permute-start | bytes 786440 | tf_op jit(solution)/shard_map/ppermute | solution.py:55
  37.8 9.8 %collective-permute-start.2 = (bf16[128,1024]{1,0:T(8,128)(2,1)}, bf16[128,1024]{1,0:T(8,128)(2,1)}, u32[]{:S(2)}, u32[]{:S(2)}) collective-permute-start(bf16[128,1024]{1,0:T(8,128)(2,1)} %a0.1), channel_id=1, source_target_pairs={{0,192},{64,0},{128,64},{192,128},{1,193},{65,1},{129,65},{193,129... | collective-permute-start | bytes 786440 | tf_op jit(solution)/shard_map/ppermute | solution.py:55
  39.5 28.0 %copy-start.15 = (s32[128,3]{0,1:T(4,128)S(1)}, s32[128,3]{0,1:T(4,128)}, u32[]{:S(2)}) copy-start(s32[128,3]{0,1:T(4,128)} %param.23) | copy-start | bytes 4612
  50.6 47.1 %copy-start.17 = (f32[384]{0:T(512)S(1)}, f32[384]{0:T(512)}, u32[]{:S(2)}) copy-start(f32[384]{0:T(512)} %param.20) | copy-start | bytes 4612
  50.6 47.2 %copy-start.16 = (f32[768]{0:T(1024)S(1)}, f32[768]{0:T(1024)}, u32[]{:S(2)}) copy-start(f32[768]{0:T(1024)} %param.21) | copy-start | bytes 9220
  50.6 48.5 %copy-start.12 = (f32[1024]{0:T(1024)S(1)}, f32[1024]{0:T(1024)}, u32[]{:S(2)}) copy-start(f32[1024]{0:T(1024)} %param.22) | copy-start | bytes 12292
  53.4 45.8 %copy-start.3 = (bf16[768,1024]{1,0:T(8,128)(2,1)S(1)}, bf16[768,1024]{1,0:T(8,128)(2,1)}, u32[]{:S(2)}) copy-start(bf16[768,1024]{1,0:T(8,128)(2,1)} %head_b.3) | copy-start | bytes 4718596
  53.4 2.0 %collective-permute-start.9 = (bf16[2,128,1024]{2,1,0:T(8,128)(2,1)S(1)}, bf16[2,128,1024]{2,1,0:T(8,128)(2,1)S(1)}, u32[]{:S(2)}, u32[]{:S(2)}) collective-permute-start(bf16[2,128,1024]{2,1,0:T(8,128)(2,1)S(1)} %get-tuple-element.60), channel_id=1, source_target_pairs={{0,1},{1,0},{2,3},{3,2},{4,5},{5,4},{6,7},{7,6},{8,9},{9,8},{10,11... | collective-permute-start | bytes 1572872 | tf_op jit(solution)/shard_map/ppermute | solution.py:59
  56.8 13.1 %collective-permute-start.10 = (bf16[128,1024]{1,0:T(8,128)(2,1)}, bf16[128,1024]{1,0:T(8,128)(2,1)}, u32[]{:S(2)}, u32[]{:S(2)}) collective-permute-start(bf16[128,1024]{1,0:T(8,128)(2,1)} %get-tuple-element.61), channel_id=1, source_target_pairs={{0,0},{1,64},{2,128},{3,192},{64,1},{65,65},{66,129},{67,193},{128... | collective-permute-start | bytes 786440 | tf_op jit(solution)/shard_map/ppermute | solution.py:390
  60.4 34.1 %collective-permute-start.11 = (bf16[128,1024]{1,0:T(8,128)(2,1)}, bf16[128,1024]{1,0:T(8,128)(2,1)}, u32[]{:S(2)}, u32[]{:S(2)}) collective-permute-start(bf16[128,1024]{1,0:T(8,128)(2,1)} %get-tuple-element.62), channel_id=1, source_target_pairs={{0,128},{1,192},{2,0},{3,64},{64,129},{65,193},{66,1},{67,65},{128... | collective-permute-start | bytes 786440 | tf_op jit(solution)/shard_map/ppermute | solution.py:390
  67.6 31.5 %copy-start.4 = (bf16[384,1024]{1,0:T(8,128)(2,1)S(1)}, bf16[384,1024]{1,0:T(8,128)(2,1)}, u32[]{:S(2)}) copy-start(bf16[384,1024]{1,0:T(8,128)(2,1)} %head_s.3) | copy-start | bytes 2359300
  69.5 28.2 %collective-permute-start.15 = (bf16[128,640]{1,0:T(8,128)(2,1)S(1)}, bf16[128,640]{1,0:T(8,128)(2,1)S(1)}, u32[]{:S(2)}, u32[]{:S(2)}) collective-permute-start(bf16[128,640]{1,0:T(8,128)(2,1)S(1)} %get-tuple-element.64.own), channel_id=1, source_target_pairs={{0,2},{2,0},{1,3},{3,1},{4,6},{6,4},{5,7},{7,5},{8,10},{10,8},{9,1... | collective-permute-start | bytes 491528 | tf_op jit(solution)/shard_map/ppermute | solution.py:59
  69.6 28.2 %collective-permute-start.14 = (bf16[128,640]{1,0:T(8,128)(2,1)S(1)}, bf16[128,640]{1,0:T(8,128)(2,1)S(1)}, u32[]{:S(2)}, u32[]{:S(2)}) collective-permute-start(bf16[128,640]{1,0:T(8,128)(2,1)S(1)} %get-tuple-element.64.own), channel_id=1, source_target_pairs={{0,1},{1,0},{2,3},{3,2},{4,5},{5,4},{6,7},{7,6},{8,9},{9,8},{10,11... | collective-permute-start | bytes 491528 | tf_op jit(solution)/shard_map/ppermute | solution.py:59
  97.7 1.4 collective-permute-start.16
  99.1 1.6 copy-start.1
  100.7 14.0 %copy-start.2 = (bf16[1024,1024]{1,0:T(8,128)(2,1)S(1)}, bf16[1024,1024]{1,0:T(8,128)(2,1)}, u32[]{:S(2)}) copy-start(bf16[1024,1024]{1,0:T(8,128)(2,1)} %head_l.3) | copy-start | bytes 6291460
  100.7 14.0 %copy-start.13 = (f32[1024]{0:T(1024)S(1)}, f32[1024]{0:T(1024)}, u32[]{:S(2)}) copy-start(f32[1024]{0:T(1024)} %param.15) | copy-start | bytes 12292
  102.7 12.0 %collective-permute-start.17 = (bf16[544,128]{1,0:T(8,128)(2,1)S(1)}, bf16[544,128]{1,0:T(8,128)(2,1)S(1)}, u32[]{:S(2)}, u32[]{:S(2)}) collective-permute-start(bf16[544,128]{1,0:T(8,128)(2,1)S(1)} %get-tuple-element.68), channel_id=1, source_target_pairs={{0,64},{64,128},{128,192},{192,0},{1,65},{65,129},{129,193},{193,1... | collective-permute-start | bytes 417800 | tf_op jit(solution)/shard_map/ppermute | solution.py:55
  103.0 11.7 %collective-permute-start.18 = (bf16[544,128]{1,0:T(8,128)(2,1)S(1)}, bf16[544,128]{1,0:T(8,128)(2,1)S(1)}, u32[]{:S(2)}, u32[]{:S(2)}) collective-permute-start(bf16[544,128]{1,0:T(8,128)(2,1)S(1)} %get-tuple-element.69), channel_id=1, source_target_pairs={{0,128},{64,192},{128,0},{192,64},{1,129},{65,193},{129,1},{193,65... | collective-permute-start | bytes 417800 | tf_op jit(solution)/shard_map/ppermute | solution.py:55
  103.9 10.8 %collective-permute-start.19 = (bf16[544,128]{1,0:T(8,128)(2,1)S(1)}, bf16[544,128]{1,0:T(8,128)(2,1)S(1)}, u32[]{:S(2)}, u32[]{:S(2)}) collective-permute-start(bf16[544,128]{1,0:T(8,128)(2,1)S(1)} %get-tuple-element.70), channel_id=1, source_target_pairs={{0,192},{64,0},{128,64},{192,128},{1,193},{65,1},{129,65},{193,129... | collective-permute-start | bytes 417800 | tf_op jit(solution)/shard_map/ppermute | solution.py:55
  106.0 1.2 collective-permute-start.12
  107.2 7.5 %collective-permute-start.13 = (f32[8,128]{1,0:T(8,128)S(1)}, f32[8,128]{1,0:T(8,128)S(1)}, u32[]{:S(2)}, u32[]{:S(2)}) collective-permute-start(f32[8,128]{1,0:T(8,128)S(1)} %add.16), channel_id=1, source_target_pairs={{0,2},{2,0},{1,3},{3,1},{4,6},{6,4},{5,7},{7,5},{8,10},{10,8},{9,1... | collective-permute-start | bytes 12296 | tf_op jit(solution)/shard_map/ppermute | solution.py:59
  114.7 3.4 %copy-start.6 = (bf16[544,128]{1,0:T(8,128)(2,1)}, bf16[544,128]{1,0:T(8,128)(2,1)S(1)}, u32[]{:S(2)}) copy-start(bf16[544,128]{1,0:T(8,128)(2,1)S(1)} %collective-permute-done.17.n1) | copy-start | bytes 417796
  114.7 3.4 %copy-start.8 = (bf16[544,128]{1,0:T(8,128)(2,1)}, bf16[544,128]{1,0:T(8,128)(2,1)S(1)}, u32[]{:S(2)}) copy-start(bf16[544,128]{1,0:T(8,128)(2,1)S(1)} %collective-permute-done.18.n2) | copy-start | bytes 417796
  114.7 3.4 %copy-start.10 = (bf16[544,128]{1,0:T(8,128)(2,1)}, bf16[544,128]{1,0:T(8,128)(2,1)S(1)}, u32[]{:S(2)}) copy-start(bf16[544,128]{1,0:T(8,128)(2,1)S(1)} %collective-permute-done.19.n3) | copy-start | bytes 417796
  118.2 4.5 %collective-permute-start.29 = (bf16[2,128,640]{2,1,0:T(8,128)(2,1)S(1)}, bf16[2,128,640]{2,1,0:T(8,128)(2,1)S(1)}, u32[]{:S(2)}, u32[]{:S(2)}) collective-permute-start(bf16[2,128,640]{2,1,0:T(8,128)(2,1)S(1)} %get-tuple-element.90), channel_id=1, source_target_pairs={{0,1},{1,0},{2,3},{3,2},{4,5},{5,4},{6,7},{7,6},{8,9},{9,8},{10,11... | collective-permute-start | bytes 983048 | tf_op jit(solution)/shard_map/ppermute | solution.py:59
  118.3 29.2 %collective-permute-start.22 = (bf16[3,128,1024]{2,1,0:T(8,128)(2,1)}, bf16[3,128,1024]{2,1,0:T(8,128)(2,1)S(1)}, u32[]{:S(2)}, u32[]{:S(2)}) collective-permute-start(bf16[3,128,1024]{2,1,0:T(8,128)(2,1)} %get-tuple-element.80.e0), channel_id=1, source_target_pairs={{0,192},{64,0},{128,64},{192,128},{1,193},{65,1},{129,65},{193,129... | collective-permute-start | bytes 2359304 | tf_op jit(solution)/shard_map/ppermute | solution.py:55
  119.4 28.0 %collective-permute-start.21 = (bf16[3,128,1024]{2,1,0:T(8,128)(2,1)}, bf16[3,128,1024]{2,1,0:T(8,128)(2,1)}, u32[]{:S(2)}, u32[]{:S(2)}) collective-permute-start(bf16[3,128,1024]{2,1,0:T(8,128)(2,1)} %get-tuple-element.80.e0), channel_id=1, source_target_pairs={{0,128},{64,192},{128,0},{192,64},{1,129},{65,193},{129,1},{193,65... | collective-permute-start | bytes 2359304 | tf_op jit(solution)/shard_map/ppermute | solution.py:55
  121.3 41.7 %collective-permute-start.20 = (bf16[3,128,1024]{2,1,0:T(8,128)(2,1)}, bf16[3,128,1024]{2,1,0:T(8,128)(2,1)}, u32[]{:S(2)}, u32[]{:S(2)}) collective-permute-start(bf16[3,128,1024]{2,1,0:T(8,128)(2,1)} %get-tuple-element.80.e0), channel_id=1, source_target_pairs={{0,64},{64,128},{128,192},{192,0},{1,65},{65,129},{129,193},{193,1... | collective-permute-start | bytes 2359304 | tf_op jit(solution)/shard_map/ppermute | solution.py:55
  123.5 9.7 %collective-permute-start.30 = (bf16[128,640]{1,0:T(8,128)(2,1)S(1)}, bf16[128,640]{1,0:T(8,128)(2,1)S(1)}, u32[]{:S(2)}, u32[]{:S(2)}) collective-permute-start(bf16[128,640]{1,0:T(8,128)(2,1)S(1)} %get-tuple-element.92), channel_id=1, source_target_pairs={{0,2},{2,0},{1,3},{3,1},{4,6},{6,4},{5,7},{7,5},{8,10},{10,8},{9,1... | collective-permute-start | bytes 491528 | tf_op jit(solution)/shard_map/ppermute | solution.py:59
  133.9 29.2 %copy-start.7 = (bf16[544,128]{1,0:T(8,128)(2,1)S(1)}, bf16[544,128]{1,0:T(8,128)(2,1)}, u32[]{:S(2)}) copy-start(bf16[544,128]{1,0:T(8,128)(2,1)} %copy-done.6) | copy-start | bytes 417796
  133.9 3.6 %collective-permute-start.31 = (f32[8,128]{1,0:T(8,128)S(1)}, f32[8,128]{1,0:T(8,128)S(1)}, u32[]{:S(2)}, u32[]{:S(2)}) collective-permute-start(f32[8,128]{1,0:T(8,128)S(1)} %shard_map.188.piece), channel_id=1, source_target_pairs={{0,4},{4,0},{8,12},{12,8},{1,5},{5,1},{9,13},{13,9},{2,6},{6,2},{1... | collective-permute-start | bytes 12296 | tf_op jit(solution)/shard_map/ppermute | solution.py:434
  139.7 50.0 %all-to-all-start.1 = ((bf16[64,16,256]{2,1,0:T(8,128)(2,1)}), bf16[64,16,256]{2,1,0:T(8,128)(2,1)S(1)}, u32[]{:S(2)}, u32[]{:S(2)}) async-start(bf16[64,16,256]{2,1,0:T(8,128)(2,1)} %bitcast.10), calls=%async_computation.1 | async-start | bytes 1048576 | tf_op jit(solution)/shard_map/all_to_all | solution.py:442
  167.5 16.5 %collective-permute-start.23 = (bf16[144,1024]{1,0:T(8,128)(2,1)S(1)}, bf16[144,1024]{1,0:T(8,128)(2,1)S(1)}, u32[]{:S(2)}, u32[]{:S(2)}) collective-permute-start(bf16[144,1024]{1,0:T(8,128)(2,1)S(1)} %get-tuple-element.82), channel_id=1, source_target_pairs={{0,16},{16,32},{32,48},{48,0},{1,17},{17,33},{33,49},{49,1},{2,18}... | collective-permute-start | bytes 884744 | tf_op jit(solution)/shard_map/ppermute | solution.py:55
  167.7 16.2 %collective-permute-start.24 = (bf16[144,1024]{1,0:T(8,128)(2,1)S(1)}, bf16[144,1024]{1,0:T(8,128)(2,1)S(1)}, u32[]{:S(2)}, u32[]{:S(2)}) collective-permute-start(bf16[144,1024]{1,0:T(8,128)(2,1)S(1)} %get-tuple-element.83), channel_id=1, source_target_pairs={{0,32},{16,48},{32,0},{48,16},{1,33},{17,49},{33,1},{49,17},{2,34}... | collective-permute-start | bytes 884744 | tf_op jit(solution)/shard_map/ppermute | solution.py:55
  170.1 14.5 %collective-permute-start.25 = (bf16[144,1024]{1,0:T(8,128)(2,1)S(1)}, bf16[144,1024]{1,0:T(8,128)(2,1)S(1)}, u32[]{:S(2)}, u32[]{:S(2)}) collective-permute-start(bf16[144,1024]{1,0:T(8,128)(2,1)S(1)} %get-tuple-element.84), channel_id=1, source_target_pairs={{0,48},{16,0},{32,16},{48,32},{1,49},{17,1},{33,17},{49,33},{2,50}... | collective-permute-start | bytes 884744 | tf_op jit(solution)/shard_map/ppermute | solution.py:55
  185.4 9.1 %collective-permute-start.26 = (bf16[48,1024]{1,0:T(8,128)(2,1)S(1)}, bf16[48,1024]{1,0:T(8,128)(2,1)S(1)}, u32[]{:S(2)}, u32[]{:S(2)}) collective-permute-start(bf16[48,1024]{1,0:T(8,128)(2,1)S(1)} %get-tuple-element.86), channel_id=1, source_target_pairs={{0,4},{4,8},{8,12},{12,0},{1,5},{5,9},{9,13},{13,1},{2,6},{6,10},{... | collective-permute-start | bytes 294920 | tf_op jit(solution)/shard_map/ppermute | solution.py:55
  188.2 7.4 %collective-permute-start.27 = (bf16[48,1024]{1,0:T(8,128)(2,1)S(1)}, bf16[48,1024]{1,0:T(8,128)(2,1)S(1)}, u32[]{:S(2)}, u32[]{:S(2)}) collective-permute-start(bf16[48,1024]{1,0:T(8,128)(2,1)S(1)} %get-tuple-element.87), channel_id=1, source_target_pairs={{0,8},{4,12},{8,0},{12,4},{1,9},{5,13},{9,1},{13,5},{2,10},{6,14},... | collective-permute-start | bytes 294920 | tf_op jit(solution)/shard_map/ppermute | solution.py:55
  188.2 7.4 %collective-permute-start.28 = (bf16[48,1024]{1,0:T(8,128)(2,1)S(1)}, bf16[48,1024]{1,0:T(8,128)(2,1)S(1)}, u32[]{:S(2)}, u32[]{:S(2)}) collective-permute-start(bf16[48,1024]{1,0:T(8,128)(2,1)S(1)} %get-tuple-element.88), channel_id=1, source_target_pairs={{0,12},{4,0},{8,4},{12,8},{1,13},{5,1},{9,5},{13,9},{2,14},{6,2},{... | collective-permute-start | bytes 294920 | tf_op jit(solution)/shard_map/ppermute | solution.py:55
  (4 other events, 3.7 us)

commit v4 on v3

--- a/solution.py
+++ b/solution.py
@@ -439,6 +439,7 @@
         scratch=[((8, BLOCK), F32)],
         flops=3 * 2 * 128 * 1024 * 256, moved=2 << 20,
     )
+    slots, errors[1], errors[2], errors[3] = lax.optimization_barrier((slots, *errors[1:]))
     got = lax.all_to_all(slots.reshape(SHARDS, SLOT, 256), ("y", "x", "zl"), 0, 0, tiled=True)
     token_gradient = got[:, :CAP].reshape(SHARDS * CAP, 256)
     gain_s, gain_b, gain_l, losses = call(

time: 198 us -> 204 us (1.030)
  local copies, waits for them, and re-layouts: 9.39 us -> 16.5 us
    unnamed x37 -> x49, local copies, waits for them, and re-layouts: 5.47 us -> 12.6 us
    ppermute x8, waiting for transfers between devices: 12.7 us -> 15 us  [swapped(): return lax.ppermute(value, axis, SWAP)]
    ppermute x21, waiting for transfers between devices: 46.6 us -> 44.4 us  [shifted(): return lax.ppermute(value, axis, [(i, (i + step) % 4) for i in range(4)])]
  transfers between devices with their start and end apart: 34 -> 34, of which waited for: 18 -> 20; matrix products, arithmetic and copies ran while one was open for 4% -> 4% of each run, Pallas kernels for 8% -> 7%
where the time goes in v4:
time: 204 us; the launch traced here: 203 us
  waiting for transfers between devices  87.5 us (43%)
  starting transfers between devices  73.6 us (36%)
  Pallas kernels  20.8 us (10%)
  local copies, waits for them, and re-layouts  16.5 us (8%)
  other arithmetic  3.72 us (2%)
    ppermute x21, waiting for transfers between devices, shifted(): return lax.ppermute(value, axis, [(i, (i + step) % 4) for i in range(4)])  44.4 us
    ppermute x21, starting transfers between devices, shifted(): return lax.ppermute(value, axis, [(i, (i + step) % 4) for i in range(4)])  34.7 us
    ppermute x2, waiting for transfers between devices, per_device(): parts.append(lax.ppermute(value, ('y', 'zh', 'c'), links))  24.6 us
    pallas_call x13, Pallas kernels, call(): pl.pallas_call(body, out_shape=[jax.ShapeDtypeStruct(shape, dtype) for sh...  20.8 us
    ppermute x8, waiting for transfers between devices, swapped(): return lax.ppermute(value, axis, SWAP)  15 us
    unnamed x49, local copies, waits for them, and re-layouts  12.6 us
    ppermute x2, starting transfers between devices, per_device(): parts.append(lax.ppermute(value, ('y', 'zh', 'c'), links))  10.7 us
    ppermute x8, starting transfers between devices, swapped(): return lax.ppermute(value, axis, SWAP)  10.3 us
  transfers between devices with their start and end apart: 34, of which 20 were waited for; matrix products, arithmetic and copies ran while one was open for 4% of the time, Pallas kernels for 7%

profile of v4, /device:TPU:32, one launch (start us, length us, event | category | flops | bytes accessed | tf_op | source)
XLA Modules:
  0.0 203.0 jit_solution(18116543000917525420)
XLA Ops:
  0.6 1.9 collective-permute-start.5
  2.6 1.5 collective-permute-start.4
  4.1 2.8 %collective-permute-start.3 = (bf16[64,1024]{1,0:T(8,128)(2,1)}, bf16[64,1024]{1,0:T(8,128)(2,1)S(1)}, u32[]{:S(2)}, u32[]{:S(2)}) collective-permute-start(bf16[64,1024]{1,0:T(8,128)(2,1)} %bitcast.25), channel_id=1, source_target_pairs={{0,4},{4,8},{8,12},{12,0},{1,5},{5,9},{9,13},{13,1},{2,6},{6,10},{... | collective-permute-start | bytes 393224 | tf_op jit(solution)/shard_map/ppermute | solution.py:55
  6.9 3.2 %collective-permute-start.1 = (bf16[128,1024]{1,0:T(8,128)(2,1)}, bf16[128,1024]{1,0:T(8,128)(2,1)}, u32[]{:S(2)}, u32[]{:S(2)}) collective-permute-start(bf16[128,1024]{1,0:T(8,128)(2,1)} %a0.1), channel_id=1, source_target_pairs={{0,128},{64,192},{128,0},{192,64},{1,129},{65,193},{129,1},{193,65... | collective-permute-start | bytes 786440 | tf_op jit(solution)/shard_map/ppermute | solution.py:55
  11.0 2.7 %collective-permute-done.4 = bf16[64,1024]{1,0:T(8,128)(2,1)S(1)} collective-permute-done((bf16[64,1024]{1,0:T(8,128)(2,1)}, bf16[64,1024]{1,0:T(8,128)(2,1)S(1)}, u32[]{:S(2)}, u32[]{:S(2)}) %collective-permute-start.4) | collective-permute-done | bytes 131104 | tf_op jit(solution)/shard_map/ppermute | solution.py:55
  13.7 1.9 collective-permute-done.3
  16.5 2.8 %collective-permute-start.8 = (bf16[256,1024]{1,0:T(8,128)(2,1)S(1)}, bf16[256,1024]{1,0:T(8,128)(2,1)S(1)}, u32[]{:S(2)}, u32[]{:S(2)}) collective-permute-start(bf16[256,1024]{1,0:T(8,128)(2,1)S(1)} %pad_maximum_fusion.w0), channel_id=1, source_target_pairs={{0,48},{16,0},{32,16},{48,32},{1,49},{17,1},{33,17},{49,33},{2,50}... | collective-permute-start | bytes 1572872 | tf_op jit(solution)/shard_map/ppermute | solution.py:55
  21.9 1.9 reshape.35
  23.9 2.0 pad_maximum_fusion.1
  25.9 10.3 %all-to-all-start = ((bf16[64,16,256]{2,1,0:T(8,128)(2,1)}), bf16[64,16,256]{2,1,0:T(8,128)(2,1)}, u32[]{:S(2)}, u32[]{:S(2)}) async-start(bf16[64,16,256]{2,1,0:T(8,128)(2,1)} %pad_maximum_fusion.1), calls=%async_computation | async-start | bytes 1048576 | tf_op jit(solution)/shard_map/all_to_all | solution.py:363
  36.2 1.5 collective-permute-start
  37.7 1.8 collective-permute-start.2
  39.6 7.5 %collective-permute-done.a1 = bf16[128,1024]{1,0:T(8,128)(2,1)} collective-permute-done((bf16[128,1024]{1,0:T(8,128)(2,1)}, bf16[128,1024]{1,0:T(8,128)(2,1)}, u32[]{:S(2)}, u32[]{:S(2)}) %collective-permute-start) | collective-permute-done | bytes 262176 | tf_op jit(solution)/shard_map/ppermute | solution.py:55
  47.5 2.1 %collective-permute-done.6.w1 = bf16[256,1024]{1,0:T(8,128)(2,1)} collective-permute-done((bf16[256,1024]{1,0:T(8,128)(2,1)S(1)}, bf16[256,1024]{1,0:T(8,128)(2,1)}, u32[]{:S(2)}, u32[]{:S(2)}) %collective-permute-start.6) | collective-permute-done | bytes 524320 | tf_op jit(solution)/shard_map/ppermute | solution.py:55
  50.6 2.8 %shard_map.179 = (bf16[2,128,1024]{2,1,0:T(8,128)(2,1)S(1)}, bf16[2,128,1024]{2,1,0:T(8,128)(2,1)S(1)}) custom-call(s32[5]{0:T(128)S(1)} %stack.23.pos, bf16[128,1024]{1,0:T(8,128)(2,1)S(1)} %copy-done.20, bf16[128,1024]{1,0:T(8,128)(2,1)} %collective-permute-done.a1, bf16[128,1024]{1,0:T(8,128)(2,1)} %collective-permute-done.1.a2, ...), custom_call_target="tpu_custom_call" | custom-call | flops 1073741824 | bytes 5242880 | tf_op jit(solution)/shard_map/pallas_call | solution.py:35
  53.5 1.9 collective-permute-done.9.got
  55.4 1.4 shard_map.180
  56.8 3.6 %collective-permute-start.10 = (bf16[128,1024]{1,0:T(8,128)(2,1)}, bf16[128,1024]{1,0:T(8,128)(2,1)}, u32[]{:S(2)}, u32[]{:S(2)}) collective-permute-start(bf16[128,1024]{1,0:T(8,128)(2,1)} %get-tuple-element.65), channel_id=1, source_target_pairs={{0,0},{1,64},{2,128},{3,192},{64,1},{65,65},{66,129},{67,193},{128... | collective-permute-start | bytes 786440 | tf_op jit(solution)/shard_map/ppermute | solution.py:390
  60.4 7.1 %collective-permute-start.11 = (bf16[128,1024]{1,0:T(8,128)(2,1)}, bf16[128,1024]{1,0:T(8,128)(2,1)}, u32[]{:S(2)}, u32[]{:S(2)}) collective-permute-start(bf16[128,1024]{1,0:T(8,128)(2,1)} %get-tuple-element.66), channel_id=1, source_target_pairs={{0,128},{1,192},{2,0},{3,64},{64,129},{65,193},{66,1},{67,65},{128... | collective-permute-start | bytes 786440 | tf_op jit(solution)/shard_map/ppermute | solution.py:390
  67.6 1.8 shard_map.182
  69.9 24.6 %collective-permute-done.11.second = bf16[128,1024]{1,0:T(8,128)(2,1)} collective-permute-done((bf16[128,1024]{1,0:T(8,128)(2,1)}, bf16[128,1024]{1,0:T(8,128)(2,1)}, u32[]{:S(2)}, u32[]{:S(2)}) %collective-permute-start.11) | collective-permute-done | bytes 262176 | tf_op jit(solution)/shard_map/ppermute | solution.py:390
  97.7 1.4 collective-permute-done.16.own_zc
  99.1 1.6 copy-done.1
  100.7 1.9 shard_map.183
  103.9 2.1 %collective-permute-start.19 = (bf16[544,128]{1,0:T(8,128)(2,1)S(1)}, bf16[544,128]{1,0:T(8,128)(2,1)S(1)}, u32[]{:S(2)}, u32[]{:S(2)}) collective-permute-start(bf16[544,128]{1,0:T(8,128)(2,1)S(1)} %get-tuple-element.74), channel_id=1, source_target_pairs={{0,192},{64,0},{128,64},{192,128},{1,193},{65,1},{129,65},{193,129... | collective-permute-start | bytes 417800 | tf_op jit(solution)/shard_map/ppermute | solution.py:55
  107.1 5.8 %collective-permute-start.13 = (f32[8,128]{1,0:T(8,128)S(1)}, f32[8,128]{1,0:T(8,128)S(1)}, u32[]{:S(2)}, u32[]{:S(2)}) collective-permute-start(f32[8,128]{1,0:T(8,128)S(1)} %add.16), channel_id=1, source_target_pairs={{0,2},{2,0},{1,3},{3,1},{4,6},{6,4},{5,7},{7,5},{8,10},{10,8},{9,1... | collective-permute-start | bytes 12296 | tf_op jit(solution)/shard_map/ppermute | solution.py:59
  112.9 1.7 collective-permute-done.13
  116.6 2.9 %shard_map.184 = (bf16[3,128,1024]{2,1,0:T(8,128)(2,1)S(1)}, f32[2,128,640]{2,1,0:T(8,128)S(1)}, bf16[2,128,640]{2,1,0:T(8,128)(2,1)S(1)}) custom-call(s32[5]{0:T(128)S(1)} %stack.23.pos, f32[128,1024]{1,0:T(8,128)S(1)} %get-tuple-element.79.hidden, f32[8,128]{1,0:T(8,128)S(1)} %add.17.sums, f32[1,1024]{1,0:T(1,128)S(1)} %bitcast.22, ...), custom_call_target="tpu_custom_call" | custom-call | flops 1140850688 | bytes 15728640 | tf_op jit(solution)/shard_map/pallas_call | solution.py:35
  120.7 2.0 collective-permute-start.24
  122.6 1.3 collective-permute-start.23
  123.9 1.6 collective-permute-done.20.got
  126.4 4.0 %collective-permute-start.21 = (bf16[128,640]{1,0:T(8,128)(2,1)S(1)}, bf16[128,640]{1,0:T(8,128)(2,1)S(1)}, u32[]{:S(2)}, u32[]{:S(2)}) collective-permute-start(bf16[128,640]{1,0:T(8,128)(2,1)S(1)} %get-tuple-element.88), channel_id=1, source_target_pairs={{0,2},{2,0},{1,3},{3,1},{4,6},{6,4},{5,7},{7,5},{8,10},{10,8},{9,1... | collective-permute-start | bytes 491528 | tf_op jit(solution)/shard_map/ppermute | solution.py:59
  130.4 6.2 %collective-permute-done.21.got = bf16[128,640]{1,0:T(8,128)(2,1)S(1)} collective-permute-done((bf16[128,640]{1,0:T(8,128)(2,1)S(1)}, bf16[128,640]{1,0:T(8,128)(2,1)S(1)}, u32[]{:S(2)}, u32[]{:S(2)}) %collective-permute-start.21) | collective-permute-done | bytes 163872 | tf_op jit(solution)/shard_map/ppermute | solution.py:59
  137.4 3.6 %collective-permute-done.22.piece_z = f32[8,128]{1,0:T(8,128)S(1)} collective-permute-done((f32[8,128]{1,0:T(8,128)S(1)}, f32[8,128]{1,0:T(8,128)S(1)}, u32[]{:S(2)}, u32[]{:S(2)}) %collective-permute-start.22) | collective-permute-done | bytes 4128 | tf_op jit(solution)/shard_map/ppermute | solution.py:434
  141.0 2.2 %shard_map.187 = bf16[1024,256]{1,0:T(8,128)(2,1)} custom-call(s32[5]{0:T(128)S(1)} %stack.23.pos, f32[128,640]{1,0:T(8,128)S(1)} %get-tuple-element.87.keep, bf16[128,640]{1,0:T(8,128)(2,1)S(1)} %collective-permute-done.21.got, f32[4,128,640]{2,1,0:T(8,128)S(1)} %get-tuple-element.83.xhat, f32[128,384]{1,0:T(8,128)S(1)} %get-tuple-element.89.scales, ...), custom_call_target="tpu_custom_call" | custom-call | flops 201326592 | bytes 2097152 | tf_op jit(solution)/shard_map/pallas_call | solution.py:35
  144.0 13.2 %collective-permute-done.23.e1 = bf16[3,128,1024]{2,1,0:T(8,128)(2,1)S(1)} collective-permute-done((bf16[3,128,1024]{2,1,0:T(8,128)(2,1)S(1)}, bf16[3,128,1024]{2,1,0:T(8,128)(2,1)S(1)}, u32[]{:S(2)}, u32[]{:S(2)}) %collective-permute-start.23) | collective-permute-done | bytes 786464 | tf_op jit(solution)/shard_map/ppermute | solution.py:55
  158.1 7.6 %all-to-all-start.1 = ((bf16[64,16,256]{2,1,0:T(8,128)(2,1)}), bf16[64,16,256]{2,1,0:T(8,128)(2,1)S(1)}, u32[]{:S(2)}, u32[]{:S(2)}) async-start(bf16[64,16,256]{2,1,0:T(8,128)(2,1)} %bitcast.10), calls=%async_computation.1 | async-start | bytes 1048576 | tf_op jit(solution)/shard_map/all_to_all | solution.py:443
  170.9 1.5 shard_map.188
  172.4 1.5 collective-permute-start.26
  174.0 2.7 %collective-permute-start.27 = (bf16[144,1024]{1,0:T(8,128)(2,1)S(1)}, bf16[144,1024]{1,0:T(8,128)(2,1)S(1)}, u32[]{:S(2)}, u32[]{:S(2)}) collective-permute-start(bf16[144,1024]{1,0:T(8,128)(2,1)S(1)} %get-tuple-element.96), channel_id=1, source_target_pairs={{0,32},{16,48},{32,0},{48,16},{1,33},{17,49},{33,1},{49,17},{2,34}... | collective-permute-start | bytes 884744 | tf_op jit(solution)/shard_map/ppermute | solution.py:55
  176.6 1.5 collective-permute-start.28
  178.1 6.2 %collective-permute-done.26.p1 = bf16[144,1024]{1,0:T(8,128)(2,1)S(1)} collective-permute-done((bf16[144,1024]{1,0:T(8,128)(2,1)S(1)}, bf16[144,1024]{1,0:T(8,128)(2,1)S(1)}, u32[]{:S(2)}, u32[]{:S(2)}) %collective-permute-start.26) | collective-permute-done | bytes 294944 | tf_op jit(solution)/shard_map/ppermute | solution.py:55
  184.3 5.9 %collective-permute-done.27.p2 = bf16[144,1024]{1,0:T(8,128)(2,1)S(1)} collective-permute-done((bf16[144,1024]{1,0:T(8,128)(2,1)S(1)}, bf16[144,1024]{1,0:T(8,128)(2,1)S(1)}, u32[]{:S(2)}, u32[]{:S(2)}) %collective-permute-start.27) | collective-permute-done | bytes 294944 | tf_op jit(solution)/shard_map/ppermute | solution.py:55
  191.1 1.5 collective-permute-start.29
  192.6 1.5 collective-permute-start.30
  195.1 1.4 shard_map.190
  197.4 1.6 collective-permute-done.29.m1
  200.0 1.8 collective-permute-done.31.m3
  (97 shorter events, 28.8 us)
Async XLA Ops:
  0.6 20.4 %copy-start = (bf16[896,1024]{1,0:T(8,128)(2,1)S(1)}, bf16[896,1024]{1,0:T(8,128)(2,1)}, u32[]{:S(2)}) copy-start(bf16[896,1024]{1,0:T(8,128)(2,1)} %param.16) | copy-start | bytes 5505028
  0.6 10.3 %collective-permute-start.5 = (bf16[64,1024]{1,0:T(8,128)(2,1)}, bf16[64,1024]{1,0:T(8,128)(2,1)S(1)}, u32[]{:S(2)}, u32[]{:S(2)}) collective-permute-start(bf16[64,1024]{1,0:T(8,128)(2,1)} %bitcast.23), channel_id=1, source_target_pairs={{0,12},{4,0},{8,4},{12,8},{1,13},{5,1},{9,5},{13,9},{2,14},{6,2},{... | collective-permute-start | bytes 393224 | tf_op jit(solution)/shard_map/ppermute | solution.py:55
  2.6 11.1 %collective-permute-start.4 = (bf16[64,1024]{1,0:T(8,128)(2,1)}, bf16[64,1024]{1,0:T(8,128)(2,1)S(1)}, u32[]{:S(2)}, u32[]{:S(2)}) collective-permute-start(bf16[64,1024]{1,0:T(8,128)(2,1)} %bitcast.24), channel_id=1, source_target_pairs={{0,8},{4,12},{8,0},{12,4},{1,9},{5,13},{9,1},{13,5},{2,10},{6,14},... | collective-permute-start | bytes 393224 | tf_op jit(solution)/shard_map/ppermute | solution.py:55
  4.1 11.5 %collective-permute-start.3 = (bf16[64,1024]{1,0:T(8,128)(2,1)}, bf16[64,1024]{1,0:T(8,128)(2,1)S(1)}, u32[]{:S(2)}, u32[]{:S(2)}) collective-permute-start(bf16[64,1024]{1,0:T(8,128)(2,1)} %bitcast.25), channel_id=1, source_target_pairs={{0,4},{4,8},{8,12},{12,0},{1,5},{5,9},{9,13},{13,1},{2,6},{6,10},{... | collective-permute-start | bytes 393224 | tf_op jit(solution)/shard_map/ppermute | solution.py:55
  6.9 30.8 %collective-permute-start.1 = (bf16[128,1024]{1,0:T(8,128)(2,1)}, bf16[128,1024]{1,0:T(8,128)(2,1)}, u32[]{:S(2)}, u32[]{:S(2)}) collective-permute-start(bf16[128,1024]{1,0:T(8,128)(2,1)} %a0.1), channel_id=1, source_target_pairs={{0,128},{64,192},{128,0},{192,64},{1,129},{65,193},{129,1},{193,65... | collective-permute-start | bytes 786440 | tf_op jit(solution)/shard_map/ppermute | solution.py:55
  16.5 31.0 %collective-permute-start.8 = (bf16[256,1024]{1,0:T(8,128)(2,1)S(1)}, bf16[256,1024]{1,0:T(8,128)(2,1)S(1)}, u32[]{:S(2)}, u32[]{:S(2)}) collective-permute-start(bf16[256,1024]{1,0:T(8,128)(2,1)S(1)} %pad_maximum_fusion.w0), channel_id=1, source_target_pairs={{0,48},{16,0},{32,16},{48,32},{1,49},{17,1},{33,17},{49,33},{2,50}... | collective-permute-start | bytes 1572872 | tf_op jit(solution)/shard_map/ppermute | solution.py:55
  19.4 28.2 %collective-permute-start.7 = (bf16[256,1024]{1,0:T(8,128)(2,1)S(1)}, bf16[256,1024]{1,0:T(8,128)(2,1)S(1)}, u32[]{:S(2)}, u32[]{:S(2)}) collective-permute-start(bf16[256,1024]{1,0:T(8,128)(2,1)S(1)} %pad_maximum_fusion.w0), channel_id=1, source_target_pairs={{0,32},{16,48},{32,0},{48,16},{1,33},{17,49},{33,1},{49,17},{2,34}... | collective-permute-start | bytes 1572872 | tf_op jit(solution)/shard_map/ppermute | solution.py:55
  20.2 29.5 %collective-permute-start.6 = (bf16[256,1024]{1,0:T(8,128)(2,1)S(1)}, bf16[256,1024]{1,0:T(8,128)(2,1)}, u32[]{:S(2)}, u32[]{:S(2)}) collective-permute-start(bf16[256,1024]{1,0:T(8,128)(2,1)S(1)} %pad_maximum_fusion.w0), channel_id=1, source_target_pairs={{0,16},{16,32},{32,48},{48,0},{1,17},{17,33},{33,49},{49,1},{2,18}... | collective-permute-start | bytes 1572872 | tf_op jit(solution)/shard_map/ppermute | solution.py:55
  25.9 41.7 %all-to-all-start = ((bf16[64,16,256]{2,1,0:T(8,128)(2,1)}), bf16[64,16,256]{2,1,0:T(8,128)(2,1)}, u32[]{:S(2)}, u32[]{:S(2)}) async-start(bf16[64,16,256]{2,1,0:T(8,128)(2,1)} %pad_maximum_fusion.1), calls=%async_computation | async-start | bytes 1048576 | tf_op jit(solution)/shard_map/all_to_all | solution.py:363
  36.2 11.0 %collective-permute-start = (bf16[128,1024]{1,0:T(8,128)(2,1)}, bf16[128,1024]{1,0:T(8,128)(2,1)}, u32[]{:S(2)}, u32[]{:S(2)}) collective-permute-start(bf16[128,1024]{1,0:T(8,128)(2,1)} %a0.1), channel_id=1, source_target_pairs={{0,64},{64,128},{128,192},{192,0},{1,65},{65,129},{129,193},{193,1... | collective-permute-start | bytes 786440 | tf_op jit(solution)/shard_map/ppermute | solution.py:55
  37.7 9.8 %collective-permute-start.2 = (bf16[128,1024]{1,0:T(8,128)(2,1)}, bf16[128,1024]{1,0:T(8,128)(2,1)}, u32[]{:S(2)}, u32[]{:S(2)}) collective-permute-start(bf16[128,1024]{1,0:T(8,128)(2,1)} %a0.1), channel_id=1, source_target_pairs={{0,192},{64,0},{128,64},{192,128},{1,193},{65,1},{129,65},{193,129... | collective-permute-start | bytes 786440 | tf_op jit(solution)/shard_map/ppermute | solution.py:55
  39.5 28.0 %copy-start.21 = (s32[128,3]{0,1:T(4,128)S(1)}, s32[128,3]{0,1:T(4,128)}, u32[]{:S(2)}) copy-start(s32[128,3]{0,1:T(4,128)} %param.23) | copy-start | bytes 4612
  50.6 47.1 %copy-start.23 = (f32[384]{0:T(512)S(1)}, f32[384]{0:T(512)}, u32[]{:S(2)}) copy-start(f32[384]{0:T(512)} %param.20) | copy-start | bytes 4612
  50.6 47.1 %copy-start.22 = (f32[768]{0:T(1024)S(1)}, f32[768]{0:T(1024)}, u32[]{:S(2)}) copy-start(f32[768]{0:T(1024)} %param.21) | copy-start | bytes 9220
  50.6 48.5 %copy-start.18 = (f32[1024]{0:T(1024)S(1)}, f32[1024]{0:T(1024)}, u32[]{:S(2)}) copy-start(f32[1024]{0:T(1024)} %param.22) | copy-start | bytes 12292
  53.4 45.7 %copy-start.3 = (bf16[768,1024]{1,0:T(8,128)(2,1)S(1)}, bf16[768,1024]{1,0:T(8,128)(2,1)}, u32[]{:S(2)}) copy-start(bf16[768,1024]{1,0:T(8,128)(2,1)} %head_b.3) | copy-start | bytes 4718596
  53.4 2.0 collective-permute-start.9
  56.8 13.1 %collective-permute-start.10 = (bf16[128,1024]{1,0:T(8,128)(2,1)}, bf16[128,1024]{1,0:T(8,128)(2,1)}, u32[]{:S(2)}, u32[]{:S(2)}) collective-permute-start(bf16[128,1024]{1,0:T(8,128)(2,1)} %get-tuple-element.65), channel_id=1, source_target_pairs={{0,0},{1,64},{2,128},{3,192},{64,1},{65,65},{66,129},{67,193},{128... | collective-permute-start | bytes 786440 | tf_op jit(solution)/shard_map/ppermute | solution.py:390
  60.4 34.0 %collective-permute-start.11 = (bf16[128,1024]{1,0:T(8,128)(2,1)}, bf16[128,1024]{1,0:T(8,128)(2,1)}, u32[]{:S(2)}, u32[]{:S(2)}) collective-permute-start(bf16[128,1024]{1,0:T(8,128)(2,1)} %get-tuple-element.66), channel_id=1, source_target_pairs={{0,128},{1,192},{2,0},{3,64},{64,129},{65,193},{66,1},{67,65},{128... | collective-permute-start | bytes 786440 | tf_op jit(solution)/shard_map/ppermute | solution.py:390
  67.6 31.5 %copy-start.4 = (bf16[384,1024]{1,0:T(8,128)(2,1)S(1)}, bf16[384,1024]{1,0:T(8,128)(2,1)}, u32[]{:S(2)}) copy-start(bf16[384,1024]{1,0:T(8,128)(2,1)} %head_s.3) | copy-start | bytes 2359300
  69.5 28.2 %collective-permute-start.15 = (bf16[128,640]{1,0:T(8,128)(2,1)S(1)}, bf16[128,640]{1,0:T(8,128)(2,1)S(1)}, u32[]{:S(2)}, u32[]{:S(2)}) collective-permute-start(bf16[128,640]{1,0:T(8,128)(2,1)S(1)} %get-tuple-element.68.own), channel_id=1, source_target_pairs={{0,2},{2,0},{1,3},{3,1},{4,6},{6,4},{5,7},{7,5},{8,10},{10,8},{9,1... | collective-permute-start | bytes 491528 | tf_op jit(solution)/shard_map/ppermute | solution.py:59
  69.6 28.2 %collective-permute-start.14 = (bf16[128,640]{1,0:T(8,128)(2,1)S(1)}, bf16[128,640]{1,0:T(8,128)(2,1)S(1)}, u32[]{:S(2)}, u32[]{:S(2)}) collective-permute-start(bf16[128,640]{1,0:T(8,128)(2,1)S(1)} %get-tuple-element.68.own), channel_id=1, source_target_pairs={{0,1},{1,0},{2,3},{3,2},{4,5},{5,4},{6,7},{7,6},{8,9},{9,8},{10,11... | collective-permute-start | bytes 491528 | tf_op jit(solution)/shard_map/ppermute | solution.py:59
  97.7 1.4 collective-permute-start.16
  99.1 1.6 copy-start.1
  100.7 15.9 %copy-start.2 = (bf16[1024,1024]{1,0:T(8,128)(2,1)S(1)}, bf16[1024,1024]{1,0:T(8,128)(2,1)}, u32[]{:S(2)}) copy-start(bf16[1024,1024]{1,0:T(8,128)(2,1)} %head_l.3) | copy-start | bytes 6291460
  100.7 15.9 %copy-start.19 = (f32[1024]{0:T(1024)S(1)}, f32[1024]{0:T(1024)}, u32[]{:S(2)}) copy-start(f32[1024]{0:T(1024)} %param.15) | copy-start | bytes 12292
  102.6 12.0 %collective-permute-start.17 = (bf16[544,128]{1,0:T(8,128)(2,1)S(1)}, bf16[544,128]{1,0:T(8,128)(2,1)S(1)}, u32[]{:S(2)}, u32[]{:S(2)}) collective-permute-start(bf16[544,128]{1,0:T(8,128)(2,1)S(1)} %get-tuple-element.72), channel_id=1, source_target_pairs={{0,64},{64,128},{128,192},{192,0},{1,65},{65,129},{129,193},{193,1... | collective-permute-start | bytes 417800 | tf_op jit(solution)/shard_map/ppermute | solution.py:55
  102.9 12.4 %collective-permute-start.18 = (bf16[544,128]{1,0:T(8,128)(2,1)S(1)}, bf16[544,128]{1,0:T(8,128)(2,1)S(1)}, u32[]{:S(2)}, u32[]{:S(2)}) collective-permute-start(bf16[544,128]{1,0:T(8,128)(2,1)S(1)} %get-tuple-element.73), channel_id=1, source_target_pairs={{0,128},{64,192},{128,0},{192,64},{1,129},{65,193},{129,1},{193,65... | collective-permute-start | bytes 417800 | tf_op jit(solution)/shard_map/ppermute | solution.py:55
  103.9 12.1 %collective-permute-start.19 = (bf16[544,128]{1,0:T(8,128)(2,1)S(1)}, bf16[544,128]{1,0:T(8,128)(2,1)S(1)}, u32[]{:S(2)}, u32[]{:S(2)}) collective-permute-start(bf16[544,128]{1,0:T(8,128)(2,1)S(1)} %get-tuple-element.74), channel_id=1, source_target_pairs={{0,192},{64,0},{128,64},{192,128},{1,193},{65,1},{129,65},{193,129... | collective-permute-start | bytes 417800 | tf_op jit(solution)/shard_map/ppermute | solution.py:55
  105.9 1.2 collective-permute-start.12
  107.1 7.5 %collective-permute-start.13 = (f32[8,128]{1,0:T(8,128)S(1)}, f32[8,128]{1,0:T(8,128)S(1)}, u32[]{:S(2)}, u32[]{:S(2)}) collective-permute-start(f32[8,128]{1,0:T(8,128)S(1)} %add.16), channel_id=1, source_target_pairs={{0,2},{2,0},{1,3},{3,1},{4,6},{6,4},{5,7},{7,5},{8,10},{10,8},{9,1... | collective-permute-start | bytes 12296 | tf_op jit(solution)/shard_map/ppermute | solution.py:59
  119.5 23.6 %copy-start.5 = (bf16[3,128,1024]{2,1,0:T(8,128)(2,1)}, bf16[3,128,1024]{2,1,0:T(8,128)(2,1)S(1)}, u32[]{:S(2)}) copy-start(bf16[3,128,1024]{2,1,0:T(8,128)(2,1)S(1)} %get-tuple-element.84.e0) | copy-start | bytes 2359300
  119.5 23.6 %collective-permute-start.25 = (bf16[3,128,1024]{2,1,0:T(8,128)(2,1)S(1)}, bf16[3,128,1024]{2,1,0:T(8,128)(2,1)S(1)}, u32[]{:S(2)}, u32[]{:S(2)}) collective-permute-start(bf16[3,128,1024]{2,1,0:T(8,128)(2,1)S(1)} %get-tuple-element.84.e0), channel_id=1, source_target_pairs={{0,192},{64,0},{128,64},{192,128},{1,193},{65,1},{129,65},{193,129... | collective-permute-start | bytes 2359304 | tf_op jit(solution)/shard_map/ppermute | solution.py:55
  120.7 22.5 %collective-permute-start.24 = (bf16[3,128,1024]{2,1,0:T(8,128)(2,1)S(1)}, bf16[3,128,1024]{2,1,0:T(8,128)(2,1)S(1)}, u32[]{:S(2)}, u32[]{:S(2)}) collective-permute-start(bf16[3,128,1024]{2,1,0:T(8,128)(2,1)S(1)} %get-tuple-element.84.e0), channel_id=1, source_target_pairs={{0,128},{64,192},{128,0},{192,64},{1,129},{65,193},{129,1},{193,65... | collective-permute-start | bytes 2359304 | tf_op jit(solution)/shard_map/ppermute | solution.py:55
  122.6 34.6 %collective-permute-start.23 = (bf16[3,128,1024]{2,1,0:T(8,128)(2,1)S(1)}, bf16[3,128,1024]{2,1,0:T(8,128)(2,1)S(1)}, u32[]{:S(2)}, u32[]{:S(2)}) collective-permute-start(bf16[3,128,1024]{2,1,0:T(8,128)(2,1)S(1)} %get-tuple-element.84.e0), channel_id=1, source_target_pairs={{0,64},{64,128},{128,192},{192,0},{1,65},{65,129},{129,193},{193,1... | collective-permute-start | bytes 2359304 | tf_op jit(solution)/shard_map/ppermute | solution.py:55
  123.9 1.6 collective-permute-start.20
  126.4 10.2 %collective-permute-start.21 = (bf16[128,640]{1,0:T(8,128)(2,1)S(1)}, bf16[128,640]{1,0:T(8,128)(2,1)S(1)}, u32[]{:S(2)}, u32[]{:S(2)}) collective-permute-start(bf16[128,640]{1,0:T(8,128)(2,1)S(1)} %get-tuple-element.88), channel_id=1, source_target_pairs={{0,2},{2,0},{1,3},{3,1},{4,6},{6,4},{5,7},{7,5},{8,10},{10,8},{9,1... | collective-permute-start | bytes 491528 | tf_op jit(solution)/shard_map/ppermute | solution.py:59
  137.3 28.3 %copy-start.13 = (bf16[544,128]{1,0:T(8,128)(2,1)S(1)}, bf16[544,128]{1,0:T(8,128)(2,1)}, u32[]{:S(2)}) copy-start(bf16[544,128]{1,0:T(8,128)(2,1)} %copy-done.12) | copy-start | bytes 417796
  137.3 3.6 %collective-permute-start.22 = (f32[8,128]{1,0:T(8,128)S(1)}, f32[8,128]{1,0:T(8,128)S(1)}, u32[]{:S(2)}, u32[]{:S(2)}) collective-permute-start(f32[8,128]{1,0:T(8,128)S(1)} %shard_map.186.piece), channel_id=1, source_target_pairs={{0,4},{4,0},{8,12},{12,8},{1,5},{5,1},{9,13},{13,9},{2,6},{6,2},{1... | collective-permute-start | bytes 12296 | tf_op jit(solution)/shard_map/ppermute | solution.py:434
  158.1 37.0 %all-to-all-start.1 = ((bf16[64,16,256]{2,1,0:T(8,128)(2,1)}), bf16[64,16,256]{2,1,0:T(8,128)(2,1)S(1)}, u32[]{:S(2)}, u32[]{:S(2)}) async-start(bf16[64,16,256]{2,1,0:T(8,128)(2,1)} %bitcast.10), calls=%async_computation.1 | async-start | bytes 1048576 | tf_op jit(solution)/shard_map/all_to_all | solution.py:443
  165.7 1.1 copy-start.6
  166.8 1.1 copy-start.8
  172.4 11.9 %collective-permute-start.26 = (bf16[144,1024]{1,0:T(8,128)(2,1)S(1)}, bf16[144,1024]{1,0:T(8,128)(2,1)S(1)}, u32[]{:S(2)}, u32[]{:S(2)}) collective-permute-start(bf16[144,1024]{1,0:T(8,128)(2,1)S(1)} %get-tuple-element.95), channel_id=1, source_target_pairs={{0,16},{16,32},{32,48},{48,0},{1,17},{17,33},{33,49},{49,1},{2,18}... | collective-permute-start | bytes 884744 | tf_op jit(solution)/shard_map/ppermute | solution.py:55
  174.0 16.2 %collective-permute-start.27 = (bf16[144,1024]{1,0:T(8,128)(2,1)S(1)}, bf16[144,1024]{1,0:T(8,128)(2,1)S(1)}, u32[]{:S(2)}, u32[]{:S(2)}) collective-permute-start(bf16[144,1024]{1,0:T(8,128)(2,1)S(1)} %get-tuple-element.96), channel_id=1, source_target_pairs={{0,32},{16,48},{32,0},{48,16},{1,33},{17,49},{33,1},{49,17},{2,34}... | collective-permute-start | bytes 884744 | tf_op jit(solution)/shard_map/ppermute | solution.py:55
  176.6 13.6 %collective-permute-start.28 = (bf16[144,1024]{1,0:T(8,128)(2,1)S(1)}, bf16[144,1024]{1,0:T(8,128)(2,1)S(1)}, u32[]{:S(2)}, u32[]{:S(2)}) collective-permute-start(bf16[144,1024]{1,0:T(8,128)(2,1)S(1)} %get-tuple-element.97), channel_id=1, source_target_pairs={{0,48},{16,0},{32,16},{48,32},{1,49},{17,1},{33,17},{49,33},{2,50}... | collective-permute-start | bytes 884744 | tf_op jit(solution)/shard_map/ppermute | solution.py:55
  191.1 7.9 %collective-permute-start.29 = (bf16[48,1024]{1,0:T(8,128)(2,1)S(1)}, bf16[48,1024]{1,0:T(8,128)(2,1)S(1)}, u32[]{:S(2)}, u32[]{:S(2)}) collective-permute-start(bf16[48,1024]{1,0:T(8,128)(2,1)S(1)} %get-tuple-element.99), channel_id=1, source_target_pairs={{0,4},{4,8},{8,12},{12,0},{1,5},{5,9},{9,13},{13,1},{2,6},{6,10},{... | collective-permute-start | bytes 294920 | tf_op jit(solution)/shard_map/ppermute | solution.py:55
  192.6 7.4 %collective-permute-start.30 = (bf16[48,1024]{1,0:T(8,128)(2,1)S(1)}, bf16[48,1024]{1,0:T(8,128)(2,1)S(1)}, u32[]{:S(2)}, u32[]{:S(2)}) collective-permute-start(bf16[48,1024]{1,0:T(8,128)(2,1)S(1)} %get-tuple-element.100), channel_id=1, source_target_pairs={{0,8},{4,12},{8,0},{12,4},{1,9},{5,13},{9,1},{13,5},{2,10},{6,14},... | collective-permute-start | bytes 294920 | tf_op jit(solution)/shard_map/ppermute | solution.py:55
  194.1 7.7 %collective-permute-start.31 = (bf16[48,1024]{1,0:T(8,128)(2,1)S(1)}, bf16[48,1024]{1,0:T(8,128)(2,1)S(1)}, u32[]{:S(2)}, u32[]{:S(2)}) collective-permute-start(bf16[48,1024]{1,0:T(8,128)(2,1)S(1)} %get-tuple-element.101), channel_id=1, source_target_pairs={{0,12},{4,0},{8,4},{12,8},{1,13},{5,1},{9,5},{13,9},{2,14},{6,2},{... | collective-permute-start | bytes 294920 | tf_op jit(solution)/shard_map/ppermute | solution.py:55
  (10 other events, 8.6 us)

commit v5 on v3

--- a/solution.py
+++ b/solution.py
@@ -375,7 +375,7 @@
         [((2, ROWS, 1024), BF16)] * 2,
         pos, *rows, *weights,
         scratch=[((512, 1024), BF16), ((1024, 1024), BF16)],
-        flops=2 * 512 * 1024 * 1024, moved=5 << 20, room=16,
+        flops=2 * 512 * 1024 * 1024, moved=5 << 20, room=13,
     )
     first, second = call(
         pair_kernel, [((ROWS, 1024), BF16)] * 2, pos, mine, swapped(other, "c"), moved=2 << 20
@@ -405,7 +405,7 @@
         + [((544, ROWS), BF16)] * 4,
         pos, block, block_c, block_z, block_zc, *gains, *heads,
         scratch=[((4, ROWS, BLOCK), BF16), ((4, 544, ROWS), BF16)],
-        flops=2 * 128 * 2176 * 1024, moved=9 << 20, room=20,
+        flops=2 * 128 * 2176 * 1024, moved=9 << 20, room=16,
     )
     sums = sums + swapped(sums, "c")
     sums = sums + swapped(sums, "zh")
@@ -418,7 +418,7 @@
         pos, hidden, sums, teacher_gain[None, :], outs, token_weights, xhat,
         *gains, *heads,
         scratch=[((4, ROWS, BLOCK), F32)],
-        flops=4 * 128 * 2176 * 1024, moved=15 << 20, room=28,
+        flops=4 * 128 * 2176 * 1024, moved=15 << 20, room=20,
     )
     errors = [errors] + [shifted(errors, "y", s) for s in (1, 2, 3)]
 
@@ -451,7 +451,7 @@
         grads_kernel,
         [((136, 1024), F32)] + [((144, 1024), BF16)] * 3,
         pos, *lines, *errors,
-        scratch=[((544, 1024), F32)], flops=2 * 512 * 544 * 1024, moved=5 << 20, room=16,
+        scratch=[((544, 1024), F32)], flops=2 * 512 * 544 * 1024, moved=5 << 20, room=14,
     )
     keep, *sent = call(
         third_kernel,

time: 198 us -> 200 us (1.010)
  no operation moved by 1% of the time
where the time goes in v5:
time: 200 us; the launch traced here: 199 us
  waiting for transfers between devices  87.7 us (44%)
  starting transfers between devices  72.6 us (36%)
  Pallas kernels  22.4 us (11%)
  local copies, waits for them, and re-layouts  11.3 us (6%)
  other arithmetic  3.73 us (2%)
    ppermute x21, waiting for transfers between devices, shifted(): return lax.ppermute(value, axis, [(i, (i + step) % 4) for i in range(4)])  46.7 us
    ppermute x21, starting transfers between devices, shifted(): return lax.ppermute(value, axis, [(i, (i + step) % 4) for i in range(4)])  33.4 us
    ppermute x2, waiting for transfers between devices, per_device(): parts.append(lax.ppermute(value, ('y', 'zh', 'c'), links))  24.6 us
    pallas_call x13, Pallas kernels, call(): pl.pallas_call(body, out_shape=[jax.ShapeDtypeStruct(shape, dtype) for sh...  22.4 us
    ppermute x8, waiting for transfers between devices, swapped(): return lax.ppermute(value, axis, SWAP)  12.8 us
    ppermute x2, starting transfers between devices, per_device(): parts.append(lax.ppermute(value, ('y', 'zh', 'c'), links))  10.7 us
    ppermute x8, starting transfers between devices, swapped(): return lax.ppermute(value, axis, SWAP)  10.4 us
    all_to_all x1, starting transfers between devices, per_device(): lax.all_to_all(sent, ('y', 'x', 'zl'), 0, 0, tiled=True)  10.3 us
  transfers between devices with their start and end apart: 34, of which 18 were waited for; matrix products, arithmetic and copies ran while one was open for 4% of the time, Pallas kernels for 8%

profile of v5, /device:TPU:32, one launch (start us, length us, event | category | flops | bytes accessed | tf_op | source)
XLA Modules:
  0.0 198.6 jit_solution(716917648225591773)
XLA Ops:
  0.6 1.9 collective-permute-start.5
  2.6 1.5 collective-permute-start.4
  4.1 2.8 %collective-permute-start.3 = (bf16[64,1024]{1,0:T(8,128)(2,1)}, bf16[64,1024]{1,0:T(8,128)(2,1)S(1)}, u32[]{:S(2)}, u32[]{:S(2)}) collective-permute-start(bf16[64,1024]{1,0:T(8,128)(2,1)} %bitcast.25), channel_id=1, source_target_pairs={{0,4},{4,8},{8,12},{12,0},{1,5},{5,9},{9,13},{13,1},{2,6},{6,10},{... | collective-permute-start | bytes 393224 | tf_op jit(solution)/shard_map/ppermute | solution.py:55
  6.9 3.2 %collective-permute-start.1 = (bf16[128,1024]{1,0:T(8,128)(2,1)}, bf16[128,1024]{1,0:T(8,128)(2,1)}, u32[]{:S(2)}, u32[]{:S(2)}) collective-permute-start(bf16[128,1024]{1,0:T(8,128)(2,1)} %a0.1), channel_id=1, source_target_pairs={{0,128},{64,192},{128,0},{192,64},{1,129},{65,193},{129,1},{193,65... | collective-permute-start | bytes 786440 | tf_op jit(solution)/shard_map/ppermute | solution.py:55
  11.0 2.7 %collective-permute-done.4 = bf16[64,1024]{1,0:T(8,128)(2,1)S(1)} collective-permute-done((bf16[64,1024]{1,0:T(8,128)(2,1)}, bf16[64,1024]{1,0:T(8,128)(2,1)S(1)}, u32[]{:S(2)}, u32[]{:S(2)}) %collective-permute-start.4) | collective-permute-done | bytes 131104 | tf_op jit(solution)/shard_map/ppermute | solution.py:55
  13.7 1.9 collective-permute-done.3
  16.6 2.8 %collective-permute-start.8 = (bf16[256,1024]{1,0:T(8,128)(2,1)S(1)}, bf16[256,1024]{1,0:T(8,128)(2,1)S(1)}, u32[]{:S(2)}, u32[]{:S(2)}) collective-permute-start(bf16[256,1024]{1,0:T(8,128)(2,1)S(1)} %pad_maximum_fusion.w0), channel_id=1, source_target_pairs={{0,48},{16,0},{32,16},{48,32},{1,49},{17,1},{33,17},{49,33},{2,50}... | collective-permute-start | bytes 1572872 | tf_op jit(solution)/shard_map/ppermute | solution.py:55
  21.9 2.0 reshape.35
  23.9 2.0 %pad_maximum_fusion.1 = bf16[64,16,256]{2,1,0:T(8,128)(2,1)} fusion(bf16[64,2,256]{2,1,0:T(2,128)(2,1)S(1)} %broadcast_in_dim.20, bf16[64,14,256]{2,1,0:T(8,128)(2,1)} %reshape.35), kind=kLoop, calls=%fused_computation.1 | loop fusion | flops 1048576 | bytes 1048576 | tf_op jit(solution)/shard_map/concatenate | solution.py:362
  25.9 10.3 %all-to-all-start = ((bf16[64,16,256]{2,1,0:T(8,128)(2,1)}), bf16[64,16,256]{2,1,0:T(8,128)(2,1)}, u32[]{:S(2)}, u32[]{:S(2)}) async-start(bf16[64,16,256]{2,1,0:T(8,128)(2,1)} %pad_maximum_fusion.1), calls=%async_computation | async-start | bytes 1048576 | tf_op jit(solution)/shard_map/all_to_all | solution.py:363
  36.2 1.5 collective-permute-start
  37.8 1.8 collective-permute-start.2
  39.6 7.5 %collective-permute-done.a1 = bf16[128,1024]{1,0:T(8,128)(2,1)} collective-permute-done((bf16[128,1024]{1,0:T(8,128)(2,1)}, bf16[128,1024]{1,0:T(8,128)(2,1)}, u32[]{:S(2)}, u32[]{:S(2)}) %collective-permute-start) | collective-permute-done | bytes 262176 | tf_op jit(solution)/shard_map/ppermute | solution.py:55
  47.6 2.1 %collective-permute-done.6.w1 = bf16[256,1024]{1,0:T(8,128)(2,1)} collective-permute-done((bf16[256,1024]{1,0:T(8,128)(2,1)S(1)}, bf16[256,1024]{1,0:T(8,128)(2,1)}, u32[]{:S(2)}, u32[]{:S(2)}) %collective-permute-start.6) | collective-permute-done | bytes 524320 | tf_op jit(solution)/shard_map/ppermute | solution.py:55
  50.6 2.8 %shard_map.179 = (bf16[2,128,1024]{2,1,0:T(8,128)(2,1)S(1)}, bf16[2,128,1024]{2,1,0:T(8,128)(2,1)S(1)}) custom-call(s32[5]{0:T(128)S(1)} %stack.23.pos, bf16[128,1024]{1,0:T(8,128)(2,1)S(1)} %copy-done.14, bf16[128,1024]{1,0:T(8,128)(2,1)} %collective-permute-done.a1, bf16[128,1024]{1,0:T(8,128)(2,1)} %collective-permute-done.1.a2, ...), custom_call_target="tpu_custom_call" | custom-call | flops 1073741824 | bytes 5242880 | tf_op jit(solution)/shard_map/pallas_call | solution.py:35
  53.5 1.9 collective-permute-done.9.got
  55.4 1.4 shard_map.180
  56.8 3.6 %collective-permute-start.10 = (bf16[128,1024]{1,0:T(8,128)(2,1)}, bf16[128,1024]{1,0:T(8,128)(2,1)}, u32[]{:S(2)}, u32[]{:S(2)}) collective-permute-start(bf16[128,1024]{1,0:T(8,128)(2,1)} %get-tuple-element.61), channel_id=1, source_target_pairs={{0,0},{1,64},{2,128},{3,192},{64,1},{65,65},{66,129},{67,193},{128... | collective-permute-start | bytes 786440 | tf_op jit(solution)/shard_map/ppermute | solution.py:390
  60.4 7.1 %collective-permute-start.11 = (bf16[128,1024]{1,0:T(8,128)(2,1)}, bf16[128,1024]{1,0:T(8,128)(2,1)}, u32[]{:S(2)}, u32[]{:S(2)}) collective-permute-start(bf16[128,1024]{1,0:T(8,128)(2,1)} %get-tuple-element.62), channel_id=1, source_target_pairs={{0,128},{1,192},{2,0},{3,64},{64,129},{65,193},{66,1},{67,65},{128... | collective-permute-start | bytes 786440 | tf_op jit(solution)/shard_map/ppermute | solution.py:390
  67.7 1.8 shard_map.182
  69.9 24.6 %collective-permute-done.11.second = bf16[128,1024]{1,0:T(8,128)(2,1)} collective-permute-done((bf16[128,1024]{1,0:T(8,128)(2,1)}, bf16[128,1024]{1,0:T(8,128)(2,1)}, u32[]{:S(2)}, u32[]{:S(2)}) %collective-permute-start.11) | collective-permute-done | bytes 262176 | tf_op jit(solution)/shard_map/ppermute | solution.py:390
  95.4 1.3 shard_map.181
  97.8 1.4 collective-permute-done.16.own_zc
  99.2 1.6 copy-done.1
  100.7 1.9 shard_map.183
  103.9 2.1 %collective-permute-start.19 = (bf16[544,128]{1,0:T(8,128)(2,1)S(1)}, bf16[544,128]{1,0:T(8,128)(2,1)S(1)}, u32[]{:S(2)}, u32[]{:S(2)}) collective-permute-start(bf16[544,128]{1,0:T(8,128)(2,1)S(1)} %get-tuple-element.70), channel_id=1, source_target_pairs={{0,192},{64,0},{128,64},{192,128},{1,193},{65,1},{129,65},{193,129... | collective-permute-start | bytes 417800 | tf_op jit(solution)/shard_map/ppermute | solution.py:55
  106.0 1.2 collective-permute-done.12
  107.2 5.8 %collective-permute-start.13 = (f32[8,128]{1,0:T(8,128)S(1)}, f32[8,128]{1,0:T(8,128)S(1)}, u32[]{:S(2)}, u32[]{:S(2)}) collective-permute-start(f32[8,128]{1,0:T(8,128)S(1)} %add.16), channel_id=1, source_target_pairs={{0,2},{2,0},{1,3},{3,1},{4,6},{6,4},{5,7},{7,5},{8,10},{10,8},{9,1... | collective-permute-start | bytes 12296 | tf_op jit(solution)/shard_map/ppermute | solution.py:59
  113.0 1.7 collective-permute-done.13
  116.7 3.4 %shard_map.184 = (bf16[3,128,1024]{2,1,0:T(8,128)(2,1)}, f32[2,128,640]{2,1,0:T(8,128)S(1)}, bf16[2,128,640]{2,1,0:T(8,128)(2,1)S(1)}) custom-call(s32[5]{0:T(128)S(1)} %stack.23.pos, f32[128,1024]{1,0:T(8,128)S(1)} %get-tuple-element.75.hidden, f32[8,128]{1,0:T(8,128)S(1)} %add.17.sums, f32[1,1024]{1,0:T(1,128)S(1)} %bitcast.22, ...), custom_call_target="tpu_custom_call" | custom-call | flops 1140850688 | bytes 15728640 | tf_op jit(solution)/shard_map/pallas_call | solution.py:35
  120.0 1.1 collective-permute-start.22
  121.1 1.8 collective-permute-start.21
  123.0 1.4 collective-permute-start.20
  125.2 4.1 %collective-permute-start.30 = (bf16[128,640]{1,0:T(8,128)(2,1)S(1)}, bf16[128,640]{1,0:T(8,128)(2,1)S(1)}, u32[]{:S(2)}, u32[]{:S(2)}) collective-permute-start(bf16[128,640]{1,0:T(8,128)(2,1)S(1)} %get-tuple-element.92), channel_id=1, source_target_pairs={{0,2},{2,0},{1,3},{3,1},{4,6},{6,4},{5,7},{7,5},{8,10},{10,8},{9,1... | collective-permute-start | bytes 491528 | tf_op jit(solution)/shard_map/ppermute | solution.py:59
  129.3 5.7 %collective-permute-done.30.got = bf16[128,640]{1,0:T(8,128)(2,1)S(1)} collective-permute-done((bf16[128,640]{1,0:T(8,128)(2,1)S(1)}, bf16[128,640]{1,0:T(8,128)(2,1)S(1)}, u32[]{:S(2)}, u32[]{:S(2)}) %collective-permute-start.30) | collective-permute-done | bytes 163872 | tf_op jit(solution)/shard_map/ppermute | solution.py:59
  135.7 3.6 %collective-permute-done.31.piece_z = f32[8,128]{1,0:T(8,128)S(1)} collective-permute-done((f32[8,128]{1,0:T(8,128)S(1)}, f32[8,128]{1,0:T(8,128)S(1)}, u32[]{:S(2)}, u32[]{:S(2)}) %collective-permute-start.31) | collective-permute-done | bytes 4128 | tf_op jit(solution)/shard_map/ppermute | solution.py:434
  139.3 2.2 %shard_map.189 = bf16[1024,256]{1,0:T(8,128)(2,1)} custom-call(s32[5]{0:T(128)S(1)} %stack.23.pos, f32[128,640]{1,0:T(8,128)S(1)} %get-tuple-element.91.keep, bf16[128,640]{1,0:T(8,128)(2,1)S(1)} %collective-permute-done.30.got, f32[4,128,640]{2,1,0:T(8,128)S(1)} %get-tuple-element.79.xhat, f32[128,384]{1,0:T(8,128)S(1)} %get-tuple-element.93.scales, ...), custom_call_target="tpu_custom_call" | custom-call | flops 201326592 | bytes 2097152 | tf_op jit(solution)/shard_map/pallas_call | solution.py:35
  141.5 7.7 %all-to-all-start.1 = ((bf16[64,16,256]{2,1,0:T(8,128)(2,1)}), bf16[64,16,256]{2,1,0:T(8,128)(2,1)S(1)}, u32[]{:S(2)}, u32[]{:S(2)}) async-start(bf16[64,16,256]{2,1,0:T(8,128)(2,1)} %bitcast.10), calls=%async_computation.1 | async-start | bytes 1048576 | tf_op jit(solution)/shard_map/all_to_all | solution.py:442
  149.3 15.6 %collective-permute-done.20.e1 = bf16[3,128,1024]{2,1,0:T(8,128)(2,1)} collective-permute-done((bf16[3,128,1024]{2,1,0:T(8,128)(2,1)}, bf16[3,128,1024]{2,1,0:T(8,128)(2,1)}, u32[]{:S(2)}, u32[]{:S(2)}) %collective-permute-start.20) | collective-permute-done | bytes 786464 | tf_op jit(solution)/shard_map/ppermute | solution.py:55
  166.6 2.6 %shard_map.185 = (f32[136,1024]{1,0:T(8,128)S(1)}, bf16[144,1024]{1,0:T(8,128)(2,1)S(1)}, bf16[144,1024]{1,0:T(8,128)(2,1)S(1)}, bf16[144,1024]{1,0:T(8,128)(2,1)S(1)}) custom-call(s32[5]{0:T(128)S(1)} %stack.23.pos, bf16[544,128]{1,0:T(8,128)(2,1)S(1)} %get-tuple-element.71.n0, bf16[544,128]{1,0:T(8,128)(2,1)S(1)} %copy-done.7, ...), custom_call_target="tpu_custom_call" | custom-call | flops 570425344 | bytes 5242880 | tf_op jit(solution)/shard_map/pallas_call | solution.py:35
  169.5 2.4 %collective-permute-start.24 = (bf16[144,1024]{1,0:T(8,128)(2,1)S(1)}, bf16[144,1024]{1,0:T(8,128)(2,1)S(1)}, u32[]{:S(2)}, u32[]{:S(2)}) collective-permute-start(bf16[144,1024]{1,0:T(8,128)(2,1)S(1)} %get-tuple-element.83), channel_id=1, source_target_pairs={{0,32},{16,48},{32,0},{48,16},{1,33},{17,49},{33,1},{49,17},{2,34}... | collective-permute-start | bytes 884744 | tf_op jit(solution)/shard_map/ppermute | solution.py:55
  171.9 1.6 collective-permute-start.25
  173.5 12.3 %collective-permute-done.23.p1 = bf16[144,1024]{1,0:T(8,128)(2,1)S(1)} collective-permute-done((bf16[144,1024]{1,0:T(8,128)(2,1)S(1)}, bf16[144,1024]{1,0:T(8,128)(2,1)S(1)}, u32[]{:S(2)}, u32[]{:S(2)}) %collective-permute-start.23) | collective-permute-done | bytes 294944 | tf_op jit(solution)/shard_map/ppermute | solution.py:55
  187.3 2.7 %collective-permute-start.26 = (bf16[48,1024]{1,0:T(8,128)(2,1)S(1)}, bf16[48,1024]{1,0:T(8,128)(2,1)S(1)}, u32[]{:S(2)}, u32[]{:S(2)}) collective-permute-start(bf16[48,1024]{1,0:T(8,128)(2,1)S(1)} %get-tuple-element.86), channel_id=1, source_target_pairs={{0,4},{4,8},{8,12},{12,0},{1,5},{5,9},{9,13},{13,1},{2,6},{6,10},{... | collective-permute-start | bytes 294920 | tf_op jit(solution)/shard_map/ppermute | solution.py:55
  190.0 1.6 collective-permute-start.28
  191.5 1.4 shard_map.190
  193.8 2.5 %collective-permute-done.26.m1 = bf16[48,1024]{1,0:T(8,128)(2,1)S(1)} collective-permute-done((bf16[48,1024]{1,0:T(8,128)(2,1)S(1)}, bf16[48,1024]{1,0:T(8,128)(2,1)S(1)}, u32[]{:S(2)}, u32[]{:S(2)}) %collective-permute-start.26) | collective-permute-done | bytes 98336 | tf_op jit(solution)/shard_map/ppermute | solution.py:55
  197.4 1.2 shard_map.191
  (85 shorter events, 18.7 us)
Async XLA Ops:
  0.6 20.5 %copy-start = (bf16[896,1024]{1,0:T(8,128)(2,1)S(1)}, bf16[896,1024]{1,0:T(8,128)(2,1)}, u32[]{:S(2)}) copy-start(bf16[896,1024]{1,0:T(8,128)(2,1)} %param.16) | copy-start | bytes 5505028
  0.6 10.3 %collective-permute-start.5 = (bf16[64,1024]{1,0:T(8,128)(2,1)}, bf16[64,1024]{1,0:T(8,128)(2,1)S(1)}, u32[]{:S(2)}, u32[]{:S(2)}) collective-permute-start(bf16[64,1024]{1,0:T(8,128)(2,1)} %bitcast.23), channel_id=1, source_target_pairs={{0,12},{4,0},{8,4},{12,8},{1,13},{5,1},{9,5},{13,9},{2,14},{6,2},{... | collective-permute-start | bytes 393224 | tf_op jit(solution)/shard_map/ppermute | solution.py:55
  2.6 11.1 %collective-permute-start.4 = (bf16[64,1024]{1,0:T(8,128)(2,1)}, bf16[64,1024]{1,0:T(8,128)(2,1)S(1)}, u32[]{:S(2)}, u32[]{:S(2)}) collective-permute-start(bf16[64,1024]{1,0:T(8,128)(2,1)} %bitcast.24), channel_id=1, source_target_pairs={{0,8},{4,12},{8,0},{12,4},{1,9},{5,13},{9,1},{13,5},{2,10},{6,14},... | collective-permute-start | bytes 393224 | tf_op jit(solution)/shard_map/ppermute | solution.py:55
  4.1 11.5 %collective-permute-start.3 = (bf16[64,1024]{1,0:T(8,128)(2,1)}, bf16[64,1024]{1,0:T(8,128)(2,1)S(1)}, u32[]{:S(2)}, u32[]{:S(2)}) collective-permute-start(bf16[64,1024]{1,0:T(8,128)(2,1)} %bitcast.25), channel_id=1, source_target_pairs={{0,4},{4,8},{8,12},{12,0},{1,5},{5,9},{9,13},{13,1},{2,6},{6,10},{... | collective-permute-start | bytes 393224 | tf_op jit(solution)/shard_map/ppermute | solution.py:55
  6.9 30.8 %collective-permute-start.1 = (bf16[128,1024]{1,0:T(8,128)(2,1)}, bf16[128,1024]{1,0:T(8,128)(2,1)}, u32[]{:S(2)}, u32[]{:S(2)}) collective-permute-start(bf16[128,1024]{1,0:T(8,128)(2,1)} %a0.1), channel_id=1, source_target_pairs={{0,128},{64,192},{128,0},{192,64},{1,129},{65,193},{129,1},{193,65... | collective-permute-start | bytes 786440 | tf_op jit(solution)/shard_map/ppermute | solution.py:55
  16.6 31.0 %collective-permute-start.8 = (bf16[256,1024]{1,0:T(8,128)(2,1)S(1)}, bf16[256,1024]{1,0:T(8,128)(2,1)S(1)}, u32[]{:S(2)}, u32[]{:S(2)}) collective-permute-start(bf16[256,1024]{1,0:T(8,128)(2,1)S(1)} %pad_maximum_fusion.w0), channel_id=1, source_target_pairs={{0,48},{16,0},{32,16},{48,32},{1,49},{17,1},{33,17},{49,33},{2,50}... | collective-permute-start | bytes 1572872 | tf_op jit(solution)/shard_map/ppermute | solution.py:55
  19.4 28.2 %collective-permute-start.7 = (bf16[256,1024]{1,0:T(8,128)(2,1)S(1)}, bf16[256,1024]{1,0:T(8,128)(2,1)S(1)}, u32[]{:S(2)}, u32[]{:S(2)}) collective-permute-start(bf16[256,1024]{1,0:T(8,128)(2,1)S(1)} %pad_maximum_fusion.w0), channel_id=1, source_target_pairs={{0,32},{16,48},{32,0},{48,16},{1,33},{17,49},{33,1},{49,17},{2,34}... | collective-permute-start | bytes 1572872 | tf_op jit(solution)/shard_map/ppermute | solution.py:55
  20.2 29.5 %collective-permute-start.6 = (bf16[256,1024]{1,0:T(8,128)(2,1)S(1)}, bf16[256,1024]{1,0:T(8,128)(2,1)}, u32[]{:S(2)}, u32[]{:S(2)}) collective-permute-start(bf16[256,1024]{1,0:T(8,128)(2,1)S(1)} %pad_maximum_fusion.w0), channel_id=1, source_target_pairs={{0,16},{16,32},{32,48},{48,0},{1,17},{17,33},{33,49},{49,1},{2,18}... | collective-permute-start | bytes 1572872 | tf_op jit(solution)/shard_map/ppermute | solution.py:55
  25.9 41.7 %all-to-all-start = ((bf16[64,16,256]{2,1,0:T(8,128)(2,1)}), bf16[64,16,256]{2,1,0:T(8,128)(2,1)}, u32[]{:S(2)}, u32[]{:S(2)}) async-start(bf16[64,16,256]{2,1,0:T(8,128)(2,1)} %pad_maximum_fusion.1), calls=%async_computation | async-start | bytes 1048576 | tf_op jit(solution)/shard_map/all_to_all | solution.py:363
  36.2 10.9 %collective-permute-start = (bf16[128,1024]{1,0:T(8,128)(2,1)}, bf16[128,1024]{1,0:T(8,128)(2,1)}, u32[]{:S(2)}, u32[]{:S(2)}) collective-permute-start(bf16[128,1024]{1,0:T(8,128)(2,1)} %a0.1), channel_id=1, source_target_pairs={{0,64},{64,128},{128,192},{192,0},{1,65},{65,129},{129,193},{193,1... | collective-permute-start | bytes 786440 | tf_op jit(solution)/shard_map/ppermute | solution.py:55
  37.8 9.8 %collective-permute-start.2 = (bf16[128,1024]{1,0:T(8,128)(2,1)}, bf16[128,1024]{1,0:T(8,128)(2,1)}, u32[]{:S(2)}, u32[]{:S(2)}) collective-permute-start(bf16[128,1024]{1,0:T(8,128)(2,1)} %a0.1), channel_id=1, source_target_pairs={{0,192},{64,0},{128,64},{192,128},{1,193},{65,1},{129,65},{193,129... | collective-permute-start | bytes 786440 | tf_op jit(solution)/shard_map/ppermute | solution.py:55
  39.5 28.0 %copy-start.15 = (s32[128,3]{0,1:T(4,128)S(1)}, s32[128,3]{0,1:T(4,128)}, u32[]{:S(2)}) copy-start(s32[128,3]{0,1:T(4,128)} %param.23) | copy-start | bytes 4612
  49.6 1.0 copy-start.14
  50.6 47.1 %copy-start.17 = (f32[384]{0:T(512)S(1)}, f32[384]{0:T(512)}, u32[]{:S(2)}) copy-start(f32[384]{0:T(512)} %param.20) | copy-start | bytes 4612
  50.6 47.2 %copy-start.16 = (f32[768]{0:T(1024)S(1)}, f32[768]{0:T(1024)}, u32[]{:S(2)}) copy-start(f32[768]{0:T(1024)} %param.21) | copy-start | bytes 9220
  50.6 48.5 %copy-start.12 = (f32[1024]{0:T(1024)S(1)}, f32[1024]{0:T(1024)}, u32[]{:S(2)}) copy-start(f32[1024]{0:T(1024)} %param.22) | copy-start | bytes 12292
  53.4 45.8 %copy-start.3 = (bf16[768,1024]{1,0:T(8,128)(2,1)S(1)}, bf16[768,1024]{1,0:T(8,128)(2,1)}, u32[]{:S(2)}) copy-start(bf16[768,1024]{1,0:T(8,128)(2,1)} %head_b.3) | copy-start | bytes 4718596
  53.4 2.0 %collective-permute-start.9 = (bf16[2,128,1024]{2,1,0:T(8,128)(2,1)S(1)}, bf16[2,128,1024]{2,1,0:T(8,128)(2,1)S(1)}, u32[]{:S(2)}, u32[]{:S(2)}) collective-permute-start(bf16[2,128,1024]{2,1,0:T(8,128)(2,1)S(1)} %get-tuple-element.60), channel_id=1, source_target_pairs={{0,1},{1,0},{2,3},{3,2},{4,5},{5,4},{6,7},{7,6},{8,9},{9,8},{10,11... | collective-permute-start | bytes 1572872 | tf_op jit(solution)/shard_map/ppermute | solution.py:59
  56.8 13.1 %collective-permute-start.10 = (bf16[128,1024]{1,0:T(8,128)(2,1)}, bf16[128,1024]{1,0:T(8,128)(2,1)}, u32[]{:S(2)}, u32[]{:S(2)}) collective-permute-start(bf16[128,1024]{1,0:T(8,128)(2,1)} %get-tuple-element.61), channel_id=1, source_target_pairs={{0,0},{1,64},{2,128},{3,192},{64,1},{65,65},{66,129},{67,193},{128... | collective-permute-start | bytes 786440 | tf_op jit(solution)/shard_map/ppermute | solution.py:390
  60.4 34.1 %collective-permute-start.11 = (bf16[128,1024]{1,0:T(8,128)(2,1)}, bf16[128,1024]{1,0:T(8,128)(2,1)}, u32[]{:S(2)}, u32[]{:S(2)}) collective-permute-start(bf16[128,1024]{1,0:T(8,128)(2,1)} %get-tuple-element.62), channel_id=1, source_target_pairs={{0,128},{1,192},{2,0},{3,64},{64,129},{65,193},{66,1},{67,65},{128... | collective-permute-start | bytes 786440 | tf_op jit(solution)/shard_map/ppermute | solution.py:390
  67.6 31.5 %copy-start.4 = (bf16[384,1024]{1,0:T(8,128)(2,1)S(1)}, bf16[384,1024]{1,0:T(8,128)(2,1)}, u32[]{:S(2)}) copy-start(bf16[384,1024]{1,0:T(8,128)(2,1)} %head_s.3) | copy-start | bytes 2359300
  69.5 28.2 %collective-permute-start.15 = (bf16[128,640]{1,0:T(8,128)(2,1)S(1)}, bf16[128,640]{1,0:T(8,128)(2,1)S(1)}, u32[]{:S(2)}, u32[]{:S(2)}) collective-permute-start(bf16[128,640]{1,0:T(8,128)(2,1)S(1)} %get-tuple-element.64.own), channel_id=1, source_target_pairs={{0,2},{2,0},{1,3},{3,1},{4,6},{6,4},{5,7},{7,5},{8,10},{10,8},{9,1... | collective-permute-start | bytes 491528 | tf_op jit(solution)/shard_map/ppermute | solution.py:59
  69.6 28.2 %collective-permute-start.14 = (bf16[128,640]{1,0:T(8,128)(2,1)S(1)}, bf16[128,640]{1,0:T(8,128)(2,1)S(1)}, u32[]{:S(2)}, u32[]{:S(2)}) collective-permute-start(bf16[128,640]{1,0:T(8,128)(2,1)S(1)} %get-tuple-element.64.own), channel_id=1, source_target_pairs={{0,1},{1,0},{2,3},{3,2},{4,5},{5,4},{6,7},{7,6},{8,9},{9,8},{10,11... | collective-permute-start | bytes 491528 | tf_op jit(solution)/shard_map/ppermute | solution.py:59
  94.5 1.0 copy-start.5
  97.7 1.4 collective-permute-start.16
  99.1 1.6 copy-start.1
  100.7 15.9 %copy-start.2 = (bf16[1024,1024]{1,0:T(8,128)(2,1)S(1)}, bf16[1024,1024]{1,0:T(8,128)(2,1)}, u32[]{:S(2)}) copy-start(bf16[1024,1024]{1,0:T(8,128)(2,1)} %head_l.3) | copy-start | bytes 6291460
  100.7 15.9 %copy-start.13 = (f32[1024]{0:T(1024)S(1)}, f32[1024]{0:T(1024)}, u32[]{:S(2)}) copy-start(f32[1024]{0:T(1024)} %param.15) | copy-start | bytes 12292
  102.7 12.0 %collective-permute-start.17 = (bf16[544,128]{1,0:T(8,128)(2,1)S(1)}, bf16[544,128]{1,0:T(8,128)(2,1)S(1)}, u32[]{:S(2)}, u32[]{:S(2)}) collective-permute-start(bf16[544,128]{1,0:T(8,128)(2,1)S(1)} %get-tuple-element.68), channel_id=1, source_target_pairs={{0,64},{64,128},{128,192},{192,0},{1,65},{65,129},{129,193},{193,1... | collective-permute-start | bytes 417800 | tf_op jit(solution)/shard_map/ppermute | solution.py:55
  103.0 12.4 %collective-permute-start.18 = (bf16[544,128]{1,0:T(8,128)(2,1)S(1)}, bf16[544,128]{1,0:T(8,128)(2,1)S(1)}, u32[]{:S(2)}, u32[]{:S(2)}) collective-permute-start(bf16[544,128]{1,0:T(8,128)(2,1)S(1)} %get-tuple-element.69), channel_id=1, source_target_pairs={{0,128},{64,192},{128,0},{192,64},{1,129},{65,193},{129,1},{193,65... | collective-permute-start | bytes 417800 | tf_op jit(solution)/shard_map/ppermute | solution.py:55
  103.9 12.1 %collective-permute-start.19 = (bf16[544,128]{1,0:T(8,128)(2,1)S(1)}, bf16[544,128]{1,0:T(8,128)(2,1)S(1)}, u32[]{:S(2)}, u32[]{:S(2)}) collective-permute-start(bf16[544,128]{1,0:T(8,128)(2,1)S(1)} %get-tuple-element.70), channel_id=1, source_target_pairs={{0,192},{64,0},{128,64},{192,128},{1,193},{65,1},{129,65},{193,129... | collective-permute-start | bytes 417800 | tf_op jit(solution)/shard_map/ppermute | solution.py:55
  106.0 1.2 collective-permute-start.12
  107.2 7.5 %collective-permute-start.13 = (f32[8,128]{1,0:T(8,128)S(1)}, f32[8,128]{1,0:T(8,128)S(1)}, u32[]{:S(2)}, u32[]{:S(2)}) collective-permute-start(f32[8,128]{1,0:T(8,128)S(1)} %add.16), channel_id=1, source_target_pairs={{0,2},{2,0},{1,3},{3,1},{4,6},{6,4},{5,7},{7,5},{8,10},{10,8},{9,1... | collective-permute-start | bytes 12296 | tf_op jit(solution)/shard_map/ppermute | solution.py:59
  120.0 4.3 %collective-permute-start.29 = (bf16[2,128,640]{2,1,0:T(8,128)(2,1)S(1)}, bf16[2,128,640]{2,1,0:T(8,128)(2,1)S(1)}, u32[]{:S(2)}, u32[]{:S(2)}) collective-permute-start(bf16[2,128,640]{2,1,0:T(8,128)(2,1)S(1)} %get-tuple-element.90), channel_id=1, source_target_pairs={{0,1},{1,0},{2,3},{3,2},{4,5},{5,4},{6,7},{7,6},{8,9},{9,8},{10,11... | collective-permute-start | bytes 983048 | tf_op jit(solution)/shard_map/ppermute | solution.py:59
  120.0 29.2 %collective-permute-start.22 = (bf16[3,128,1024]{2,1,0:T(8,128)(2,1)}, bf16[3,128,1024]{2,1,0:T(8,128)(2,1)S(1)}, u32[]{:S(2)}, u32[]{:S(2)}) collective-permute-start(bf16[3,128,1024]{2,1,0:T(8,128)(2,1)} %get-tuple-element.80.e0), channel_id=1, source_target_pairs={{0,192},{64,0},{128,64},{192,128},{1,193},{65,1},{129,65},{193,129... | collective-permute-start | bytes 2359304 | tf_op jit(solution)/shard_map/ppermute | solution.py:55
  121.1 28.1 %collective-permute-start.21 = (bf16[3,128,1024]{2,1,0:T(8,128)(2,1)}, bf16[3,128,1024]{2,1,0:T(8,128)(2,1)}, u32[]{:S(2)}, u32[]{:S(2)}) collective-permute-start(bf16[3,128,1024]{2,1,0:T(8,128)(2,1)} %get-tuple-element.80.e0), channel_id=1, source_target_pairs={{0,128},{64,192},{128,0},{192,64},{1,129},{65,193},{129,1},{193,65... | collective-permute-start | bytes 2359304 | tf_op jit(solution)/shard_map/ppermute | solution.py:55
  123.0 41.9 %collective-permute-start.20 = (bf16[3,128,1024]{2,1,0:T(8,128)(2,1)}, bf16[3,128,1024]{2,1,0:T(8,128)(2,1)}, u32[]{:S(2)}, u32[]{:S(2)}) collective-permute-start(bf16[3,128,1024]{2,1,0:T(8,128)(2,1)} %get-tuple-element.80.e0), channel_id=1, source_target_pairs={{0,64},{64,128},{128,192},{192,0},{1,65},{65,129},{129,193},{193,1... | collective-permute-start | bytes 2359304 | tf_op jit(solution)/shard_map/ppermute | solution.py:55
  125.2 9.8 %collective-permute-start.30 = (bf16[128,640]{1,0:T(8,128)(2,1)S(1)}, bf16[128,640]{1,0:T(8,128)(2,1)S(1)}, u32[]{:S(2)}, u32[]{:S(2)}) collective-permute-start(bf16[128,640]{1,0:T(8,128)(2,1)S(1)} %get-tuple-element.92), channel_id=1, source_target_pairs={{0,2},{2,0},{1,3},{3,1},{4,6},{6,4},{5,7},{7,5},{8,10},{10,8},{9,1... | collective-permute-start | bytes 491528 | tf_op jit(solution)/shard_map/ppermute | solution.py:59
  135.7 29.2 %copy-start.7 = (bf16[544,128]{1,0:T(8,128)(2,1)S(1)}, bf16[544,128]{1,0:T(8,128)(2,1)}, u32[]{:S(2)}) copy-start(bf16[544,128]{1,0:T(8,128)(2,1)} %copy-done.6) | copy-start | bytes 417796
  135.7 3.6 %collective-permute-start.31 = (f32[8,128]{1,0:T(8,128)S(1)}, f32[8,128]{1,0:T(8,128)S(1)}, u32[]{:S(2)}, u32[]{:S(2)}) collective-permute-start(f32[8,128]{1,0:T(8,128)S(1)} %shard_map.188.piece), channel_id=1, source_target_pairs={{0,4},{4,0},{8,12},{12,8},{1,5},{5,1},{9,13},{13,9},{2,6},{6,2},{1... | collective-permute-start | bytes 12296 | tf_op jit(solution)/shard_map/ppermute | solution.py:434
  141.5 50.0 %all-to-all-start.1 = ((bf16[64,16,256]{2,1,0:T(8,128)(2,1)}), bf16[64,16,256]{2,1,0:T(8,128)(2,1)S(1)}, u32[]{:S(2)}, u32[]{:S(2)}) async-start(bf16[64,16,256]{2,1,0:T(8,128)(2,1)} %bitcast.10), calls=%async_computation.1 | async-start | bytes 1048576 | tf_op jit(solution)/shard_map/all_to_all | solution.py:442
  164.8 0.9 copy-start.9
  169.3 16.5 %collective-permute-start.23 = (bf16[144,1024]{1,0:T(8,128)(2,1)S(1)}, bf16[144,1024]{1,0:T(8,128)(2,1)S(1)}, u32[]{:S(2)}, u32[]{:S(2)}) collective-permute-start(bf16[144,1024]{1,0:T(8,128)(2,1)S(1)} %get-tuple-element.82), channel_id=1, source_target_pairs={{0,16},{16,32},{32,48},{48,0},{1,17},{17,33},{33,49},{49,1},{2,18}... | collective-permute-start | bytes 884744 | tf_op jit(solution)/shard_map/ppermute | solution.py:55
  169.5 16.3 %collective-permute-start.24 = (bf16[144,1024]{1,0:T(8,128)(2,1)S(1)}, bf16[144,1024]{1,0:T(8,128)(2,1)S(1)}, u32[]{:S(2)}, u32[]{:S(2)}) collective-permute-start(bf16[144,1024]{1,0:T(8,128)(2,1)S(1)} %get-tuple-element.83), channel_id=1, source_target_pairs={{0,32},{16,48},{32,0},{48,16},{1,33},{17,49},{33,1},{49,17},{2,34}... | collective-permute-start | bytes 884744 | tf_op jit(solution)/shard_map/ppermute | solution.py:55
  171.9 14.5 %collective-permute-start.25 = (bf16[144,1024]{1,0:T(8,128)(2,1)S(1)}, bf16[144,1024]{1,0:T(8,128)(2,1)S(1)}, u32[]{:S(2)}, u32[]{:S(2)}) collective-permute-start(bf16[144,1024]{1,0:T(8,128)(2,1)S(1)} %get-tuple-element.84), channel_id=1, source_target_pairs={{0,48},{16,0},{32,16},{48,32},{1,49},{17,1},{33,17},{49,33},{2,50}... | collective-permute-start | bytes 884744 | tf_op jit(solution)/shard_map/ppermute | solution.py:55
  187.3 9.1 %collective-permute-start.26 = (bf16[48,1024]{1,0:T(8,128)(2,1)S(1)}, bf16[48,1024]{1,0:T(8,128)(2,1)S(1)}, u32[]{:S(2)}, u32[]{:S(2)}) collective-permute-start(bf16[48,1024]{1,0:T(8,128)(2,1)S(1)} %get-tuple-element.86), channel_id=1, source_target_pairs={{0,4},{4,8},{8,12},{12,0},{1,5},{5,9},{9,13},{13,1},{2,6},{6,10},{... | collective-permute-start | bytes 294920 | tf_op jit(solution)/shard_map/ppermute | solution.py:55
  190.0 7.4 %collective-permute-start.27 = (bf16[48,1024]{1,0:T(8,128)(2,1)S(1)}, bf16[48,1024]{1,0:T(8,128)(2,1)S(1)}, u32[]{:S(2)}, u32[]{:S(2)}) collective-permute-start(bf16[48,1024]{1,0:T(8,128)(2,1)S(1)} %get-tuple-element.87), channel_id=1, source_target_pairs={{0,8},{4,12},{8,0},{12,4},{1,9},{5,13},{9,1},{13,5},{2,10},{6,14},... | collective-permute-start | bytes 294920 | tf_op jit(solution)/shard_map/ppermute | solution.py:55
  190.0 7.4 %collective-permute-start.28 = (bf16[48,1024]{1,0:T(8,128)(2,1)S(1)}, bf16[48,1024]{1,0:T(8,128)(2,1)S(1)}, u32[]{:S(2)}, u32[]{:S(2)}) collective-permute-start(bf16[48,1024]{1,0:T(8,128)(2,1)S(1)} %get-tuple-element.88), channel_id=1, source_target_pairs={{0,12},{4,0},{8,4},{12,8},{1,13},{5,1},{9,5},{13,9},{2,14},{6,2},{... | collective-permute-start | bytes 294920 | tf_op jit(solution)/shard_map/ppermute | solution.py:55
  (4 other events, 2.9 us)
